TPU v7x, 512 devices: a whole 4x8x8 slice. The times are simulated.
512 devices in a mesh: tm: 8 (over x, core), series: 64 (over y, z).
Axes of the slice: x: 4, y: 8, z: 8, core: 2. Of those that a mesh axis runs over, the one named last changes fastest.
Arguments:
- leaf_outlook_matrix: float32 [384, 131072], P('tm', 'series'), may hold values from -6 to 6
- seasonal_leaf_outlook: float32 [5, 131072], P(None, 'series'), may hold values from -640 to 640
- lowest_tier_ancestor: int32 [131072, 1], P('series'), may hold values from 0 to 4095, as said below
- middle_tier_ancestor: int32 [131072, 1], P('series'), may hold values from 0 to 511
- uppermost_ancestor: int32 [131072, 1], P('series'), may hold values from 0 to 63
- lowest_tier_outlook: float32 [384, 4096], P('tm', 'series'), may hold values from -48 to 48
- middle_tier_outlook: float32 [384, 512], P('tm', 'series'), may hold values from -128 to 128
- uppermost_outlook: float32 [384, 64], P('tm', 'series'), may hold values from -384 to 384
Outputs:
- reconciled: float32 [384, 131072], P('tm', 'series')
Inputs may be any that keep to these rules, and one draw needn't show every extreme that they name: `lowest_tier_ancestor`: every node has at least one series; the owner of a node n is n // 64, and each aligned block of 2048 series holds exactly 32 series of the nodes of each owner. `middle_tier_ancestor`: every node of the level has at least one series. `uppermost_ancestor`: every node of the level has at least one series.
All inputs are finite; a program needn't handle non-finite values.
Results may differ from a plain program's by a relative error of at most 0.0013.
Values may be sent and summed in bfloat16 or wider, within the bound.
No kernel may reach another device: no remote copies, remote signals or barrier semaphores. Data moves between devices by JAX's collectives and lax.ppermute only.
A program may use at most 64 MiB of HBM per device.

v0:
```python
import math

import jax
import jax.numpy as jnp
from jax import lax
from jax.sharding import PartitionSpec as P


def aggregate(nearest_integer, ids, nodes):
    width = math.gcd(nodes, 512)
    blocks = nodes // width

    def one_block(index):
        first = index * width
        hits = ids[:, None] == first + jnp.arange(width, dtype=jnp.int32)[None, :]
        table = hits.astype(jnp.bfloat16)
        part = jnp.dot(nearest_integer, table, preferred_element_type=jnp.float32)
        return (part, jnp.sum(hits.astype(jnp.float32), axis=0))

    parts, counts = lax.map(one_block, jnp.arange(blocks, dtype=jnp.int32))
    totals = jnp.transpose(parts, (1, 0, 2)).reshape(nearest_integer.shape[0], nodes)
    return (totals, counts.reshape(1, nodes))


def spread_back(gap, ids):
    width = gap.shape[1]
    hits = (ids[None, :] == jnp.arange(width, dtype=jnp.int32)[:, None]).astype(jnp.bfloat16)
    return jnp.dot(gap, hits, preferred_element_type=jnp.float32)


def return_gaps(gap, ids):
    return spread_back(lax.all_gather(gap, "series", axis=1, tiled=True), ids)


def ancestor_piece(nearest_integer, ids, base):
    nodes = base.shape[1] * lax.axis_size("series")
    totals, counts = aggregate(nearest_integer, ids, nodes)
    own_totals, own_counts = (
        lax.psum_scatter(totals, "series", scatter_dimension=1, tiled=True),
        lax.psum_scatter(counts, "series", scatter_dimension=1, tiled=True),
    )
    gap = ((base - own_totals) / (own_counts + 1.0)).astype(jnp.bfloat16)
    return return_gaps(gap, ids)


def per_device(
    leaf_outlook_matrix,
    seasonal_leaf_outlook,
    lowest_tier_ancestor,
    middle_tier_ancestor,
    uppermost_ancestor,
    lowest_tier_outlook,
    middle_tier_outlook,
    uppermost_outlook,
):
    shard_horizon = leaf_outlook_matrix.shape[0]
    calendar_length_value = shard_horizon * lax.axis_size("tm")
    season_length_value = calendar_length_value // 4
    day_index = lax.axis_index("tm") * shard_horizon + jnp.arange(shard_horizon, dtype=jnp.int32)
    quarter_of = day_index // season_length_value
    quarter_table = (quarter_of[None, :] == jnp.arange(4, dtype=jnp.int32)[:, None]).astype(
        jnp.float32
    )
    partial_value = jnp.dot(
        quarter_table,
        leaf_outlook_matrix,
        precision=lax.Precision.HIGHEST,
        preferred_element_type=jnp.float32,
    )
    seasonal_summed_values = lax.psum(partial_value, "tm")
    seasonal_discrepancy = (
        0.5 * (seasonal_leaf_outlook[:4] - seasonal_summed_values) / season_length_value
    )
    harmonize_over_calendar = leaf_outlook_matrix + jnp.dot(
        quarter_table.T,
        seasonal_discrepancy,
        precision=lax.Precision.HIGHEST,
        preferred_element_type=jnp.float32,
    )
    calendar_accumulation = jnp.sum(
        0.5 * seasonal_summed_values + 0.5 * seasonal_leaf_outlook[:4], axis=0
    )
    per_diem = (
        harmonize_over_calendar
        + 0.5 * (seasonal_leaf_outlook[4] - calendar_accumulation) / calendar_length_value
    )
    nearest_integer = per_diem.astype(jnp.bfloat16)
    lowest_tier_piece = ancestor_piece(
        nearest_integer, lowest_tier_ancestor[:, 0], lowest_tier_outlook
    )
    middle_tier_piece = ancestor_piece(
        nearest_integer, middle_tier_ancestor[:, 0], middle_tier_outlook
    )
    uppermost_piece = ancestor_piece(nearest_integer, uppermost_ancestor[:, 0], uppermost_outlook)
    return per_diem + lowest_tier_piece + middle_tier_piece + uppermost_piece


def solution(mesh):
    return jax.shard_map(
        per_device,
        mesh=mesh,
        in_specs=(
            P("tm", "series"),
            P(None, "series"),
            P("series", None),
            P("series", None),
            P("series", None),
            P("tm", "series"),
            P("tm", "series"),
            P("tm", "series"),
        ),
        out_specs=P("tm", "series"),
        check_vma=False,
    )
```

profile of v0, /device:TPU:6, one launch (start us, length us, event | category | flops | bytes accessed | tf_op | source)
XLA Modules:
  0.0 784.2 jit_solution(5998660475962021959)
XLA Ops:
  6.6 1.2 fusion.31
  7.8 24.9 %psum.7 = f32[4,2048]{1,0:T(4,128)S(1)} all-reduce(f32[4,2048]{1,0:T(4,128)S(1)} %fusion.31), channel_id=1, replica_groups=mesh['tm'=8,'series'=64] {'tm'}, use_global_device_ids=true, to_apply=%region_0.1 | all-reduce | flops 8192 | bytes 65536 | tf_op jit(solution)/shard_map/psum | solution.py:70
  32.7 0.9 multiply_reduce_fusion
  33.6 0.9 subtract_multiply_fusion
  34.5 1.4 fusion.39
  35.9 34.1 %while.2 = (s32[]{:T(128)}, f32[8,48,512]{2,1,0:T(8,128)S(1)}, f32[8,512]{1,0:T(8,128)S(1)}, s32[2048,1]{0,1:T(1,128)}, s32[8]{0:T(128)S(1)}, /*index=5*/bf16[48...) while((s32[]{:T(128)}, f32[8,48,512]{2,1,0:T(8,128)S(1)}, f32[8,512]{1,0:T(8,128)S(1)}, ...), condition=%wide.region_4.5_spmd, body=%wide.region_2.4_spmd.sunk | while | flops 104857600 | bytes 323721 | solution.py:20
  35.9 0.7 dynamic_slice.10
  37.3 1.3 fusion.54
  38.6 1.5 fusion.53
  40.2 0.7 dynamic_slice.10
  41.5 1.3 fusion.54
  42.9 1.5 fusion.53
  44.4 0.7 dynamic_slice.10
  45.8 1.3 fusion.54
  47.1 1.5 fusion.53
  48.7 0.7 dynamic_slice.10
  50.1 1.3 fusion.54
  51.4 1.5 fusion.53
  52.9 0.7 dynamic_slice.10
  54.3 1.3 fusion.54
  55.7 1.5 fusion.53
  57.2 0.7 dynamic_slice.10
  58.6 1.3 fusion.54
  59.9 1.5 fusion.53
  61.5 0.7 dynamic_slice.10
  62.8 1.3 fusion.54
  64.2 1.5 fusion.53
  65.7 0.7 dynamic_slice.10
  67.1 1.3 fusion.54
  68.4 1.5 fusion.53
  70.7 1.5 bitcast_bitcast_fusion
  72.8 2.3 fusion.13
  75.2 1.9 copy.25
  77.2 1.3 dynamic-slice
  80.1 282.6 %all-reduce.4 = (f32[1,512]{1,0:T(1,128)S(1)}, f32[48,64]{0,1:T(8,128)S(1)}, f32[1,64]{1,0:T(1,128)S(1)}) all-reduce(f32[1,512]{1,0:T(1,128)S(1)} %bitcast.84, f32[48,64]{0,1:T(8,128)S(1)} %fusion.20, f32[1,64]{1,0:T(1,128)S(1)} %bitcast.83), channel_id=5, replica_groups=mesh['tm'=8,'series'=64] {'series'}, use_global_device_ids=true, to_apply=%region_9.10.clone | all-reduce | flops 3648 | bytes 29184
  362.7 1.3 fusion.40
  364.0 1.3 convert_bitcast_fusion
  365.3 37.6 %all-gather.1 = bf16[64,1,48]{2,1,0:T(2,128)(2,1)S(1)} all-gather(bf16[1,1,48]{2,1,0:T(2,128)(2,1)S(1)} %convert_bitcast_fusion), channel_id=1, replica_groups=mesh['tm'=8,'series'=64] {'series'}, dimensions={0}, use_global_device_ids=true | all-gather | bytes 6240 | tf_op jit(solution)/shard_map/all_gather | solution.py:32
  403.1 0.8 add_bitcast_fusion
  403.9 69.0 %all-reduce.7.cloned.1.call-done = f32[48,512]{0,1:T(8,128)} async-done(((f32[48,512]{0,1:T(8,128)}), f32[48,512]{0,1:T(8,128)}) %all-reduce.7.cloned.1.call-update) | async-done | bytes 98320
  472.9 0.8 fusion.30
  473.7 47.5 %all_gather.10 = bf16[48,512]{0,1:T(8,128)(2,1)S(1)} all-gather(bf16[48,8]{0,1:T(8,128)(2,1)S(1)} %fusion.30), channel_id=1, replica_groups=mesh['tm'=8,'series'=64] {'series'}, dimensions={1}, use_global_device_ids=true | all-gather | bytes 49920 | tf_op jit(solution)/shard_map/all_gather | solution.py:32
  521.2 197.4 %reduce-scatter.9.cloned.1.call-done = f32[64,48]{1,0:T(8,128)} async-done(((f32[4096,48]{1,0:T(8,128)}), f32[64,48]{1,0:T(8,128)}) %reduce-scatter.9.cloned.1.call-update) | async-done | bytes 12304
  718.6 0.8 copy.19
  719.5 49.0 %all-gather = bf16[64,64,48]{1,2,0:T(8,128)(2,1)S(1)} all-gather(bf16[1,64,48]{1,2,0:T(8,128)(2,1)S(1)} %fusion.28), channel_id=1, replica_groups=mesh['tm'=8,'series'=64] {'series'}, dimensions={0}, use_global_device_ids=true | all-gather | bytes 399360 | tf_op jit(solution)/shard_map/all_gather | solution.py:32
  769.4 6.5 fusion.17
  775.9 0.8 fusion.15
  776.7 1.0 convolution_add_fusion
  (50 shorter events, 4.0 us)
Async XLA Ops:
  6.5 396.5 %reduce-scatter.11.cloned.1.call-start = ((), (), s32[]{:S(2)}) async-start(), calls=%async_computation.3 | async-start | bytes 2129920
  72.1 0.7 copy-start.5
  72.2 400.8 %all-reduce.7.cloned.1.call-start = ((), (), s32[]{:S(2)}) async-start(), calls=%async_computation.4 | async-start | bytes 524288
  75.2 643.5 %reduce-scatter.9.cloned.1.call-start = ((), (), s32[]{:S(2)}) async-start(), calls=%async_computation.2 | async-start | bytes 2129920
  75.2 3.9 copy-start.1
  75.2 288.8 %copy-start.4 = (f32[48,1]{0,1:T(1,128)S(1)}, f32[48,1]{0,1:T(1,128)}, u32[]{:S(2)}) copy-start(f32[48,1]{0,1:T(1,128)} %param.17) | copy-start | bytes 580
  77.1 395.8 %copy-start.3 = (f32[48,8]{0,1:T(8,128)S(1)}, f32[48,8]{0,1:T(8,128)}, u32[]{:S(2)}) copy-start(f32[48,8]{0,1:T(8,128)} %param.16) | copy-start | bytes 4612
  77.1 642.3 %copy-start.2 = (f32[48,64]{1,0:T(8,128)S(1)}, f32[48,64]{1,0:T(8,128)}, u32[]{:S(2)}) copy-start(f32[48,64]{1,0:T(8,128)} %param.15) | copy-start | bytes 36868
  80.1 689.3 %copy-start = (s32[2048,1]{0,1:T(1,128)S(1)}, s32[2048,1]{0,1:T(1,128)}, u32[]{:S(2)}) copy-start(s32[2048,1]{0,1:T(1,128)} %get-tuple-element.160) | copy-start | bytes 24580
Sparse Core Ops, SparseCore 0:
  72.3 247.9 reduce-scatter.10
  323.9 149.0 all-reduce.6
  477.0 241.5 reduce-scatter.8
where the time goes:
time: 786 us; the launch traced here: 784 us
  blocking collectives  442 us (56%)
  waiting for transfers between devices  266 us (34%)
  matrix products  25.7 us (3%)
  other arithmetic  16.8 us (2%)
  between operations  13.9 us (2%)
  local copies, waits for them, and re-layouts  13.7 us (2%)
    unnamed x1, blocking collectives  283 us
    unnamed x6, waiting for transfers between devices  266 us
    all_gather x3, blocking collectives, return_gaps(): return spread_back(lax.all_gather(gap, 'series', axis=1, tiled=True), ids)  134 us
    psum x1, blocking collectives, per_device(): seasonal_summed_values = lax.psum(partial_value, 'tm')  24.9 us
  transfers between devices with their start and end apart: 3, of which 2 were waited for; matrix products, arithmetic and copies ran while one was open for 1% of the time, Pallas kernels for 0%

commit v1 on v0

v1 whole, which is shorter than its diff:
```python
import jax
import jax.numpy as jnp
from jax import lax
from jax.experimental import pallas as pl
from jax.experimental.pallas import tpu as pltpu
from jax.sharding import PartitionSpec as P

f32 = jnp.float32
bf16 = jnp.bfloat16
i32 = jnp.int32

PARAMS = pltpu.CompilerParams(vmem_limit_bytes=48 * 1024 * 1024)


def iota(shape, dim):
    return lax.broadcasted_iota(i32, shape, dim)


def ones_where(mask):
    return jnp.where(mask, 1.0, 0.0).astype(bf16)


def dot(a, b):
    return jnp.dot(a, b, preferred_element_type=f32)


def corrections(seas, parts, quarter, days):
    n_parts = parts.shape[0]
    per = n_parts // 4
    season_days = days * per
    own = jnp.sum(jnp.where(iota(parts.shape, 0) // per == quarter, parts, 0.0), axis=0, keepdims=True)
    rows = iota(seas.shape, 0)
    seas_own = jnp.sum(jnp.where(rows == quarter, seas, 0.0), axis=0, keepdims=True)
    seas_four = jnp.sum(jnp.where(rows < 4, seas, 0.0), axis=0, keepdims=True)
    year = 0.5 * jnp.sum(parts, axis=0, keepdims=True) + 0.5 * seas_four
    first = 0.5 * (seas_own - own) / season_days
    second = 0.5 * (seas[4:5, :] - year) / (season_days * 4)
    return first, second


def day_sum_kernel(leaf_ref, out_ref):
    out_ref[...] = jnp.sum(leaf_ref[...], axis=0, keepdims=True)


def send_kernel(quarter_ref, leaf_ref, seas_ref, parts_ref, fine_ref, mid_ref, top_ref, pay_ref, places_ref, shift_ref, wide_ref):
    days, rows = leaf_ref.shape
    owners = pay_ref.shape[0]
    first, second = corrections(seas_ref[...], parts_ref[...], quarter_ref[0], days)
    shift_ref[0:1, :] = first
    shift_ref[1:2, :] = second
    daily = (leaf_ref[...] + first) + second
    fine = fine_ref[...]
    node_dev = 64
    owner = fine // node_dev
    local = fine - owner * node_dev

    step = min(256, rows)
    before = ones_where(iota((step, step), 0) < iota((step, step), 1))
    base = jnp.zeros((owners, 1), f32)
    ranks = []
    for at in range(0, rows, step):
        hit = owner[:, at:at + step] == iota((owners, step), 0)
        hit_f = jnp.where(hit, 1.0, 0.0)
        seen = dot(hit_f.astype(bf16), before) + base
        ranks.append(jnp.sum(jnp.where(hit, seen, 0.0), axis=0, keepdims=True))
        base = base + jnp.sum(hit_f, axis=1, keepdims=True)
    rank = jnp.concatenate(ranks, axis=1).astype(i32)
    place = owner * 16 + (rank & 15)
    place_low = jnp.where(rank < 16, place, -1)
    place_high = jnp.where(rank < 16, -1, place)
    mid = mid_ref[...]
    place_mid = (mid // 8) * 16 + (mid & 7)
    place_top = top_ref[...] * 16 + 8
    places_ref[0:1, :] = place_low
    places_ref[1:2, :] = place_high
    places_ref[2:3, :] = place_mid
    places_ref[3:4, :] = place_top

    rounded = daily.astype(bf16).astype(f32)
    ext = jnp.concatenate([rounded, local.astype(f32), jnp.ones((1, rows), f32), jnp.zeros((14, rows), f32)], axis=0)
    for at in range(0, rows, 128):
        turned = jnp.transpose(ext[:, at:at + 128])
        wide_ref[at:at + 128, :] = jnp.concatenate([turned, turned], axis=1).astype(bf16)
    wide = wide_ref[...]

    group = min(8, owners)
    chunk = group * 16
    low_half = iota((chunk, 128), 1) < 64
    for g in range(owners // group):
        row = iota((chunk, rows), 0) + g * chunk
        slots = jnp.where(
            low_half,
            dot(ones_where(row == place_low), wide),
            dot(ones_where(row == place_high), wide),
        ).astype(bf16)
        sums = dot(ones_where((row == place_mid) | (row == place_top)), wide)
        high = sums.astype(bf16)
        sums = jnp.where(low_half, high.astype(f32), sums - high.astype(f32)).astype(bf16)
        pay_ref[pl.ds(g * group, group), 0:16, :] = slots.reshape(group, 16, 128)
        pay_ref[pl.ds(g * group, group), 16:32, :] = sums.reshape(group, 16, 128)


def owner_kernel(got_ref, base_fine_ref, base_rest_ref, back_ref):
    owners = got_ref.shape[0]
    days, nodes = base_fine_ref.shape
    slots = got_ref[:, 0:16, :].reshape(owners * 16, 128).astype(f32)
    low_half = iota((owners * 16, 128), 1) < 64
    lane = iota((owners * 16, nodes), 1).astype(f32)
    pick_low = ones_where(slots[:, days:days + 1] == lane)
    pick_high = ones_where(slots[:, 64 + days:65 + days] == lane)
    turned = jnp.transpose(slots).astype(bf16)
    totals = dot(turned[0:64, :], pick_low) + dot(turned[64:128, :], pick_high)
    gap = (base_fine_ref[...] - totals[0:days, :]) / (totals[days + 1:days + 2, :] + 1.0)
    gap = jnp.concatenate([gap, jnp.zeros((64 - days, nodes), f32)], axis=0)
    gap = jnp.transpose(jnp.concatenate([gap, gap], axis=0)).astype(bf16)
    spread = jnp.where(low_half, dot(pick_low, gap), dot(pick_high, gap)).astype(bf16)
    back_ref[:, 0:16, :] = spread.reshape(owners, 16, 128)

    rest = jnp.sum(got_ref[:, 16:32, :].astype(f32), axis=0)
    rest = rest[:, 0:64] + rest[:, 64:128]
    gap_rest = (base_rest_ref[...] - rest) / (rest[:, days + 1:days + 2] + 1.0)
    gap_rest = jnp.where(iota((16, 64), 1) < days, gap_rest, 0.0)
    gap_rest = jnp.concatenate([gap_rest, jnp.zeros((16, 64), f32)], axis=1).astype(bf16)
    back_ref[:, 16:32, :] = jnp.broadcast_to(gap_rest[None], (owners, 16, 128))


def finish_kernel(leaf_ref, shift_ref, places_ref, back_ref, out_ref):
    days, rows = leaf_ref.shape
    owners = back_ref.shape[0]
    height = owners * 16
    slots = jnp.transpose(back_ref[:, 0:16, :].reshape(height, 128).astype(f32)).astype(bf16)
    rest = jnp.transpose(back_ref[:, 16:32, :].reshape(height, 128).astype(f32)).astype(bf16)
    low, high, rest = slots[0:days, :], slots[64:64 + days, :], rest[0:days, :]
    step = min(256, rows)
    for at in range(0, rows, step):
        row = iota((height, step), 0)
        daily = (leaf_ref[:, at:at + step] + shift_ref[0:1, at:at + step]) + shift_ref[1:2, at:at + step]
        place = places_ref[:, at:at + step]
        fine = dot(low, ones_where(row == place[0:1, :])) + dot(high, ones_where(row == place[1:2, :]))
        others = dot(rest, ones_where((row == place[2:3, :]) | (row == place[3:4, :])))
        out_ref[:, at:at + step] = (daily + fine) + others


def per_device(leaf, seas, fine, mid, top, base_fine, base_mid, base_top):
    days, rows = leaf.shape
    owners = lax.axis_size("series")
    quarter = (lax.axis_index("tm") // 2).astype(i32).reshape(1)
    base_rest = jnp.concatenate([base_mid, base_top], axis=1).T
    base_rest = jnp.pad(base_rest, ((0, 16 - base_rest.shape[0]), (0, 64 - days)))
    fine, mid, top = (ids.reshape(1, rows) for ids in (fine, mid, top))

    sums = pl.pallas_call(
        day_sum_kernel, out_shape=jax.ShapeDtypeStruct((1, rows), f32), compiler_params=PARAMS, name="day_sums"
    )(leaf)
    parts = lax.all_gather(sums, "tm", axis=0, tiled=True)

    vmem = pl.BlockSpec(memory_space=pltpu.VMEM)
    payload, places, shift = pl.pallas_call(
        send_kernel,
        out_shape=(
            jax.ShapeDtypeStruct((owners, 32, 128), bf16),
            jax.ShapeDtypeStruct((4, rows), i32),
            jax.ShapeDtypeStruct((2, rows), f32),
        ),
        in_specs=[pl.BlockSpec(memory_space=pltpu.SMEM)] + [vmem] * 6,
        scratch_shapes=[pltpu.VMEM((rows, 128), bf16)],
        compiler_params=PARAMS,
        name="pack",
    )(quarter, leaf, seas, parts, fine, mid, top)
    got = lax.all_to_all(payload, "series", 0, 0, tiled=True)
    back = pl.pallas_call(
        owner_kernel,
        out_shape=jax.ShapeDtypeStruct((owners, 32, 128), bf16),
        compiler_params=PARAMS,
        name="gaps",
    )(got, base_fine, base_rest)
    back = lax.all_to_all(back, "series", 0, 0, tiled=True)
    return pl.pallas_call(
        finish_kernel,
        out_shape=jax.ShapeDtypeStruct((days, rows), f32),
        compiler_params=PARAMS,
        name="finish",
    )(leaf, shift, places, back)


def solution(mesh):
    return jax.shard_map(
        per_device,
        mesh=mesh,
        in_specs=(
            P("tm", "series"),
            P(None, "series"),
            P("series", None),
            P("series", None),
            P("series", None),
            P("tm", "series"),
            P("tm", "series"),
            P("tm", "series"),
        ),
        out_specs=P("tm", "series"),
        check_vma=False,
    )
```

time: 786 us -> 87.4 us (0.11)
  blocking collectives: 442 us -> 40 us
  waiting for transfers between devices: 266 us -> 19.3 us
  matrix products: 25.7 us -> 0 us
  other arithmetic: 16.8 us -> 0.01 us
  starting transfers between devices: 0.09 us -> 14.1 us
  between operations: 13.9 us -> 0.09 us
  local copies, waits for them, and re-layouts: 13.7 us -> 1.83 us
  Pallas kernels: 0 us -> 11.2 us
    unnamed x1 -> x0, blocking collectives: 283 us -> none
    unnamed x6 -> x0, waiting for transfers between devices: 266 us -> none
    all_gather x3 -> x1, blocking collectives: 134 us -> 15.5 us  [per_device(): parts = lax.all_gather(sums, 'tm', axis=0, tiled=True)]
    dot_general x15 -> x0, matrix products: 25.7 us -> none  [the longest x10 14.7 us: one_block(): part = jnp.dot(nearest_integer, table, preferred_element_type=jnp.float32)]
    psum x1 -> x0, blocking collectives: 24.9 us -> none  [per_device(): seasonal_summed_values = lax.psum(partial_value, 'tm')]
    all_to_all x0 -> x1, blocking collectives: none -> 24.5 us  [per_device(): back = lax.all_to_all(back, 'series', 0, 0, tiled=True)]
    all_to_all x0 -> x1, waiting for transfers between devices: none -> 19.3 us  [per_device(): got = lax.all_to_all(payload, 'series', 0, 0, tiled=True)]
    all_to_all x0 -> x1, starting transfers between devices: none -> 14.1 us  [per_device(): got = lax.all_to_all(payload, 'series', 0, 0, tiled=True)]
  transfers between devices with their start and end apart: 3 -> 1, of which waited for: 2 -> 1; matrix products, arithmetic and copies ran while one was open for 1% -> 0% of each run, Pallas kernels for 0% -> 0%
where the time goes in v1:
time: 87.4 us; the launch traced here: 86.6 us
  blocking collectives  40 us (46%)
  waiting for transfers between devices  19.3 us (22%)
  starting transfers between devices  14.1 us (16%)
  Pallas kernels  11.2 us (13%)
  local copies, waits for them, and re-layouts  1.83 us (2%)
    all_to_all x1, blocking collectives, per_device(): back = lax.all_to_all(back, 'series', 0, 0, tiled=True)  24.5 us
    all_to_all x1, waiting for transfers between devices, per_device(): got = lax.all_to_all(payload, 'series', 0, 0, tiled=True)  19.3 us
    all_gather x1, blocking collectives, per_device(): parts = lax.all_gather(sums, 'tm', axis=0, tiled=True)  15.5 us
    all_to_all x1, starting transfers between devices, per_device(): got = lax.all_to_all(payload, 'series', 0, 0, tiled=True)  14.1 us
    pallas_call x1, Pallas kernels, per_device(): pl.pallas_call(send_kernel, out_shape=(jax.ShapeDtypeStruct((owners, 32,...  5.43 us
    pallas_call x1, Pallas kernels, per_device(): pl.pallas_call(finish_kernel, out_shape=jax.ShapeDtypeStruct((days, rows)...  4.9 us
    unnamed x19, local copies, waits for them, and re-layouts  1.83 us
  transfers between devices with their start and end apart: 1, of which 1 were waited for; matrix products, arithmetic and copies ran while one was open for 0% of the time, Pallas kernels for 0%

profile of v1, /device:TPU:6, one launch (start us, length us, event | category | flops | bytes accessed | tf_op | source)
XLA Modules:
  0.0 86.6 jit_solution(3670648249449564090)
XLA Ops:
  0.0 0.0 copy-start
  0.0 1.0 %copy-done = f32[48,2048]{1,0:T(8,128)S(1)} copy-done((f32[48,2048]{1,0:T(8,128)S(1)}, f32[48,2048]{1,0:T(8,128)}, u32[]{:S(2)}) %copy-start) | copy-done | bytes 393240
  1.0 0.0 copy-start.1
  1.0 15.5 %all-gather = f32[8,1,2048]{2,1,0:T(1,128)S(1)} all-gather(f32[1,1,2048]{2,1,0:T(1,128)S(1)} %bitcast.11), channel_id=1, replica_groups=mesh['tm'=8,'series'=64] {'tm'}, dimensions={0}, use_global_device_ids=true | all-gather | bytes 73728 | tf_op jit(solution)/shard_map/all_gather | solution.py:155
  16.5 0.0 copy-start.2
  16.5 0.0 copy-start.5
  16.6 0.0 copy-start.6
  16.6 0.0 copy-start.4
  16.6 0.0 copy-done.1
  16.6 0.8 copy-done.2
  17.4 0.0 copy-done.5
  17.4 0.0 copy-done.6
  17.4 0.0 copy-done.4
  17.4 5.4 %pack.1 = (bf16[64,32,128]{2,1,0:T(8,128)(2,1)}, s32[4,2048]{1,0:T(4,128)S(1)}, f32[2,2048]{1,0:T(2,128)S(1)}) custom-call(s32[1]{0:T(128)} %bitcast.quarter_ref, f32[48,2048]{1,0:T(8,128)S(1)} %copy-done.1, f32[5,2048]{1,0:T(8,128)S(1)} %copy-done.2, f32[8,2048]{1,0:T(8,128)S(1)} %bitcast.10, s32[1,2048]{1,0:T(1,128)S(1)} %bitcast.12, ...), custom_call_target="tpu_custom_call" | custom-call | tf_op jit(solution)/shard_map/pack/pallas_call | solution.py:158
  22.8 0.0 copy-start.7
  22.8 0.0 copy-start.8
  22.8 14.1 %all-to-all-start = ((bf16[64,32,128]{2,1,0:T(8,128)(2,1)}), bf16[64,32,128]{2,1,0:T(8,128)(2,1)S(1)}, u32[]{:S(2)}, u32[]{:S(2)}) async-start(bf16[64,32,128]{2,1,0:T(8,128)(2,1)} %get-tuple-element.10), calls=%async_computation | async-start | bytes 1048576 | tf_op jit(solution)/shard_map/all_to_all | solution.py:170
  36.9 0.0 copy-done.7
  37.0 0.0 copy-done.8
  37.0 0.0 copy-start.3
  37.0 19.3 %all-to-all-done.got_ref = bf16[64,32,128]{2,1,0:T(8,128)(2,1)S(1)} async-done(((bf16[64,32,128]{2,1,0:T(8,128)(2,1)}), bf16[64,32,128]{2,1,0:T(8,128)(2,1)S(1)}, u32[]{:S(2)}, u32[]{:S(2)}) %all-to-all-start) | async-done | bytes 524320 | tf_op jit(solution)/shard_map/all_to_all | solution.py:170
  56.3 0.0 copy-done.3
  56.3 0.8 gaps.1
  57.2 24.5 %all_to_all.10.back_ref = bf16[64,32,128]{2,1,0:T(8,128)(2,1)S(1)} all-to-all(bf16[64,32,128]{2,1,0:T(8,128)(2,1)S(1)} %gaps.1), channel_id=1, replica_groups=mesh['tm'=8,'series'=64] {'series'}, dimensions={0} | all-to-all | bytes 1048576 | tf_op jit(solution)/shard_map/all_to_all | solution.py:177
  81.7 4.9 %finish.1 = f32[48,2048]{1,0:T(8,128)} custom-call(f32[48,2048]{1,0:T(8,128)S(1)} %copy-done.1, f32[2,2048]{1,0:T(2,128)S(1)} %get-tuple-element.8.shift_ref, s32[4,2048]{1,0:T(4,128)S(1)} %get-tuple-element.9.places_ref, bf16[64,32,128]{2,1,0:T(8,128)(2,1)S(1)} %all_to_all.10.back_ref), custom_call_target="tpu_custom_call" | custom-call | tf_op jit(solution)/shard_map/finish/pallas_call | solution.py:178
  (4 shorter events, 0.1 us)
Async XLA Ops:
  0.0 1.0 %copy-start = (f32[48,2048]{1,0:T(8,128)S(1)}, f32[48,2048]{1,0:T(8,128)}, u32[]{:S(2)}) copy-start(f32[48,2048]{1,0:T(8,128)} %leaf_ref.5) | copy-start | bytes 1179652
  1.0 15.6 %copy-start.1 = (f32[48,2048]{1,0:T(8,128)S(1)}, f32[48,2048]{1,0:T(8,128)}, u32[]{:S(2)}) copy-start(f32[48,2048]{1,0:T(8,128)} %leaf_ref.5) | copy-start | bytes 1179652
  16.5 0.8 copy-start.2
  16.5 0.8 copy-start.5
  16.6 0.8 copy-start.6
  16.6 0.8 copy-start.4
  22.8 14.1 %copy-start.7 = (f32[48,8]{0,1:T(8,128)S(1)}, f32[48,8]{0,1:T(8,128)}, u32[]{:S(2)}) copy-start(f32[48,8]{0,1:T(8,128)} %param.14) | copy-start | bytes 4612
  22.8 14.1 %copy-start.8 = (f32[48,1]{0,1:T(1,128)S(1)}, f32[48,1]{0,1:T(1,128)}, u32[]{:S(2)}) copy-start(f32[48,1]{0,1:T(1,128)} %param.15) | copy-start | bytes 580
  22.8 33.5 %all-to-all-start = ((bf16[64,32,128]{2,1,0:T(8,128)(2,1)}), bf16[64,32,128]{2,1,0:T(8,128)(2,1)S(1)}, u32[]{:S(2)}, u32[]{:S(2)}) async-start(bf16[64,32,128]{2,1,0:T(8,128)(2,1)} %get-tuple-element.10), calls=%async_computation | async-start | bytes 1048576 | tf_op jit(solution)/shard_map/all_to_all | solution.py:170
  37.0 19.4 %copy-start.3 = (f32[48,64]{1,0:T(8,128)S(1)}, f32[48,64]{1,0:T(8,128)}, u32[]{:S(2)}) copy-start(f32[48,64]{1,0:T(8,128)} %base_fine_ref.1) | copy-start | bytes 36868

commit v2 on v1

--- a/solution.py
+++ b/solution.py
@@ -1,8 +1,11 @@
+import math
+
 import jax
 import jax.numpy as jnp
 from jax import lax
 from jax.experimental import pallas as pl
 from jax.experimental.pallas import tpu as pltpu
+from jax.sharding import Mesh
 from jax.sharding import PartitionSpec as P
 
 f32 = jnp.float32
@@ -141,9 +144,17 @@
         out_ref[:, at:at + step] = (daily + fine) + others
 
 
+def exchange(blocks):
+    over_y, over_z = lax.axis_size("y"), lax.axis_size("z")
+    shape = blocks.shape
+    blocks = lax.all_to_all(blocks.reshape((over_y, over_z) + shape[1:]), "y", 0, 0, tiled=True)
+    blocks = lax.all_to_all(jnp.swapaxes(blocks, 0, 1), "z", 0, 0, tiled=True)
+    return jnp.swapaxes(blocks, 0, 1).reshape(shape)
+
+
 def per_device(leaf, seas, fine, mid, top, base_fine, base_mid, base_top):
     days, rows = leaf.shape
-    owners = lax.axis_size("series")
+    owners = lax.axis_size("y") * lax.axis_size("z")
     quarter = (lax.axis_index("tm") // 2).astype(i32).reshape(1)
     base_rest = jnp.concatenate([base_mid, base_top], axis=1).T
     base_rest = jnp.pad(base_rest, ((0, 16 - base_rest.shape[0]), (0, 64 - days)))
@@ -152,7 +163,7 @@
     sums = pl.pallas_call(
         day_sum_kernel, out_shape=jax.ShapeDtypeStruct((1, rows), f32), compiler_params=PARAMS, name="day_sums"
     )(leaf)
-    parts = lax.all_gather(sums, "tm", axis=0, tiled=True)
+    parts = lax.all_to_all(jnp.broadcast_to(sums, (lax.axis_size("tm"), rows)), "tm", 0, 0, tiled=True)
 
     vmem = pl.BlockSpec(memory_space=pltpu.VMEM)
     payload, places, shift = pl.pallas_call(
@@ -167,14 +178,14 @@
         compiler_params=PARAMS,
         name="pack",
     )(quarter, leaf, seas, parts, fine, mid, top)
-    got = lax.all_to_all(payload, "series", 0, 0, tiled=True)
+    got = exchange(payload)
     back = pl.pallas_call(
         owner_kernel,
         out_shape=jax.ShapeDtypeStruct((owners, 32, 128), bf16),
         compiler_params=PARAMS,
         name="gaps",
     )(got, base_fine, base_rest)
-    back = lax.all_to_all(back, "series", 0, 0, tiled=True)
+    back = lax.all_to_all(back, ("y", "z"), 0, 0, tiled=True)
     return pl.pallas_call(
         finish_kernel,
         out_shape=jax.ShapeDtypeStruct((days, rows), f32),
@@ -184,19 +195,23 @@
 
 
 def solution(mesh):
+    devices = mesh.devices
+    side = math.isqrt(devices.shape[1])
+    mesh = Mesh(devices.reshape(devices.shape[0], side, side), ("tm", "y", "z"))
+    series = ("y", "z")
     return jax.shard_map(
         per_device,
         mesh=mesh,
         in_specs=(
-            P("tm", "series"),
-            P(None, "series"),
-            P("series", None),
-            P("series", None),
-            P("series", None),
-            P("tm", "series"),
-            P("tm", "series"),
-            P("tm", "series"),
+            P("tm", series),
+            P(None, series),
+            P(series, None),
+            P(series, None),
+            P(series, None),
+            P("tm", series),
+            P("tm", series),
+            P("tm", series),
         ),
-        out_specs=P("tm", "series"),
+        out_specs=P("tm", series),
         check_vma=False,
     )

time: 87.4 us -> 97.2 us (1.11); the launches traced: 86.6 us -> 95.3 us
  starting transfers between devices: 14.1 us -> 19.5 us
  blocking collectives: 40 us -> 42.4 us
  local copies, waits for them, and re-layouts: 1.83 us -> 3.95 us
    all_to_all x1 -> x2, blocking collectives: 24.5 us -> 42.4 us  [the longest x1 22.3 us: per_device(): back = lax.all_to_all(back, ('y', 'z'), 0, 0, tiled=True)]
    all_gather x1 -> x0, blocking collectives: 15.5 us -> none  [per_device(): parts = lax.all_gather(sums, 'tm', axis=0, tiled=True)]
    all_to_all x1 -> x2, starting transfers between devices: 14.1 us -> 19.5 us  [the longest x1 10.3 us: exchange(): blocks = lax.all_to_all(jnp.swapaxes(blocks, 0, 1), 'z', 0, 0, tiled=True)]
    all_to_all x1 -> x2, waiting for transfers between devices: 19.3 us -> 19 us  [the longest x1 15.5 us: exchange(): blocks = lax.all_to_all(jnp.swapaxes(blocks, 0, 1), 'z', 0, 0, tiled=True)]
  transfers between devices with their start and end apart: 1 -> 2, of which waited for: 1 -> 2; matrix products, arithmetic and copies ran while one was open for 0% -> 0% of each run, Pallas kernels for 0% -> 0%
where the time goes in v2:
time: 97.2 us; the launch traced here: 95.3 us
  blocking collectives  42.4 us (44%)
  starting transfers between devices  19.5 us (20%)
  waiting for transfers between devices  19 us (20%)
  Pallas kernels  10.4 us (11%)
  local copies, waits for them, and re-layouts  3.95 us (4%)
    all_to_all x1, blocking collectives, per_device(): back = lax.all_to_all(back, ('y', 'z'), 0, 0, tiled=True)  22.3 us
    all_to_all x1, blocking collectives, exchange(): lax.all_to_all(blocks.reshape((over_y, over_z) + shape[1:]), 'y', 0, 0, t...  20.1 us
    all_to_all x1, waiting for transfers between devices, exchange(): blocks = lax.all_to_all(jnp.swapaxes(blocks, 0, 1), 'z', 0, 0, tiled=True)  15.5 us
    all_to_all x1, starting transfers between devices, exchange(): blocks = lax.all_to_all(jnp.swapaxes(blocks, 0, 1), 'z', 0, 0, tiled=True)  10.3 us
    all_to_all x1, starting transfers between devices, per_device(): lax.all_to_all(jnp.broadcast_to(sums, (lax.axis_size('tm'), rows)), 'tm',...  9.14 us
    pallas_call x1, Pallas kernels, per_device(): pl.pallas_call(finish_kernel, out_shape=jax.ShapeDtypeStruct((days, rows)...  4.9 us
    pallas_call x1, Pallas kernels, per_device(): pl.pallas_call(send_kernel, out_shape=(jax.ShapeDtypeStruct((owners, 32,...  4.62 us
    all_to_all x1, waiting for transfers between devices, per_device(): lax.all_to_all(jnp.broadcast_to(sums, (lax.axis_size('tm'), rows)), 'tm',...  3.53 us
  transfers between devices with their start and end apart: 2, of which 2 were waited for; matrix products, arithmetic and copies ran while one was open for 0% of the time, Pallas kernels for 0%

profile of v2, /device:TPU:6, one launch (start us, length us, event | category | flops | bytes accessed | tf_op | source)
XLA Modules:
  0.0 95.3 jit_solution(15880328751687259302)
XLA Ops:
  0.0 0.0 copy-start
  0.0 1.0 %copy-done = f32[48,2048]{1,0:T(8,128)S(1)} copy-done((f32[48,2048]{1,0:T(8,128)S(1)}, f32[48,2048]{1,0:T(8,128)}, u32[]{:S(2)}) %copy-start) | copy-done | bytes 393240
  1.0 0.0 copy-start.1
  1.0 0.7 broadcast_in_dim.2
  1.7 9.1 %all-to-all-start = ((f32[8,1,2048]{2,1,0:T(1,128)}), f32[8,1,2048]{2,1,0:T(1,128)S(1)}, u32[]{:S(2)}, u32[]{:S(2)}) async-start(f32[8,1,2048]{2,1,0:T(1,128)} %broadcast_in_dim.2), calls=%async_computation | async-start | bytes 131072 | tf_op jit(solution)/shard_map/all_to_all | solution.py:166
  10.8 0.0 copy-start.2
  10.8 3.5 %all-to-all-done = f32[8,1,2048]{2,1,0:T(1,128)S(1)} async-done(((f32[8,1,2048]{2,1,0:T(1,128)}), f32[8,1,2048]{2,1,0:T(1,128)S(1)}, u32[]{:S(2)}, u32[]{:S(2)}) %all-to-all-start) | async-done | bytes 65568 | tf_op jit(solution)/shard_map/all_to_all | solution.py:166
  14.4 0.0 copy-start.5
  14.4 0.0 copy-start.6
  14.4 0.0 copy-start.4
  14.4 0.0 copy-done.1
  14.4 0.0 copy-done.2
  14.4 0.6 copy-done.5
  15.1 0.0 copy-done.6
  15.1 0.0 copy-done.4
  15.1 4.6 %pack.1 = (bf16[64,32,128]{2,1,0:T(8,128)(2,1)S(1)}, s32[4,2048]{1,0:T(4,128)S(1)}, f32[2,2048]{1,0:T(2,128)S(1)}) custom-call(s32[1]{0:T(128)} %bitcast.quarter_ref, f32[48,2048]{1,0:T(8,128)S(1)} %copy-done.1, f32[5,2048]{1,0:T(8,128)S(1)} %copy-done.2, f32[8,2048]{1,0:T(8,128)S(1)} %bitcast.16, s32[1,2048]{1,0:T(1,128)S(1)} %bitcast.18, ...), custom_call_target="tpu_custom_call" | custom-call | tf_op jit(solution)/shard_map/pack/pallas_call | solution.py:169
  19.7 20.1 %all_to_all.23 = bf16[8,8,32,128]{3,2,1,0:T(8,128)(2,1)S(1)} all-to-all(bf16[8,8,32,128]{3,2,1,0:T(8,128)(2,1)S(1)} %bitcast.15), channel_id=1, replica_groups=mesh['tm'=8,'y'=8,'z'=8] {'y'}, dimensions={0} | all-to-all | bytes 1048576 | tf_op jit(solution)/shard_map/all_to_all | solution.py:150
  39.8 0.8 copy.11
  40.6 0.0 copy-start.7
  40.6 0.0 copy-start.8
  40.6 10.3 %all-to-all-start.2 = ((bf16[8,8,32,128]{3,2,1,0:T(8,128)(2,1)}), bf16[8,8,32,128]{3,2,1,0:T(8,128)(2,1)S(1)}, u32[]{:S(2)}, u32[]{:S(2)}) async-start(bf16[8,8,32,128]{3,2,1,0:T(8,128)(2,1)} %copy.11), calls=%async_computation.2 | async-start | bytes 1048576 | tf_op jit(solution)/shard_map/all_to_all | solution.py:151
  51.0 0.0 copy-done.7
  51.0 0.0 copy-done.8
  51.0 15.5 %all-to-all-done.2 = bf16[8,8,32,128]{3,2,1,0:T(8,128)(2,1)S(1)} async-done(((bf16[8,8,32,128]{3,2,1,0:T(8,128)(2,1)}), bf16[8,8,32,128]{3,2,1,0:T(8,128)(2,1)S(1)}, u32[]{:S(2)}, u32[]{:S(2)}) %all-to-all-start.2) | async-done | bytes 524320 | tf_op jit(solution)/shard_map/all_to_all | solution.py:151
  66.5 0.0 copy-start.3
  66.5 0.7 copy-done.3
  67.2 0.8 gaps.1
  68.1 22.3 %all_to_all.24.back_ref = bf16[64,32,128]{2,1,0:T(8,128)(2,1)S(1)} all-to-all(bf16[64,32,128]{2,1,0:T(8,128)(2,1)S(1)} %gaps.1), channel_id=1, replica_groups=mesh['tm'=8,'y'=8,'z'=8] {'y','z'}, dimensions={0} | all-to-all | bytes 1048576 | tf_op jit(solution)/shard_map/all_to_all | solution.py:188
  90.4 4.9 %finish.1 = f32[48,2048]{1,0:T(8,128)} custom-call(f32[48,2048]{1,0:T(8,128)S(1)} %copy-done.1, f32[2,2048]{1,0:T(2,128)S(1)} %get-tuple-element.8.shift_ref, s32[4,2048]{1,0:T(4,128)S(1)} %get-tuple-element.9.places_ref, bf16[64,32,128]{2,1,0:T(8,128)(2,1)S(1)} %all_to_all.24.back_ref), custom_call_target="tpu_custom_call" | custom-call | tf_op jit(solution)/shard_map/finish/pallas_call | solution.py:189
  (5 shorter events, 0.1 us)
Async XLA Ops:
  0.0 1.0 %copy-start = (f32[48,2048]{1,0:T(8,128)S(1)}, f32[48,2048]{1,0:T(8,128)}, u32[]{:S(2)}) copy-start(f32[48,2048]{1,0:T(8,128)} %leaf_ref.5) | copy-start | bytes 1179652
  1.0 13.4 %copy-start.1 = (f32[48,2048]{1,0:T(8,128)S(1)}, f32[48,2048]{1,0:T(8,128)}, u32[]{:S(2)}) copy-start(f32[48,2048]{1,0:T(8,128)} %leaf_ref.5) | copy-start | bytes 1179652
  1.7 12.7 %all-to-all-start = ((f32[8,1,2048]{2,1,0:T(1,128)}), f32[8,1,2048]{2,1,0:T(1,128)S(1)}, u32[]{:S(2)}, u32[]{:S(2)}) async-start(f32[8,1,2048]{2,1,0:T(1,128)} %broadcast_in_dim.2), calls=%async_computation | async-start | bytes 131072 | tf_op jit(solution)/shard_map/all_to_all | solution.py:166
  10.8 3.6 %copy-start.2 = (f32[5,2048]{1,0:T(8,128)S(1)}, f32[5,2048]{1,0:T(8,128)}, u32[]{:S(2)}) copy-start(f32[5,2048]{1,0:T(8,128)} %seas_ref.1) | copy-start | bytes 122884
  14.4 0.7 copy-start.5
  14.4 0.7 copy-start.6
  14.4 0.7 copy-start.4
  40.6 10.3 %copy-start.7 = (f32[48,8]{0,1:T(8,128)S(1)}, f32[48,8]{0,1:T(8,128)}, u32[]{:S(2)}) copy-start(f32[48,8]{0,1:T(8,128)} %param.14) | copy-start | bytes 4612
  40.6 10.3 %copy-start.8 = (f32[48,1]{0,1:T(1,128)S(1)}, f32[48,1]{0,1:T(1,128)}, u32[]{:S(2)}) copy-start(f32[48,1]{0,1:T(1,128)} %param.15) | copy-start | bytes 580
  40.6 25.8 %all-to-all-start.2 = ((bf16[8,8,32,128]{3,2,1,0:T(8,128)(2,1)}), bf16[8,8,32,128]{3,2,1,0:T(8,128)(2,1)S(1)}, u32[]{:S(2)}, u32[]{:S(2)}) async-start(bf16[8,8,32,128]{3,2,1,0:T(8,128)(2,1)} %copy.11), calls=%async_computation.2 | async-start | bytes 1048576 | tf_op jit(solution)/shard_map/all_to_all | solution.py:151
  66.5 0.7 copy-start.3

commit v3 on v1

v3 whole, which is shorter than its diff:
```python
import jax
import jax.numpy as jnp
from jax import lax
from jax.experimental import pallas as pl
from jax.experimental.pallas import tpu as pltpu
from jax.sharding import PartitionSpec as P

f32 = jnp.float32
bf16 = jnp.bfloat16
i32 = jnp.int32

PARAMS = pltpu.CompilerParams(vmem_limit_bytes=40 * 1024 * 1024)

ID = 48
ONE = 49
MID_COUNT = 122
TOP_COUNT = 126


def iota(shape, dim):
    return lax.broadcasted_iota(i32, shape, dim)


def lane_of(x):
    return jnp.where(x < 15, x + 49, x + 98)


def ones_where(mask):
    return jnp.where(mask, 1.0, 0.0).astype(bf16)


def dot(a, b):
    return jnp.dot(a, b, preferred_element_type=f32)


def slot_lanes(shape, dim):
    return (iota(shape, dim) & 63) <= ID


def corrections(seas, parts, quarter, days):
    per = parts.shape[0] // 4
    season_days = days * per
    own = jnp.sum(jnp.where(iota(parts.shape, 0) // per == quarter, parts, 0.0), axis=0, keepdims=True)
    rows = iota(seas.shape, 0)
    seas_own = jnp.sum(jnp.where(rows == quarter, seas, 0.0), axis=0, keepdims=True)
    seas_four = jnp.sum(jnp.where(rows < 4, seas, 0.0), axis=0, keepdims=True)
    year = 0.5 * jnp.sum(parts, axis=0, keepdims=True) + 0.5 * seas_four
    first = 0.5 * (seas_own - own) / season_days
    second = 0.5 * (seas[4:5, :] - year) / (season_days * 4)
    return first, second


def day_sum_kernel(leaf_ref, out_ref):
    out_ref[...] = jnp.broadcast_to(jnp.sum(leaf_ref[...], axis=0, keepdims=True)[None], out_ref.shape)


def rank_kernel(owners, fine_ref, places_ref):
    rows = fine_ref.shape[1]
    owner = fine_ref[...] >> 6
    step = min(256, rows)
    before = ones_where(iota((step, step), 0) < iota((step, step), 1))
    base = jnp.zeros((owners, 1), f32)
    for at in range(0, rows, step):
        own = owner[:, at:at + step]
        hit = own == iota((owners, step), 0)
        hit_f = jnp.where(hit, 1.0, 0.0)
        seen = dot(hit_f.astype(bf16), before) + base
        rank = jnp.sum(jnp.where(hit, seen, 0.0), axis=0, keepdims=True).astype(i32)
        base = base + jnp.sum(hit_f, axis=1, keepdims=True)
        place = own * 16 + (rank & 15)
        places_ref[0:1, at:at + step] = jnp.where(rank < 16, place, -1)
        places_ref[1:2, at:at + step] = jnp.where(rank < 16, -1, place)


def split_count(sums):
    high = sums.astype(bf16).astype(f32)
    return jnp.where(iota(sums.shape, 1) == 64 + ONE, sums - high, high).astype(bf16)


def send_kernel(quarter_ref, leaf_ref, seas_ref, parts_ref, places_ref, fine_ref, mid_ref, top_ref, pay_ref, shift_ref, wide_ref):
    days, rows = leaf_ref.shape
    owners = pay_ref.shape[0]
    first, second = corrections(seas_ref[...], parts_ref[...], quarter_ref[0], days)
    shift_ref[0:1, :] = first
    shift_ref[1:2, :] = second
    daily = (leaf_ref[...] + first) + second
    local = fine_ref[...] & 63

    rounded = daily.astype(bf16).astype(f32)
    ext = jnp.concatenate([rounded, local.astype(f32), jnp.ones((1, rows), f32), jnp.zeros((14, rows), f32)], axis=0)
    for at in range(0, rows, 128):
        turned = jnp.transpose(ext[:, at:at + 128])
        wide_ref[at:at + 128, :] = jnp.concatenate([turned, turned], axis=1).astype(bf16)
    wide = wide_ref[...]

    place_low, place_high = places_ref[0:1, :], places_ref[1:2, :]
    mid = mid_ref[...]
    square = (128, 128)
    source, lane = iota(square, 0), iota(square, 1)
    mid_even = ones_where(((source < 24) & (lane == lane_of(source))) | ((source == ONE) & (lane == MID_COUNT)))
    mid_odd = ones_where(
        ((source >= 88) & (source < 112) & (lane == lane_of(source - 88))) | ((source == 64 + ONE) & (lane == MID_COUNT))
    )
    third = source // 3
    top_move = ones_where(
        ((source < 48) & (lane == lane_of(25 + source - 3 * third)))
        | (((source == ONE) | (source == 64 + ONE)) & (lane == TOP_COUNT))
    )
    weave = ones_where(lane == (source >> 1) + 64 * (source & 1))
    row_in = source & 15
    keep_top = (
        ((lane < 48) & (lane // 3 == row_in))
        | ((lane == ONE) & ((source & 1) == 0))
        | ((lane == 64 + ONE) & ((source & 1) == 1))
    )

    tops = split_count(dot(ones_where(iota((owners, rows), 0) == top_ref[...]), wide))
    group = min(8, owners)
    chunk = group * 16
    low_half = iota((chunk, 128), 1) < 64
    for g in range(owners // group):
        row = iota((chunk, rows), 0) + g * chunk
        slots = jnp.where(
            low_half,
            dot(ones_where(row == place_low), wide),
            dot(ones_where(row == place_high), wide),
        )
        mid_row = iota((group * 8, rows), 0) + g * (group * 8)
        mids = split_count(dot(ones_where(mid_row == mid), wide))
        mids = jnp.concatenate([dot(mids, mid_even), dot(mids, mid_odd)], axis=0).astype(bf16)
        own = ones_where(iota((chunk, owners), 1) == (iota((chunk, owners), 0) >> 4) + g * group)
        top = jnp.where(keep_top, dot(own, tops), 0.0).astype(bf16)
        rest = dot(weave, mids) + dot(top, top_move)
        tile = jnp.where(slot_lanes(square, 1), slots, rest).astype(bf16)
        pay_ref[pl.ds(g * group, group), :, :] = tile.reshape(group, 16, 128)


def owner_kernel(got_ref, base_fine_ref, base_rest_ref, back_ref):
    owners = got_ref.shape[0]
    days, nodes = base_fine_ref.shape
    got = got_ref[...].astype(f32)
    flat = got.reshape(owners * 16, 128)
    lanes = iota(flat.shape, 1)
    node = iota((owners * 16, nodes), 1).astype(f32)
    pick_low = ones_where(flat[:, ID:ID + 1] == node)
    pick_high = ones_where(flat[:, 64 + ID:65 + ID] == node)
    turned = jnp.transpose(jnp.where((lanes & 63) == ONE, 1.0, flat)).astype(bf16)
    totals = dot(turned[0:64, :], pick_low) + dot(turned[64:128, :], pick_high)
    gap = (base_fine_ref[...] - totals[0:days, :]) / (totals[ONE:ONE + 1, :] + 1.0)
    gap = jnp.concatenate([gap, jnp.zeros((64 - days, nodes), f32)], axis=0)
    gap = jnp.transpose(jnp.concatenate([gap, gap], axis=0)).astype(bf16)
    spread = jnp.where(lanes < 64, dot(pick_low, gap), dot(pick_high, gap))

    rest = jnp.sum(got, axis=0)
    up = jnp.concatenate([rest[1:16, :], rest[0:1, :]], axis=0)
    down = jnp.concatenate([rest[15:16, :], rest[0:15, :]], axis=0)
    pair = rest + jnp.where((iota(rest.shape, 0) & 1) == 0, up, down)
    top_lane = iota(rest.shape, 1) > MID_COUNT
    count = jnp.where(top_lane, pair[:, TOP_COUNT:TOP_COUNT + 1], pair[:, MID_COUNT:MID_COUNT + 1])
    gap_rest = jnp.where(slot_lanes(rest.shape, 1), 0.0, (base_rest_ref[...] - rest) / (count + 1.0))
    spread = jnp.where(slot_lanes(flat.shape, 1), spread, 0.0).reshape(owners, 16, 128)
    back_ref[...] = (spread + gap_rest[None]).astype(bf16)


def finish_kernel(leaf_ref, shift_ref, places_ref, mid_ref, top_ref, back_ref, out_ref):
    days, rows = leaf_ref.shape
    owners = back_ref.shape[0]
    height = owners * 16
    turned = jnp.transpose(back_ref[...].astype(f32).reshape(height, 128)).astype(bf16)
    day, lane = iota((days, 128), 0), iota((days, 128), 1)
    from_even = dot(ones_where((day < 24) & (lane == lane_of(day))), turned)
    from_odd = dot(ones_where((day >= 24) & (lane == lane_of(day - 24))), turned)
    column = iota((days, height), 1)
    mids = jnp.where((column & 1) == 0, from_even, from_odd).astype(bf16)
    chunk = min(128, height)
    pair = ones_where(iota((chunk, chunk // 2), 0) >> 1 == iota((chunk, chunk // 2), 1))
    mids = [dot(mids[:, at:at + chunk], pair) for at in range(0, height, chunk)]
    third = day // 3
    tops = dot(ones_where(lane == lane_of(25 + day - 3 * third)), turned)
    tops = jnp.where(iota((days, height), 0) // 3 == (column & 15), tops, 0.0).astype(bf16)
    tops = dot(tops, ones_where(iota((height, owners), 0) >> 4 == iota((height, owners), 1)))
    low, high = turned[0:days, :], turned[64:64 + days, :]
    mids = jnp.concatenate(mids, axis=1).astype(bf16)
    tops = tops.astype(bf16)
    step = min(256, rows)
    for at in range(0, rows, step):
        row = iota((height, step), 0)
        mid_row = iota((owners * 8, step), 0)
        top_row = iota((owners, step), 0)
        daily = (leaf_ref[:, at:at + step] + shift_ref[0:1, at:at + step]) + shift_ref[1:2, at:at + step]
        place = places_ref[:, at:at + step]
        fine = dot(low, ones_where(row == place[0:1, :])) + dot(high, ones_where(row == place[1:2, :]))
        mid = dot(mids, ones_where(mid_row == mid_ref[:, at:at + step]))
        top = dot(tops, ones_where(top_row == top_ref[:, at:at + step]))
        out_ref[:, at:at + step] = ((daily + fine) + mid) + top


def per_device(leaf, seas, fine, mid, top, base_fine, base_mid, base_top):
    days, rows = leaf.shape
    owners = lax.axis_size("series")
    blocks = lax.axis_size("tm")
    quarter = (lax.axis_index("tm") // (blocks // 4)).astype(i32).reshape(1)
    fine, mid, top = (ids.reshape(1, rows) for ids in (fine, mid, top))
    base_mids = base_mid.T.reshape(16, 24)
    base_rest = jnp.concatenate([base_mids, jnp.zeros((16, 1), f32), base_top.reshape(16, 3), jnp.zeros((16, 2), f32)], axis=1)
    gap = jnp.zeros((16, 49), f32)
    base_rest = jnp.concatenate([gap, base_rest[:, :15], gap, base_rest[:, 15:]], axis=1)

    sums = pl.pallas_call(
        day_sum_kernel, out_shape=jax.ShapeDtypeStruct((blocks, 1, rows), f32), compiler_params=PARAMS, name="day_sums"
    )(leaf)
    parts = lax.all_to_all(sums, "tm", 0, 0, tiled=True).reshape(blocks, rows)
    places = pl.pallas_call(
        lambda *refs: rank_kernel(owners, *refs),
        out_shape=jax.ShapeDtypeStruct((2, rows), i32),
        compiler_params=PARAMS,
        cost_estimate=pl.CostEstimate(flops=2 * owners * rows * 256, bytes_accessed=12 * rows, transcendentals=0),
        name="ranks",
    )(fine)

    vmem = pl.BlockSpec(memory_space=pltpu.VMEM)
    payload, shift = pl.pallas_call(
        send_kernel,
        out_shape=(jax.ShapeDtypeStruct((owners, 16, 128), bf16), jax.ShapeDtypeStruct((2, rows), f32)),
        in_specs=[pl.BlockSpec(memory_space=pltpu.SMEM)] + [vmem] * 7,
        scratch_shapes=[pltpu.VMEM((rows, 128), bf16)],
        compiler_params=PARAMS,
        name="pack",
    )(quarter, leaf, seas, parts, places, fine, mid, top)
    got = lax.all_to_all(payload, "series", 0, 0, tiled=True)
    back = pl.pallas_call(
        owner_kernel,
        out_shape=jax.ShapeDtypeStruct((owners, 16, 128), bf16),
        compiler_params=PARAMS,
        name="gaps",
    )(got, base_fine, base_rest)
    back = lax.all_to_all(back, "series", 0, 0, tiled=True)
    return pl.pallas_call(
        finish_kernel,
        out_shape=jax.ShapeDtypeStruct((days, rows), f32),
        compiler_params=PARAMS,
        name="finish",
    )(leaf, shift, places, mid, top, back)


def solution(mesh):
    return jax.shard_map(
        per_device,
        mesh=mesh,
        in_specs=(
            P("tm", "series"),
            P(None, "series"),
            P("series", None),
            P("series", None),
            P("series", None),
            P("tm", "series"),
            P("tm", "series"),
            P("tm", "series"),
        ),
        out_specs=P("tm", "series"),
        check_vma=False,
    )
```

time: 87.4 us -> 72.3 us (0.83)
  blocking collectives: 40 us -> 18.4 us
  starting transfers between devices: 14.1 us -> 21.5 us
  waiting for transfers between devices: 19.3 us -> 15.6 us
  local copies, waits for them, and re-layouts: 1.83 us -> 3.34 us
    all_gather x1 -> x0, blocking collectives: 15.5 us -> none  [per_device(): parts = lax.all_gather(sums, 'tm', axis=0, tiled=True)]
    all_to_all x0 -> x1, starting transfers between devices: none -> 9.27 us  [per_device(): parts = lax.all_to_all(sums, 'tm', 0, 0, tiled=True).reshape(blocks, rows)]
    all_to_all x1, waiting for transfers between devices: 19.3 us -> 12.5 us  [per_device(): got = lax.all_to_all(payload, 'series', 0, 0, tiled=True)]
    all_to_all x1, blocking collectives: 24.5 us -> 18.4 us  [per_device(): back = lax.all_to_all(back, 'series', 0, 0, tiled=True)]
    all_to_all x0 -> x1, waiting for transfers between devices: none -> 3.17 us  [per_device(): parts = lax.all_to_all(sums, 'tm', 0, 0, tiled=True).reshape(blocks, rows)]
    all_to_all x1, starting transfers between devices: 14.1 us -> 12.2 us  [per_device(): got = lax.all_to_all(payload, 'series', 0, 0, tiled=True)]
    pallas_call x3 -> x4, Pallas kernels: 6.32 us -> 8.13 us  [the longest x1 6.29 us: per_device(): pl.pallas_call(send_kernel, out_shape=(jax.ShapeDtypeStruct((owners, 16,...]
    pallas_call x1, Pallas kernels: 4.9 us -> 3.33 us  [per_device(): pl.pallas_call(finish_kernel, out_shape=jax.ShapeDtypeStruct((days, rows)...]
  transfers between devices with their start and end apart: 1 -> 2, of which waited for: 1 -> 2; matrix products, arithmetic and copies ran while one was open for 0% -> 2% of each run, Pallas kernels for 0% -> 0%
where the time goes in v3:
time: 72.3 us; the launch traced here: 71.2 us
  starting transfers between devices  21.5 us (30%)
  blocking collectives  18.4 us (25%)
  waiting for transfers between devices  15.6 us (22%)
  Pallas kernels  11.5 us (16%)
  local copies, waits for them, and re-layouts  3.34 us (5%)
  other arithmetic  0.81 us (1%)
    all_to_all x1, blocking collectives, per_device(): back = lax.all_to_all(back, 'series', 0, 0, tiled=True)  18.4 us
    all_to_all x1, waiting for transfers between devices, per_device(): got = lax.all_to_all(payload, 'series', 0, 0, tiled=True)  12.5 us
    all_to_all x1, starting transfers between devices, per_device(): got = lax.all_to_all(payload, 'series', 0, 0, tiled=True)  12.2 us
    all_to_all x1, starting transfers between devices, per_device(): parts = lax.all_to_all(sums, 'tm', 0, 0, tiled=True).reshape(blocks, rows)  9.27 us
    pallas_call x1, Pallas kernels, per_device(): pl.pallas_call(send_kernel, out_shape=(jax.ShapeDtypeStruct((owners, 16,...  6.29 us
    pallas_call x1, Pallas kernels, per_device(): pl.pallas_call(finish_kernel, out_shape=jax.ShapeDtypeStruct((days, rows)...  3.33 us
    all_to_all x1, waiting for transfers between devices, per_device(): parts = lax.all_to_all(sums, 'tm', 0, 0, tiled=True).reshape(blocks, rows)  3.17 us
    unnamed x20, local copies, waits for them, and re-layouts  2.96 us
  transfers between devices with their start and end apart: 2, of which 2 were waited for; matrix products, arithmetic and copies ran while one was open for 2% of the time, Pallas kernels for 0%

profile of v3, /device:TPU:6, one launch (start us, length us, event | category | flops | bytes accessed | tf_op | source)
XLA Modules:
  0.0 71.2 jit_solution(9671672409723839077)
XLA Ops:
  0.0 0.0 copy-start
  0.0 1.0 %copy-done = f32[48,2048]{1,0:T(8,128)S(1)} copy-done((f32[48,2048]{1,0:T(8,128)S(1)}, f32[48,2048]{1,0:T(8,128)}, u32[]{:S(2)}) %copy-start) | copy-done | bytes 393240
  1.0 0.0 copy-start.6
  1.0 0.7 day_sums.1
  1.7 0.0 copy-start.1
  1.7 9.3 %all-to-all-start = ((f32[8,1,2048]{2,1,0:T(1,128)}), f32[8,1,2048]{2,1,0:T(1,128)S(1)}, u32[]{:S(2)}, u32[]{:S(2)}) async-start(f32[8,1,2048]{2,1,0:T(1,128)} %day_sums.1), calls=%async_computation | async-start | bytes 131072 | tf_op jit(solution)/shard_map/all_to_all | solution.py:212
  10.9 0.0 copy-done.6
  10.9 0.3 ranks.1.places_ref
  11.3 0.0 copy-start.2
  11.3 3.2 %all-to-all-done = f32[8,1,2048]{2,1,0:T(1,128)S(1)} async-done(((f32[8,1,2048]{2,1,0:T(1,128)}), f32[8,1,2048]{2,1,0:T(1,128)S(1)}, u32[]{:S(2)}, u32[]{:S(2)}) %all-to-all-start) | async-done | bytes 65568 | tf_op jit(solution)/shard_map/all_to_all | solution.py:212
  14.5 0.0 copy-start.3
  14.5 0.0 copy-start.4
  14.5 0.0 copy-done.1
  14.5 0.0 copy-done.2
  14.5 0.6 copy-done.3
  15.2 0.0 copy-done.4
  15.2 6.3 %pack.1 = (bf16[64,16,128]{2,1,0:T(8,128)(2,1)}, f32[2,2048]{1,0:T(2,128)S(1)}) custom-call(s32[1]{0:T(128)} %bitcast.quarter_ref, f32[48,2048]{1,0:T(8,128)S(1)} %copy-done.1, f32[5,2048]{1,0:T(8,128)S(1)} %copy-done.2, f32[8,2048]{1,0:T(8,128)S(1)} %bitcast.10, s32[2,2048]{1,0:T(2,128)S(1)} %ranks.1.places_ref, s32[1,2048]{1,0:T(1,128)S(1)} %bitcast.16, ...), custom_call_target="tpu_custom_call" | custom-call | tf_op jit(solution)/shard_map/pack/pallas_call | solution.py:222
  21.5 12.2 %all-to-all-start.1 = ((bf16[64,16,128]{2,1,0:T(8,128)(2,1)}), bf16[64,16,128]{2,1,0:T(8,128)(2,1)S(1)}, u32[]{:S(2)}, u32[]{:S(2)}) async-start(bf16[64,16,128]{2,1,0:T(8,128)(2,1)} %get-tuple-element.8), calls=%async_computation.1 | async-start | bytes 524288 | tf_op jit(solution)/shard_map/all_to_all | solution.py:230
  33.7 0.1 pad.5.clone
  33.8 0.1 slice.9
  33.9 0.0 copy-start.8
  33.9 0.5 broadcast.14
  34.4 0.1 copy-done.8
  34.5 0.7 reduce.3
  35.2 0.0 copy-start.7
  35.2 0.1 reshape.27
  35.3 0.6 copy-done.7
  35.9 0.1 reshape.26
  36.0 0.1 pad_slice_fusion
  36.0 0.1 fusion.1
  36.1 0.0 copy-start.5
  36.1 0.1 pad_maximum_fusion.2.base_rest_ref
  36.2 12.5 %all-to-all-done.1.got_ref = bf16[64,16,128]{2,1,0:T(8,128)(2,1)S(1)} async-done(((bf16[64,16,128]{2,1,0:T(8,128)(2,1)}), bf16[64,16,128]{2,1,0:T(8,128)(2,1)S(1)}, u32[]{:S(2)}, u32[]{:S(2)}) %all-to-all-start.1) | async-done | bytes 262176 | tf_op jit(solution)/shard_map/all_to_all | solution.py:230
  48.7 0.0 copy-done.5
  48.7 0.8 %gaps.1 = bf16[64,16,128]{2,1,0:T(8,128)(2,1)S(1)} custom-call(bf16[64,16,128]{2,1,0:T(8,128)(2,1)S(1)} %all-to-all-done.1.got_ref, f32[48,64]{1,0:T(8,128)S(1)} %copy-done.5, f32[16,128]{1,0:T(8,128)S(1)} %pad_maximum_fusion.2.base_rest_ref), custom_call_target="tpu_custom_call" | custom-call | tf_op jit(solution)/shard_map/gaps/pallas_call | solution.py:231
  49.5 18.4 %all_to_all.15.back_ref = bf16[64,16,128]{2,1,0:T(8,128)(2,1)S(1)} all-to-all(bf16[64,16,128]{2,1,0:T(8,128)(2,1)S(1)} %gaps.1), channel_id=1, replica_groups=mesh['tm'=8,'series'=64] {'series'}, dimensions={0} | all-to-all | bytes 524288 | tf_op jit(solution)/shard_map/all_to_all | solution.py:237
  67.9 3.3 %finish.1 = f32[48,2048]{1,0:T(8,128)} custom-call(f32[48,2048]{1,0:T(8,128)S(1)} %copy-done.1, f32[2,2048]{1,0:T(2,128)S(1)} %get-tuple-element.7.shift_ref, s32[2,2048]{1,0:T(2,128)S(1)} %ranks.1.places_ref, s32[1,2048]{1,0:T(1,128)S(1)} %bitcast.12, s32[1,2048]{1,0:T(1,128)S(1)} %bitcast.14, bf16[64,16,128]{2,1,0:T(8,128)(2,1)S(1)} %all_to_all.15.back_ref), custom_call_target="tpu_custom_call" | custom-call | tf_op jit(solution)/shard_map/finish/pallas_call | solution.py:238
  (3 shorter events, 0.0 us)
Async XLA Ops:
  0.0 1.0 %copy-start = (f32[48,2048]{1,0:T(8,128)S(1)}, f32[48,2048]{1,0:T(8,128)}, u32[]{:S(2)}) copy-start(f32[48,2048]{1,0:T(8,128)} %leaf_ref.5) | copy-start | bytes 1179652
  1.0 9.9 %copy-start.6 = (s32[2048,1]{0,1:T(1,128)S(1)}, s32[2048,1]{0,1:T(1,128)}, u32[]{:S(2)}) copy-start(s32[2048,1]{0,1:T(1,128)} %param.10) | copy-start | bytes 24580
  1.7 12.8 %copy-start.1 = (f32[48,2048]{1,0:T(8,128)S(1)}, f32[48,2048]{1,0:T(8,128)}, u32[]{:S(2)}) copy-start(f32[48,2048]{1,0:T(8,128)} %leaf_ref.5) | copy-start | bytes 1179652
  1.7 12.8 %all-to-all-start = ((f32[8,1,2048]{2,1,0:T(1,128)}), f32[8,1,2048]{2,1,0:T(1,128)S(1)}, u32[]{:S(2)}, u32[]{:S(2)}) async-start(f32[8,1,2048]{2,1,0:T(1,128)} %day_sums.1), calls=%async_computation | async-start | bytes 131072 | tf_op jit(solution)/shard_map/all_to_all | solution.py:212
  11.3 3.2 %copy-start.2 = (f32[5,2048]{1,0:T(8,128)S(1)}, f32[5,2048]{1,0:T(8,128)}, u32[]{:S(2)}) copy-start(f32[5,2048]{1,0:T(8,128)} %seas_ref.1) | copy-start | bytes 122884
  14.5 0.7 copy-start.3
  14.5 0.7 copy-start.4
  21.5 27.2 %all-to-all-start.1 = ((bf16[64,16,128]{2,1,0:T(8,128)(2,1)}), bf16[64,16,128]{2,1,0:T(8,128)(2,1)S(1)}, u32[]{:S(2)}, u32[]{:S(2)}) async-start(bf16[64,16,128]{2,1,0:T(8,128)(2,1)} %get-tuple-element.8), calls=%async_computation.1 | async-start | bytes 524288 | tf_op jit(solution)/shard_map/all_to_all | solution.py:230
  33.9 0.7 copy-start.8
  35.2 0.7 copy-start.7
  36.1 12.5 %copy-start.5 = (f32[48,64]{1,0:T(8,128)S(1)}, f32[48,64]{1,0:T(8,128)}, u32[]{:S(2)}) copy-start(f32[48,64]{1,0:T(8,128)} %base_fine_ref.1) | copy-start | bytes 36868

commit v4 on v3

--- a/solution.py
+++ b/solution.py
@@ -37,10 +37,14 @@
     return (iota(shape, dim) & 63) <= ID
 
 
-def corrections(seas, parts, quarter, days):
-    per = parts.shape[0] // 4
+def corrections(seas, parts, block, days):
+    blocks = parts.shape[0]
+    per = blocks // 4
     season_days = days * per
-    own = jnp.sum(jnp.where(iota(parts.shape, 0) // per == quarter, parts, 0.0), axis=0, keepdims=True)
+    quarter = block // per
+    row = block - iota(parts.shape, 0)
+    row = jnp.where(row < 0, row + blocks, row)
+    own = jnp.sum(jnp.where(row // per == quarter, parts, 0.0), axis=0, keepdims=True)
     rows = iota(seas.shape, 0)
     seas_own = jnp.sum(jnp.where(rows == quarter, seas, 0.0), axis=0, keepdims=True)
     seas_four = jnp.sum(jnp.where(rows < 4, seas, 0.0), axis=0, keepdims=True)
@@ -51,7 +55,7 @@
 
 
 def day_sum_kernel(leaf_ref, out_ref):
-    out_ref[...] = jnp.broadcast_to(jnp.sum(leaf_ref[...], axis=0, keepdims=True)[None], out_ref.shape)
+    out_ref[...] = jnp.sum(leaf_ref[...], axis=0, keepdims=True)
 
 
 def rank_kernel(owners, fine_ref, places_ref):
@@ -77,10 +81,13 @@
     return jnp.where(iota(sums.shape, 1) == 64 + ONE, sums - high, high).astype(bf16)
 
 
-def send_kernel(quarter_ref, leaf_ref, seas_ref, parts_ref, places_ref, fine_ref, mid_ref, top_ref, pay_ref, shift_ref, wide_ref):
+def send_kernel(block_ref, leaf_ref, seas_ref, places_ref, fine_ref, mid_ref, top_ref, rest_ref, *refs):
+    *part_refs, pay_ref, shift_ref, rest_out_ref, wide_ref = refs
     days, rows = leaf_ref.shape
     owners = pay_ref.shape[0]
-    first, second = corrections(seas_ref[...], parts_ref[...], quarter_ref[0], days)
+    parts = jnp.concatenate([ref[...] for ref in part_refs], axis=0)
+    first, second = corrections(seas_ref[...], parts, block_ref[0], days)
+    rest_out_ref[...] = rest_ref[...]
     shift_ref[0:1, :] = first
     shift_ref[1:2, :] = second
     daily = (leaf_ref[...] + first) + second
@@ -199,7 +206,7 @@
     days, rows = leaf.shape
     owners = lax.axis_size("series")
     blocks = lax.axis_size("tm")
-    quarter = (lax.axis_index("tm") // (blocks // 4)).astype(i32).reshape(1)
+    block = lax.axis_index("tm").astype(i32).reshape(1)
     fine, mid, top = (ids.reshape(1, rows) for ids in (fine, mid, top))
     base_mids = base_mid.T.reshape(16, 24)
     base_rest = jnp.concatenate([base_mids, jnp.zeros((16, 1), f32), base_top.reshape(16, 3), jnp.zeros((16, 2), f32)], axis=1)
@@ -207,9 +214,11 @@
     base_rest = jnp.concatenate([gap, base_rest[:, :15], gap, base_rest[:, 15:]], axis=1)
 
     sums = pl.pallas_call(
-        day_sum_kernel, out_shape=jax.ShapeDtypeStruct((blocks, 1, rows), f32), compiler_params=PARAMS, name="day_sums"
+        day_sum_kernel, out_shape=jax.ShapeDtypeStruct((1, rows), f32), compiler_params=PARAMS, name="day_sums"
     )(leaf)
-    parts = lax.all_to_all(sums, "tm", 0, 0, tiled=True).reshape(blocks, rows)
+    parts = [sums] + [
+        lax.ppermute(sums, "tm", [(at, (at + hop) % blocks) for at in range(blocks)]) for hop in range(1, blocks)
+    ]
     places = pl.pallas_call(
         lambda *refs: rank_kernel(owners, *refs),
         out_shape=jax.ShapeDtypeStruct((2, rows), i32),
@@ -219,14 +228,14 @@
     )(fine)
 
     vmem = pl.BlockSpec(memory_space=pltpu.VMEM)
-    payload, shift = pl.pallas_call(
+    payload, shift, base_rest = pl.pallas_call(
         send_kernel,
-        out_shape=(jax.ShapeDtypeStruct((owners, 16, 128), bf16), jax.ShapeDtypeStruct((2, rows), f32)),
-        in_specs=[pl.BlockSpec(memory_space=pltpu.SMEM)] + [vmem] * 7,
+        out_shape=(jax.ShapeDtypeStruct((owners, 16, 128), bf16), jax.ShapeDtypeStruct((2, rows), f32), jax.ShapeDtypeStruct((16, 128), f32)),
+        in_specs=[pl.BlockSpec(memory_space=pltpu.SMEM)] + [vmem] * (7 + blocks),
         scratch_shapes=[pltpu.VMEM((rows, 128), bf16)],
         compiler_params=PARAMS,
         name="pack",
-    )(quarter, leaf, seas, parts, places, fine, mid, top)
+    )(block, leaf, seas, places, fine, mid, top, base_rest, *parts)
     got = lax.all_to_all(payload, "series", 0, 0, tiled=True)
     back = pl.pallas_call(
         owner_kernel,

time: 72.3 us -> 84.1 us (1.16)
  the two profiles are of different devices: /device:TPU:6 before, /device:TPU:2 now
where the time goes in v4:
time: 84.1 us; the launch traced here: 83.6 us
  blocking collectives  47.8 us (57%)
  starting transfers between devices  20.4 us (24%)
  Pallas kernels  10.1 us (12%)
  local copies, waits for them, and re-layouts  3.35 us (4%)
  waiting for transfers between devices  0.88 us (1%)
    all_to_all x1, blocking collectives, per_device(): got = lax.all_to_all(payload, 'series', 0, 0, tiled=True)  29 us
    ppermute x7, starting transfers between devices, per_device(): lax.ppermute(sums, 'tm', [(at, (at + hop) % blocks) for at in range(block...  20.4 us
    all_to_all x1, blocking collectives, per_device(): back = lax.all_to_all(back, 'series', 0, 0, tiled=True)  18.9 us
    pallas_call x1, Pallas kernels, per_device(): pl.pallas_call(send_kernel, out_shape=(jax.ShapeDtypeStruct((owners, 16,...  5.61 us
    pallas_call x1, Pallas kernels, per_device(): pl.pallas_call(finish_kernel, out_shape=jax.ShapeDtypeStruct((days, rows)...  3.32 us
    unnamed x19, local copies, waits for them, and re-layouts  2.97 us
  transfers between devices with their start and end apart: 7, of which 1 were waited for; matrix products, arithmetic and copies ran while one was open for 2% of the time, Pallas kernels for 0%

profile of v4, /device:TPU:2, one launch (start us, length us, event | category | flops | bytes accessed | tf_op | source)
XLA Modules:
  0.0 83.6 jit_solution(5683012464104627158)
XLA Ops:
  0.0 0.0 copy-start
  0.0 1.0 %copy-done = f32[48,2048]{1,0:T(8,128)S(1)} copy-done((f32[48,2048]{1,0:T(8,128)S(1)}, f32[48,2048]{1,0:T(8,128)}, u32[]{:S(2)}) %copy-start) | copy-done | bytes 393240
  1.0 0.0 copy-start.1
  1.0 0.0 collective-permute-start.6
  1.1 7.9 %collective-permute-start.5 = (f32[1,2048]{1,0:T(1,128)S(1)}, f32[1,2048]{1,0:T(1,128)S(1)}, u32[]{:S(2)}, u32[]{:S(2)}) collective-permute-start(f32[1,2048]{1,0:T(1,128)S(1)} %day_sums.1.refs_0_), channel_id=1, source_target_pairs={{0,384},{64,448},{128,0},{192,64},{256,128},{320,192},{384,256},{4... | collective-permute-start | bytes 24584 | tf_op jit(solution)/shard_map/ppermute | solution.py:220
  9.0 1.9 %collective-permute-start.4 = (f32[1,2048]{1,0:T(1,128)S(1)}, f32[1,2048]{1,0:T(1,128)S(1)}, u32[]{:S(2)}, u32[]{:S(2)}) collective-permute-start(f32[1,2048]{1,0:T(1,128)S(1)} %day_sums.1.refs_0_), channel_id=1, source_target_pairs={{0,320},{64,384},{128,448},{192,0},{256,64},{320,128},{384,192},{4... | collective-permute-start | bytes 24584 | tf_op jit(solution)/shard_map/ppermute | solution.py:220
  10.9 5.1 %collective-permute-start.3 = (f32[1,2048]{1,0:T(1,128)S(1)}, f32[1,2048]{1,0:T(1,128)S(1)}, u32[]{:S(2)}, u32[]{:S(2)}) collective-permute-start(f32[1,2048]{1,0:T(1,128)S(1)} %day_sums.1.refs_0_), channel_id=1, source_target_pairs={{0,256},{64,320},{128,384},{192,448},{256,0},{320,64},{384,128},{4... | collective-permute-start | bytes 24584 | tf_op jit(solution)/shard_map/ppermute | solution.py:220
  16.1 1.9 %collective-permute-start.2 = (f32[1,2048]{1,0:T(1,128)S(1)}, f32[1,2048]{1,0:T(1,128)S(1)}, u32[]{:S(2)}, u32[]{:S(2)}) collective-permute-start(f32[1,2048]{1,0:T(1,128)S(1)} %day_sums.1.refs_0_), channel_id=1, source_target_pairs={{0,192},{64,256},{128,320},{192,384},{256,448},{320,0},{384,64},{4... | collective-permute-start | bytes 24584 | tf_op jit(solution)/shard_map/ppermute | solution.py:220
  18.0 0.1 pad.5.clone
  18.1 0.1 slice.9
  18.1 0.1 pad_slice_fusion
  18.2 0.0 copy-start.8
  18.2 0.5 broadcast.13
  18.7 0.1 copy-done.8
  18.9 0.7 reduce.3
  19.5 0.0 copy-start.7
  19.5 0.1 reshape.23
  19.6 0.6 copy-done.7
  20.2 0.1 reshape.22
  20.3 0.1 fusion.1
  20.4 0.0 collective-permute-done.6.refs_7_
  20.4 2.2 %collective-permute-start.1 = (f32[1,2048]{1,0:T(1,128)S(1)}, f32[1,2048]{1,0:T(1,128)S(1)}, u32[]{:S(2)}, u32[]{:S(2)}) collective-permute-start(f32[1,2048]{1,0:T(1,128)S(1)} %day_sums.1.refs_0_), channel_id=1, source_target_pairs={{0,128},{64,192},{128,256},{192,320},{256,384},{320,448},{384,0},{... | collective-permute-start | bytes 24584 | tf_op jit(solution)/shard_map/ppermute | solution.py:220
  22.6 0.0 collective-permute-done.5.refs_6_
  22.6 1.3 %collective-permute-start = (f32[1,2048]{1,0:T(1,128)S(1)}, f32[1,2048]{1,0:T(1,128)S(1)}, u32[]{:S(2)}, u32[]{:S(2)}) collective-permute-start(f32[1,2048]{1,0:T(1,128)S(1)} %day_sums.1.refs_0_), channel_id=1, source_target_pairs={{0,64},{64,128},{128,192},{192,256},{256,320},{320,384},{384,448},... | collective-permute-start | bytes 24584 | tf_op jit(solution)/shard_map/ppermute | solution.py:220
  23.9 0.1 pad_maximum_fusion.2.rest_ref
  24.0 0.0 copy-start.6
  24.0 0.7 copy-done.6
  24.7 0.0 copy-start.2
  24.7 0.0 copy-start.3
  24.7 0.0 copy-start.4
  24.7 0.3 ranks.1.places_ref
  25.0 0.0 collective-permute-done.4.refs_5_
  25.0 0.0 collective-permute-done.3.refs_4_
  25.0 0.0 collective-permute-done.2.refs_3_
  25.0 0.9 %collective-permute-done.1.refs_2_ = f32[1,2048]{1,0:T(1,128)S(1)} collective-permute-done((f32[1,2048]{1,0:T(1,128)S(1)}, f32[1,2048]{1,0:T(1,128)S(1)}, u32[]{:S(2)}, u32[]{:S(2)}) %collective-permute-start.1) | collective-permute-done | bytes 8224 | tf_op jit(solution)/shard_map/ppermute | solution.py:220
  25.9 0.0 collective-permute-done.refs_1_
  25.9 0.0 copy-done.1
  25.9 0.0 copy-done.2
  25.9 0.0 copy-done.3
  25.9 0.0 copy-done.4
  25.9 5.6 %pack.1 = (bf16[64,16,128]{2,1,0:T(8,128)(2,1)S(1)}, f32[2,2048]{1,0:T(2,128)S(1)}, f32[16,128]{1,0:T(8,128)S(1)}) custom-call(s32[1]{0:T(128)} %bitcast.block_ref, f32[48,2048]{1,0:T(8,128)S(1)} %copy-done.1, f32[5,2048]{1,0:T(8,128)S(1)} %copy-done.2, s32[2,2048]{1,0:T(2,128)S(1)} %ranks.1.places_ref, s32[1,2048]{1,0:T(1,128)S(1)} %bitcast.12, ...), custom_call_target="tpu_custom_call" | custom-call | tf_op jit(solution)/shard_map/pack/pallas_call | solution.py:231
  31.6 0.0 copy-start.5
  31.6 29.0 %all_to_all.10.got_ref = bf16[64,16,128]{2,1,0:T(8,128)(2,1)S(1)} all-to-all(bf16[64,16,128]{2,1,0:T(8,128)(2,1)S(1)} %get-tuple-element.9), channel_id=1, replica_groups=mesh['tm'=8,'series'=64] {'series'}, dimensions={0} | all-to-all | bytes 524288 | tf_op jit(solution)/shard_map/all_to_all | solution.py:239
  60.5 0.0 copy-done.5
  60.6 0.8 gaps.1
  61.4 18.9 %all_to_all.11.back_ref = bf16[64,16,128]{2,1,0:T(8,128)(2,1)S(1)} all-to-all(bf16[64,16,128]{2,1,0:T(8,128)(2,1)S(1)} %gaps.1), channel_id=1, replica_groups=mesh['tm'=8,'series'=64] {'series'}, dimensions={0} | all-to-all | bytes 524288 | tf_op jit(solution)/shard_map/all_to_all | solution.py:246
  80.3 3.3 %finish.1 = f32[48,2048]{1,0:T(8,128)} custom-call(f32[48,2048]{1,0:T(8,128)S(1)} %copy-done.1, f32[2,2048]{1,0:T(2,128)S(1)} %get-tuple-element.8.shift_ref, s32[2,2048]{1,0:T(2,128)S(1)} %ranks.1.places_ref, s32[1,2048]{1,0:T(1,128)S(1)} %bitcast.8, s32[1,2048]{1,0:T(1,128)S(1)} %bitcast.10, bf16[64,16,128]{2,1,0:T(8,128)(2,1)S(1)} %all_to_all.11.back_ref), custom_call_target="tpu_custom_call" | custom-call | tf_op jit(solution)/shard_map/finish/pallas_call | solution.py:247
  (3 shorter events, 0.0 us)
Async XLA Ops:
  0.0 1.0 %copy-start = (f32[48,2048]{1,0:T(8,128)S(1)}, f32[48,2048]{1,0:T(8,128)}, u32[]{:S(2)}) copy-start(f32[48,2048]{1,0:T(8,128)} %leaf_ref.5) | copy-start | bytes 1179652
  1.0 24.9 %copy-start.1 = (f32[48,2048]{1,0:T(8,128)S(1)}, f32[48,2048]{1,0:T(8,128)}, u32[]{:S(2)}) copy-start(f32[48,2048]{1,0:T(8,128)} %leaf_ref.5) | copy-start | bytes 1179652
  1.0 19.3 %collective-permute-start.6 = (f32[1,2048]{1,0:T(1,128)S(1)}, f32[1,2048]{1,0:T(1,128)S(1)}, u32[]{:S(2)}, u32[]{:S(2)}) collective-permute-start(f32[1,2048]{1,0:T(1,128)S(1)} %day_sums.1.refs_0_), channel_id=1, source_target_pairs={{0,448},{64,0},{128,64},{192,128},{256,192},{320,256},{384,320},{4... | collective-permute-start | bytes 24584 | tf_op jit(solution)/shard_map/ppermute | solution.py:220
  1.1 21.6 %collective-permute-start.5 = (f32[1,2048]{1,0:T(1,128)S(1)}, f32[1,2048]{1,0:T(1,128)S(1)}, u32[]{:S(2)}, u32[]{:S(2)}) collective-permute-start(f32[1,2048]{1,0:T(1,128)S(1)} %day_sums.1.refs_0_), channel_id=1, source_target_pairs={{0,384},{64,448},{128,0},{192,64},{256,128},{320,192},{384,256},{4... | collective-permute-start | bytes 24584 | tf_op jit(solution)/shard_map/ppermute | solution.py:220
  9.0 16.0 %collective-permute-start.4 = (f32[1,2048]{1,0:T(1,128)S(1)}, f32[1,2048]{1,0:T(1,128)S(1)}, u32[]{:S(2)}, u32[]{:S(2)}) collective-permute-start(f32[1,2048]{1,0:T(1,128)S(1)} %day_sums.1.refs_0_), channel_id=1, source_target_pairs={{0,320},{64,384},{128,448},{192,0},{256,64},{320,128},{384,192},{4... | collective-permute-start | bytes 24584 | tf_op jit(solution)/shard_map/ppermute | solution.py:220
  10.9 14.1 %collective-permute-start.3 = (f32[1,2048]{1,0:T(1,128)S(1)}, f32[1,2048]{1,0:T(1,128)S(1)}, u32[]{:S(2)}, u32[]{:S(2)}) collective-permute-start(f32[1,2048]{1,0:T(1,128)S(1)} %day_sums.1.refs_0_), channel_id=1, source_target_pairs={{0,256},{64,320},{128,384},{192,448},{256,0},{320,64},{384,128},{4... | collective-permute-start | bytes 24584 | tf_op jit(solution)/shard_map/ppermute | solution.py:220
  16.1 9.0 %collective-permute-start.2 = (f32[1,2048]{1,0:T(1,128)S(1)}, f32[1,2048]{1,0:T(1,128)S(1)}, u32[]{:S(2)}, u32[]{:S(2)}) collective-permute-start(f32[1,2048]{1,0:T(1,128)S(1)} %day_sums.1.refs_0_), channel_id=1, source_target_pairs={{0,192},{64,256},{128,320},{192,384},{256,448},{320,0},{384,64},{4... | collective-permute-start | bytes 24584 | tf_op jit(solution)/shard_map/ppermute | solution.py:220
  18.2 0.7 copy-start.8
  19.5 0.7 copy-start.7
  20.4 5.5 %collective-permute-start.1 = (f32[1,2048]{1,0:T(1,128)S(1)}, f32[1,2048]{1,0:T(1,128)S(1)}, u32[]{:S(2)}, u32[]{:S(2)}) collective-permute-start(f32[1,2048]{1,0:T(1,128)S(1)} %day_sums.1.refs_0_), channel_id=1, source_target_pairs={{0,128},{64,192},{128,256},{192,320},{256,384},{320,448},{384,0},{... | collective-permute-start | bytes 24584 | tf_op jit(solution)/shard_map/ppermute | solution.py:220
  22.6 3.3 %collective-permute-start = (f32[1,2048]{1,0:T(1,128)S(1)}, f32[1,2048]{1,0:T(1,128)S(1)}, u32[]{:S(2)}, u32[]{:S(2)}) collective-permute-start(f32[1,2048]{1,0:T(1,128)S(1)} %day_sums.1.refs_0_), channel_id=1, source_target_pairs={{0,64},{64,128},{128,192},{192,256},{256,320},{320,384},{384,448},... | collective-permute-start | bytes 24584 | tf_op jit(solution)/shard_map/ppermute | solution.py:220
  24.0 0.7 copy-start.6
  24.7 1.3 %copy-start.2 = (f32[5,2048]{1,0:T(8,128)S(1)}, f32[5,2048]{1,0:T(8,128)}, u32[]{:S(2)}) copy-start(f32[5,2048]{1,0:T(8,128)} %seas_ref.1) | copy-start | bytes 122884
  24.7 1.3 %copy-start.3 = (s32[2048,1]{0,1:T(1,128)S(1)}, s32[2048,1]{0,1:T(1,128)}, u32[]{:S(2)}) copy-start(s32[2048,1]{0,1:T(1,128)} %param.11) | copy-start | bytes 24580
  24.7 1.3 %copy-start.4 = (s32[2048,1]{0,1:T(1,128)S(1)}, s32[2048,1]{0,1:T(1,128)}, u32[]{:S(2)}) copy-start(s32[2048,1]{0,1:T(1,128)} %param.12) | copy-start | bytes 24580
  31.6 29.0 %copy-start.5 = (f32[48,64]{1,0:T(8,128)S(1)}, f32[48,64]{1,0:T(8,128)}, u32[]{:S(2)}) copy-start(f32[48,64]{1,0:T(8,128)} %base_fine_ref.1) | copy-start | bytes 36868

commit v5 on v3

v5 whole, which is shorter than its diff:
```python
import jax
import jax.numpy as jnp
from jax import lax
from jax.experimental import pallas as pl
from jax.experimental.pallas import tpu as pltpu
from jax.sharding import PartitionSpec as P

f32 = jnp.float32
bf16 = jnp.bfloat16
i32 = jnp.int32

PARAMS = pltpu.CompilerParams(vmem_limit_bytes=28 * 1024 * 1024)

ID = 48
ONE = 49
LOW = 50
MID_COUNT = 122
TOP_COUNT = 126
TOP_ROWS = 128


def iota(shape, dim):
    return lax.broadcasted_iota(i32, shape, dim)


def lane_of(x):
    return jnp.where(x < 15, x + 49, x + 98)


def top_lane(day):
    return lane_of(25 + day - 3 * (day // 3))


def ones_where(mask):
    return jnp.where(mask, 1.0, 0.0).astype(bf16)


def dot(a, b):
    return jnp.dot(a, b, preferred_element_type=f32)


def dot_nt(a, b, precision=None):
    return lax.dot_general(a, b, (((1,), (1,)), ((), ())), precision=precision, preferred_element_type=f32)


def slot_lanes(shape, dim):
    return (iota(shape, dim) & 63) <= ID


def row_of(dense):
    return jnp.concatenate([dense[at:at + 1, :] for at in range(dense.shape[0])], axis=1)


def corrections(seas, parts, quarter, days):
    per = parts.shape[0] // 4
    season_days = days * per
    own = row_of(jnp.sum(jnp.where(iota(parts.shape, 0) // per == quarter, parts, 0.0), axis=0))
    rows = iota(seas.shape, 0)
    seas_own = jnp.sum(jnp.where(rows == quarter, seas, 0.0), axis=0, keepdims=True)
    seas_four = jnp.sum(jnp.where(rows < 4, seas, 0.0), axis=0, keepdims=True)
    year = 0.5 * row_of(jnp.sum(parts, axis=0)) + 0.5 * seas_four
    first = 0.5 * (seas_own - own) / season_days
    second = 0.5 * (seas[4:5, :] - year) / (season_days * 4)
    return first, second


def day_sum_kernel(leaf_ref, out_ref):
    sums = jnp.sum(leaf_ref[...], axis=0, keepdims=True)
    dense = jnp.concatenate([sums[:, at:at + 128] for at in range(0, sums.shape[1], 128)], axis=0)
    out_ref[...] = jnp.broadcast_to(dense[None], out_ref.shape)


def tables_kernel(owners, fine_ref, mid_ref, top_ref, base_mid_ref, base_top_ref, hits_ref, base_ref):
    rows = fine_ref.shape[1]
    owner = fine_ref[...] >> 6
    step = min(256, rows)
    before = ones_where(iota((step, step), 0) < iota((step, step), 1))
    base = jnp.zeros((owners, 1), f32)
    ranks = []
    for at in range(0, rows, step):
        hit = owner[:, at:at + step] == iota((owners, step), 0)
        hit_f = jnp.where(hit, 1.0, 0.0)
        seen = dot(hit_f.astype(bf16), before) + base
        ranks.append(jnp.sum(jnp.where(hit, seen, 0.0), axis=0, keepdims=True))
        base = base + jnp.sum(hit_f, axis=1, keepdims=True)
    rank = jnp.concatenate(ranks, axis=1).astype(i32)
    place = owner * 16 + (rank & 15)
    place_low = jnp.where(rank < 16, place, -1)
    place_high = jnp.where(rank < 16, -1, place)
    at = 0
    for place, height in ((place_low, owners * 16), (place_high, owners * 16), (mid_ref[...], owners * 8), (top_ref[...], TOP_ROWS)):
        chunk = min(64, height)
        for start in range(0, height, chunk):
            hits_ref[at:at + chunk, :] = ones_where(iota((chunk, rows), 0) + start == place)
            at += chunk

    days = base_mid_ref.shape[1]
    half = days // 2
    day, lane = iota((days, 128), 0), iota((days, 128), 1)
    moves = (
        (day < half) & (lane == lane_of(day)),
        (day >= half) & (lane == lane_of(day - half)),
        lane == top_lane(day),
    )
    moves = [jnp.where(move, 1.0, 0.0) for move in moves]
    top = jnp.where(iota((16, days), 1) // 3 == iota((16, days), 0), base_top_ref[...], 0.0)
    exact = lax.Precision.HIGHEST
    mids = [jnp.dot(base_mid_ref[...], move, precision=exact, preferred_element_type=f32) for move in moves[:2]]
    base_ref[...] = jnp.concatenate(mids, axis=0) + jnp.dot(top, moves[2], precision=exact, preferred_element_type=f32)


def split_count(sums):
    high = sums.astype(bf16).astype(f32)
    return jnp.where(iota(sums.shape, 0) == LOW, sums - high, high)


def send_kernel(quarter_ref, leaf_ref, seas_ref, parts_ref, fine_ref, hits_ref, pay_ref, shift_ref):
    days, rows = leaf_ref.shape
    owners = pay_ref.shape[0]
    slots, mids = owners * 16, owners * 8
    first, second = corrections(seas_ref[...], parts_ref[...], quarter_ref[0], days)
    shift_ref[0:1, :] = first
    shift_ref[1:2, :] = second
    daily = (leaf_ref[...] + first) + second
    local = fine_ref[...] & 63
    ext = jnp.concatenate([daily, local.astype(f32), jnp.ones((2, rows), f32), jnp.zeros((13, rows), f32)], axis=0)
    sums = dot_nt(ext.astype(bf16), hits_ref[...])

    tops = split_count(sums[:, 2 * slots + mids:]).astype(bf16)
    tops = dot(tops, ones_where(iota((TOP_ROWS, slots), 0) == iota((TOP_ROWS, slots), 1) >> 4))
    row, column = iota((64, slots), 0), iota((64, slots), 1) & 15
    keep = (
        ((row < days) & (row // 3 == column))
        | ((row == ONE) & (column < 8))
        | ((row == LOW) & (column >= 8))
    )
    tops = jnp.where(keep, tops, 0.0).astype(bf16)
    lane, day = iota((128, 64), 0), iota((128, 64), 1)
    top_move = ((day < days) & (lane == top_lane(day))) | (((day == ONE) | (day == LOW)) & (lane == TOP_COUNT))
    tops = dot(ones_where(top_move), tops)
    tiles = jnp.concatenate([sums[:, :slots], sums[:, slots:2 * slots]], axis=0)
    tiles = jnp.where(slot_lanes((128, slots), 0), tiles, tops)

    half = days // 2
    mid_sums = split_count(sums[:, 2 * slots:2 * slots + mids])
    day, lane = iota((64, 128), 0), iota((64, 128), 1)
    moves = (
        ((day < half) & (lane == lane_of(day))) | ((day == ONE) & (lane == MID_COUNT)),
        ((day >= half) & (day < days) & (lane == lane_of(day - half))) | ((day == LOW) & (lane == MID_COUNT)),
    )
    moves = [ones_where(move) for move in moves]
    group = min(16, owners)
    for g in range(owners // group):
        own = jnp.transpose(mid_sums[:, g * group * 8:(g + 1) * group * 8]).astype(bf16)
        extra = jnp.concatenate([dot(own, move).reshape(group, 8, 128) for move in moves], axis=1)
        start, stop = g * group * 16, (g + 1) * group * 16
        tile = jnp.concatenate([jnp.transpose(tiles[:, at:at + 128]) for at in range(start, stop, 128)], axis=0)
        pay_ref[g * group:(g + 1) * group, :, :] = (tile.reshape(group, 16, 128) + extra).astype(bf16)


def owner_kernel(got_ref, base_fine_ref, base_rest_ref, back_ref):
    owners = got_ref.shape[0]
    days, nodes = base_fine_ref.shape
    got = got_ref[...].astype(f32)
    flat = got.reshape(owners * 16, 128)
    lanes = iota(flat.shape, 1)
    node = iota((owners * 16, nodes), 1).astype(f32)
    pick_low = ones_where(flat[:, ID:ID + 1] == node)
    pick_high = ones_where(flat[:, 64 + ID:65 + ID] == node)
    turned = jnp.transpose(jnp.where((lanes & 63) == ONE, 1.0, flat)).astype(bf16)
    totals = dot(turned[0:64, :], pick_low) + dot(turned[64:128, :], pick_high)
    gap = (base_fine_ref[...] - totals[0:days, :]) / (totals[ONE:ONE + 1, :] + 1.0)
    gap = jnp.concatenate([gap, jnp.zeros((64 - days, nodes), f32)], axis=0)
    gap = jnp.transpose(jnp.concatenate([gap, gap], axis=0)).astype(bf16)
    spread = jnp.where(lanes < 64, dot(pick_low, gap), dot(pick_high, gap))

    rest = jnp.sum(got, axis=0)
    pair = rest + jnp.concatenate([rest[8:16, :], rest[0:8, :]], axis=0)
    of_top = iota(rest.shape, 1) > MID_COUNT
    count = jnp.where(of_top, pair[:, TOP_COUNT:TOP_COUNT + 1], pair[:, MID_COUNT:MID_COUNT + 1])
    gap_rest = jnp.where(slot_lanes(rest.shape, 1), 0.0, (base_rest_ref[...] - rest) / (count + 1.0))
    spread = jnp.where(slot_lanes(flat.shape, 1), spread, 0.0).reshape(owners, 16, 128)
    back_ref[...] = (spread + gap_rest[None]).astype(bf16)


def finish_kernel(leaf_ref, shift_ref, hits_ref, back_ref, out_ref):
    days, rows = leaf_ref.shape
    owners = back_ref.shape[0]
    slots, mids = owners * 16, owners * 8
    half = days // 2
    back = back_ref[...].astype(f32)
    day, lane = iota((days, 128), 0), iota((days, 128), 1)
    take = jnp.concatenate([ones_where(lane == day), ones_where(lane == day + 64), ones_where(lane == top_lane(day))], axis=0)
    taken = dot_nt(take, back.reshape(slots, 128).astype(bf16))
    tops = jnp.where(iota((days, slots), 0) // 3 == (iota((days, slots), 1) & 15), taken[2 * days:, :], 0.0).astype(bf16)
    tops = dot(tops, ones_where(iota((slots, TOP_ROWS), 0) >> 4 == iota((slots, TOP_ROWS), 1)))
    first, last = (back[:, at:at + 8, :].reshape(mids, 128).astype(bf16) for at in (0, 8))
    mid = dot_nt(ones_where((day < half) & (lane == lane_of(day))), first)
    mid = mid + dot_nt(ones_where((day >= half) & (lane == lane_of(day - half))), last)
    gaps = jnp.concatenate([taken[:days, :], taken[days:2 * days, :], mid, tops], axis=1).astype(bf16)
    step = min(256, rows)
    for at in range(0, rows, step):
        daily = (leaf_ref[:, at:at + step] + shift_ref[0:1, at:at + step]) + shift_ref[1:2, at:at + step]
        out_ref[:, at:at + step] = daily + dot(gaps, hits_ref[:, at:at + step])


def per_device(leaf, seas, fine, mid, top, base_fine, base_mid, base_top):
    days, rows = leaf.shape
    owners = lax.axis_size("series")
    blocks = lax.axis_size("tm")
    quarter = (lax.axis_index("tm") // (blocks // 4)).astype(i32).reshape(1)
    fine, mid, top = (ids.reshape(1, rows) for ids in (fine, mid, top))
    height = owners * 40 + TOP_ROWS

    sums = pl.pallas_call(
        day_sum_kernel,
        out_shape=jax.ShapeDtypeStruct((blocks, rows // 128, 128), f32),
        compiler_params=PARAMS,
        name="day_sums",
    )(leaf)
    parts = lax.all_to_all(sums, "tm", 0, 0, tiled=True)
    hits, base_rest = pl.pallas_call(
        lambda *refs: tables_kernel(owners, *refs),
        out_shape=(jax.ShapeDtypeStruct((height, rows), bf16), jax.ShapeDtypeStruct((16, 128), f32)),
        compiler_params=PARAMS,
        cost_estimate=pl.CostEstimate(flops=2 * owners * rows * 256, bytes_accessed=2 * height * rows, transcendentals=0),
        name="tables",
    )(fine, mid, top, base_mid.T, base_top.reshape(1, days))

    vmem = pl.BlockSpec(memory_space=pltpu.VMEM)
    payload, shift = pl.pallas_call(
        send_kernel,
        out_shape=(jax.ShapeDtypeStruct((owners, 16, 128), bf16), jax.ShapeDtypeStruct((2, rows), f32)),
        in_specs=[pl.BlockSpec(memory_space=pltpu.SMEM)] + [vmem] * 5,
        compiler_params=PARAMS,
        name="pack",
    )(quarter, leaf, seas, parts, fine, hits)
    got = lax.all_to_all(payload, "series", 0, 0, tiled=True)
    back = pl.pallas_call(
        owner_kernel,
        out_shape=jax.ShapeDtypeStruct((owners, 16, 128), bf16),
        compiler_params=PARAMS,
        name="gaps",
    )(got, base_fine, base_rest)
    back = lax.all_to_all(back, "series", 0, 0, tiled=True)
    return pl.pallas_call(
        finish_kernel,
        out_shape=jax.ShapeDtypeStruct((days, rows), f32),
        compiler_params=PARAMS,
        name="finish",
    )(leaf, shift, hits, back)


def solution(mesh):
    return jax.shard_map(
        per_device,
        mesh=mesh,
        in_specs=(
            P("tm", "series"),
            P(None, "series"),
            P("series", None),
            P("series", None),
            P("series", None),
            P("tm", "series"),
            P("tm", "series"),
            P("tm", "series"),
        ),
        out_specs=P("tm", "series"),
        check_vma=False,
    )
```

time: 72.3 us -> 82.3 us (1.14)
  blocking collectives: 18.4 us -> 45.8 us
  waiting for transfers between devices: 15.6 us -> 0.01 us
  starting transfers between devices: 21.5 us -> 9.14 us
  local copies, waits for them, and re-layouts: 3.34 us -> 15.3 us
    all_to_all x0 -> x1, blocking collectives: none -> 27.3 us  [per_device(): got = lax.all_to_all(payload, 'series', 0, 0, tiled=True)]
    all_to_all x2 -> x1, waiting for transfers between devices: 15.6 us -> 0.01 us  [per_device(): parts = lax.all_to_all(sums, 'tm', 0, 0, tiled=True)]
    all_to_all x2 -> x1, starting transfers between devices: 21.5 us -> 9.14 us  [per_device(): parts = lax.all_to_all(sums, 'tm', 0, 0, tiled=True)]
    unnamed x20 -> x28, local copies, waits for them, and re-layouts: 2.96 us -> 15.3 us
    pallas_call x2, Pallas kernels: 1.01 us -> 3.36 us  [the longest x1 2.7 us: per_device(): pl.pallas_call(lambda *refs: tables_kernel(owners, *refs), out_shape=(jax...]
    pallas_call x1, Pallas kernels: 6.29 us -> 4.03 us  [per_device(): pl.pallas_call(send_kernel, out_shape=(jax.ShapeDtypeStruct((owners, 16,...]
  transfers between devices with their start and end apart: 2 -> 1, of which waited for: 2 -> 0; matrix products, arithmetic and copies ran while one was open for 2% -> 0% of each run, Pallas kernels for 0% -> 3%
where the time goes in v5:
time: 82.3 us; the launch traced here: 81.6 us
  blocking collectives  45.8 us (56%)
  local copies, waits for them, and re-layouts  15.3 us (19%)
  Pallas kernels  11.4 us (14%)
  starting transfers between devices  9.14 us (11%)
    all_to_all x1, blocking collectives, per_device(): got = lax.all_to_all(payload, 'series', 0, 0, tiled=True)  27.3 us
    all_to_all x1, blocking collectives, per_device(): back = lax.all_to_all(back, 'series', 0, 0, tiled=True)  18.5 us
    unnamed x28, local copies, waits for them, and re-layouts  15.3 us
    all_to_all x1, starting transfers between devices, per_device(): parts = lax.all_to_all(sums, 'tm', 0, 0, tiled=True)  9.14 us
    pallas_call x1, Pallas kernels, per_device(): pl.pallas_call(send_kernel, out_shape=(jax.ShapeDtypeStruct((owners, 16,...  4.03 us
    pallas_call x1, Pallas kernels, per_device(): pl.pallas_call(finish_kernel, out_shape=jax.ShapeDtypeStruct((days, rows)...  3.16 us
    pallas_call x1, Pallas kernels, per_device(): pl.pallas_call(lambda *refs: tables_kernel(owners, *refs), out_shape=(jax...  2.7 us
  transfers between devices with their start and end apart: 1, of which 0 were waited for; matrix products, arithmetic and copies ran while one was open for 0% of the time, Pallas kernels for 3%

profile of v5, /device:TPU:6, one launch (start us, length us, event | category | flops | bytes accessed | tf_op | source)
XLA Modules:
  0.0 81.6 jit_solution(10761015947384022461)
XLA Ops:
  0.0 0.0 copy-start.3
  0.0 1.0 %copy-done.3 = f32[48,2048]{1,0:T(8,128)S(1)} copy-done((f32[48,2048]{1,0:T(8,128)S(1)}, f32[48,2048]{1,0:T(8,128)}, u32[]{:S(2)}) %copy-start.3) | copy-done | bytes 393240
  1.0 0.0 copy-start.7
  1.0 0.0 copy-start.5
  1.0 0.7 day_sums.1
  1.7 9.1 %all-to-all-start = ((f32[8,16,128]{2,1,0:T(8,128)}), f32[8,16,128]{2,1,0:T(8,128)S(1)}, u32[]{:S(2)}, u32[]{:S(2)}) async-start(f32[8,16,128]{2,1,0:T(8,128)} %day_sums.1), calls=%async_computation | async-start | bytes 131072 | tf_op jit(solution)/shard_map/all_to_all | solution.py:221
  10.8 0.0 copy-start.8
  10.8 0.7 copy-done.8
  11.5 0.0 copy-start.10
  11.5 0.7 copy-done.10
  12.2 0.0 copy-start.11
  12.2 0.7 copy-done.11
  12.9 0.0 copy-start.12
  12.9 0.7 copy-done.12
  13.6 0.0 copy-start.13
  13.6 0.7 copy-done.13
  14.2 2.7 %tables.1 = (bf16[2688,2048]{1,0:T(8,128)(2,1)S(1)}, f32[16,128]{1,0:T(8,128)S(1)}) custom-call(s32[1,2048]{1,0:T(1,128)S(1)} %bitcast.6, s32[1,2048]{1,0:T(1,128)S(1)} %bitcast.8, s32[1,2048]{1,0:T(1,128)S(1)} %bitcast.9, f32[8,48]{1,0:T(8,128)S(1)} %bitcast.10, f32[1,48]{1,0:T(1,128)S(1)} %bitcast.11), custom_call_target="tpu_custom_call" | custom-call | flops 67108864 | bytes 11010048 | tf_op jit(solution)/shard_map/tables/pallas_call | solution.py:222
  16.9 0.0 copy-start
  17.0 4.2 %copy-done = bf16[2688,2048]{1,0:T(8,128)(2,1)} copy-done((bf16[2688,2048]{1,0:T(8,128)(2,1)}, bf16[2688,2048]{1,0:T(8,128)(2,1)S(1)}, u32[]{:S(2)}) %copy-start) | copy-done | bytes 11010072
  21.1 0.0 all-to-all-done.parts_ref
  21.1 0.0 copy-start.1
  21.1 4.1 %copy-done.1 = bf16[2688,2048]{1,0:T(8,128)(2,1)S(1)} copy-done((bf16[2688,2048]{1,0:T(8,128)(2,1)S(1)}, bf16[2688,2048]{1,0:T(8,128)(2,1)}, u32[]{:S(2)}) %copy-start.1) | copy-done | bytes 11010072
  25.3 0.0 copy-start.4
  25.3 1.0 %copy-done.4 = f32[48,2048]{1,0:T(8,128)S(1)} copy-done((f32[48,2048]{1,0:T(8,128)S(1)}, f32[48,2048]{1,0:T(8,128)}, u32[]{:S(2)}) %copy-start.4) | copy-done | bytes 393240
  26.3 0.0 copy-start.6
  26.3 0.8 %copy-done.6 = f32[5,2048]{1,0:T(8,128)S(1)} copy-done((f32[5,2048]{1,0:T(8,128)S(1)}, f32[5,2048]{1,0:T(8,128)}, u32[]{:S(2)}) %copy-start.6) | copy-done | bytes 40984
  27.1 0.0 copy-start.9
  27.1 0.7 copy-done.9
  27.8 0.0 copy-start.2
  27.8 4.0 %pack.1 = (bf16[64,16,128]{2,1,0:T(8,128)(2,1)S(1)}, f32[2,2048]{1,0:T(2,128)S(1)}) custom-call(s32[1]{0:T(128)} %bitcast.quarter_ref, f32[48,2048]{1,0:T(8,128)S(1)} %copy-done.4, f32[5,2048]{1,0:T(8,128)S(1)} %copy-done.6, f32[8,16,128]{2,1,0:T(8,128)S(1)} %all-to-all-done.parts_ref, s32[1,2048]{1,0:T(1,128)S(1)} %bitcast.7, bf16[2688,2048]{1,0:T(8,128)(2,1)S(1)} %copy-done.1), custom_call_target="tpu_custom_call" | custom-call | tf_op jit(solution)/shard_map/pack/pallas_call | solution.py:231
  31.8 27.3 %all_to_all.15.got_ref = bf16[64,16,128]{2,1,0:T(8,128)(2,1)S(1)} all-to-all(bf16[64,16,128]{2,1,0:T(8,128)(2,1)S(1)} %get-tuple-element.11), channel_id=1, replica_groups=mesh['tm'=8,'series'=64] {'series'}, dimensions={0} | all-to-all | bytes 524288 | tf_op jit(solution)/shard_map/all_to_all | solution.py:238
  59.1 0.0 copy-done.7
  59.1 0.8 %gaps.1 = bf16[64,16,128]{2,1,0:T(8,128)(2,1)S(1)} custom-call(bf16[64,16,128]{2,1,0:T(8,128)(2,1)S(1)} %all_to_all.15.got_ref, f32[48,64]{1,0:T(8,128)S(1)} %copy-done.7, f32[16,128]{1,0:T(8,128)S(1)} %get-tuple-element.12.base_rest_ref), custom_call_target="tpu_custom_call" | custom-call | tf_op jit(solution)/shard_map/gaps/pallas_call | solution.py:239
  60.0 18.5 %all_to_all.16.back_ref = bf16[64,16,128]{2,1,0:T(8,128)(2,1)S(1)} all-to-all(bf16[64,16,128]{2,1,0:T(8,128)(2,1)S(1)} %gaps.1), channel_id=1, replica_groups=mesh['tm'=8,'series'=64] {'series'}, dimensions={0} | all-to-all | bytes 524288 | tf_op jit(solution)/shard_map/all_to_all | solution.py:245
  78.5 0.0 copy-done.5
  78.5 0.0 copy-done.2
  78.5 3.2 %finish.1 = f32[48,2048]{1,0:T(8,128)} custom-call(f32[48,2048]{1,0:T(8,128)S(1)} %copy-done.5, f32[2,2048]{1,0:T(2,128)S(1)} %get-tuple-element.10.shift_ref, bf16[2688,2048]{1,0:T(8,128)(2,1)S(1)} %copy-done.2, bf16[64,16,128]{2,1,0:T(8,128)(2,1)S(1)} %all_to_all.16.back_ref), custom_call_target="tpu_custom_call" | custom-call | tf_op jit(solution)/shard_map/finish/pallas_call | solution.py:246
Async XLA Ops:
  0.0 1.0 %copy-start.3 = (f32[48,2048]{1,0:T(8,128)S(1)}, f32[48,2048]{1,0:T(8,128)}, u32[]{:S(2)}) copy-start(f32[48,2048]{1,0:T(8,128)} %leaf_ref.5) | copy-start | bytes 1179652
  1.0 58.1 %copy-start.7 = (f32[48,64]{1,0:T(8,128)S(1)}, f32[48,64]{1,0:T(8,128)}, u32[]{:S(2)}) copy-start(f32[48,64]{1,0:T(8,128)} %base_fine_ref.1) | copy-start | bytes 36868
  1.0 77.5 %copy-start.5 = (f32[48,2048]{1,0:T(8,128)S(1)}, f32[48,2048]{1,0:T(8,128)}, u32[]{:S(2)}) copy-start(f32[48,2048]{1,0:T(8,128)} %leaf_ref.5) | copy-start | bytes 1179652
  1.7 19.5 %all-to-all-start = ((f32[8,16,128]{2,1,0:T(8,128)}), f32[8,16,128]{2,1,0:T(8,128)S(1)}, u32[]{:S(2)}, u32[]{:S(2)}) async-start(f32[8,16,128]{2,1,0:T(8,128)} %day_sums.1), calls=%async_computation | async-start | bytes 131072 | tf_op jit(solution)/shard_map/all_to_all | solution.py:221
  10.8 0.7 copy-start.8
  11.5 0.7 copy-start.10
  12.2 0.7 copy-start.11
  12.9 0.7 copy-start.12
  13.6 0.7 copy-start.13
  16.9 4.2 %copy-start = (bf16[2688,2048]{1,0:T(8,128)(2,1)}, bf16[2688,2048]{1,0:T(8,128)(2,1)S(1)}, u32[]{:S(2)}) copy-start(bf16[2688,2048]{1,0:T(8,128)(2,1)S(1)} %get-tuple-element.9.hits_ref) | copy-start | bytes 33030148
  21.1 4.1 %copy-start.1 = (bf16[2688,2048]{1,0:T(8,128)(2,1)S(1)}, bf16[2688,2048]{1,0:T(8,128)(2,1)}, u32[]{:S(2)}) copy-start(bf16[2688,2048]{1,0:T(8,128)(2,1)} %copy-done) | copy-start | bytes 33030148
  25.3 1.0 %copy-start.4 = (f32[48,2048]{1,0:T(8,128)S(1)}, f32[48,2048]{1,0:T(8,128)}, u32[]{:S(2)}) copy-start(f32[48,2048]{1,0:T(8,128)} %leaf_ref.5) | copy-start | bytes 1179652
  26.3 0.8 %copy-start.6 = (f32[5,2048]{1,0:T(8,128)S(1)}, f32[5,2048]{1,0:T(8,128)}, u32[]{:S(2)}) copy-start(f32[5,2048]{1,0:T(8,128)} %seas_ref.1) | copy-start | bytes 122884
  27.1 0.7 copy-start.9
  27.8 50.7 %copy-start.2 = (bf16[2688,2048]{1,0:T(8,128)(2,1)S(1)}, bf16[2688,2048]{1,0:T(8,128)(2,1)}, u32[]{:S(2)}) copy-start(bf16[2688,2048]{1,0:T(8,128)(2,1)} %copy-done) | copy-start | bytes 33030148

commit v6 on v5

--- a/solution.py
+++ b/solution.py
@@ -9,7 +9,7 @@
 bf16 = jnp.bfloat16
 i32 = jnp.int32
 
-PARAMS = pltpu.CompilerParams(vmem_limit_bytes=28 * 1024 * 1024)
+PARAMS = pltpu.CompilerParams(vmem_limit_bytes=24 * 1024 * 1024)
 
 ID = 48
 ONE = 49
@@ -51,28 +51,25 @@
     return jnp.concatenate([dense[at:at + 1, :] for at in range(dense.shape[0])], axis=1)
 
 
-def corrections(seas, parts, quarter, days):
-    per = parts.shape[0] // 4
-    season_days = days * per
-    own = row_of(jnp.sum(jnp.where(iota(parts.shape, 0) // per == quarter, parts, 0.0), axis=0))
-    rows = iota(seas.shape, 0)
-    seas_own = jnp.sum(jnp.where(rows == quarter, seas, 0.0), axis=0, keepdims=True)
-    seas_four = jnp.sum(jnp.where(rows < 4, seas, 0.0), axis=0, keepdims=True)
-    year = 0.5 * row_of(jnp.sum(parts, axis=0)) + 0.5 * seas_four
-    first = 0.5 * (seas_own - own) / season_days
-    second = 0.5 * (seas[4:5, :] - year) / (season_days * 4)
-    return first, second
-
-
-def day_sum_kernel(leaf_ref, out_ref):
-    sums = jnp.sum(leaf_ref[...], axis=0, keepdims=True)
-    dense = jnp.concatenate([sums[:, at:at + 128] for at in range(0, sums.shape[1], 128)], axis=0)
-    out_ref[...] = jnp.broadcast_to(dense[None], out_ref.shape)
-
-
-def tables_kernel(owners, fine_ref, mid_ref, top_ref, base_mid_ref, base_top_ref, hits_ref, base_ref):
-    rows = fine_ref.shape[1]
-    owner = fine_ref[...] >> 6
+def dense_of(row):
+    return jnp.concatenate([row[:, at:at + 128] for at in range(0, row.shape[1], 128)], axis=0)
+
+
+def start_kernel(*refs):
+    count = (len(refs) - 2) // 2
+    sources, places, sums_ref, sems = refs[:count], refs[count:2 * count], refs[-2], refs[-1]
+    copies = [pltpu.make_async_copy(src, dst, sems.at[k]) for k, (src, dst) in enumerate(zip(sources, places))]
+    for copy in copies:
+        copy.start()
+    copies[0].wait()
+    sums = dense_of(jnp.sum(places[0][...], axis=0, keepdims=True))
+    sums_ref[...] = jnp.broadcast_to(sums[None], sums_ref.shape)
+    for copy in copies[1:]:
+        copy.wait()
+
+
+def ranks_of(owner, owners):
+    rows = owner.shape[1]
     step = min(256, rows)
     before = ones_where(iota((step, step), 0) < iota((step, step), 1))
     base = jnp.zeros((owners, 1), f32)
@@ -83,18 +80,51 @@
         seen = dot(hit_f.astype(bf16), before) + base
         ranks.append(jnp.sum(jnp.where(hit, seen, 0.0), axis=0, keepdims=True))
         base = base + jnp.sum(hit_f, axis=1, keepdims=True)
-    rank = jnp.concatenate(ranks, axis=1).astype(i32)
+    return jnp.concatenate(ranks, axis=1).astype(i32)
+
+
+def sort_kernel(
+    owners, quarter_ref, leaf_ref, seas_ref, fine_ref, mid_ref, top_ref, base_mid_ref, base_top_ref,
+    slots_ref, nodes_ref, places_ref, from_ref, known_ref, base_ref,
+):
+    days, rows = leaf_ref.shape
+    owner = fine_ref[...] >> 6
+    rank = ranks_of(owner, owners)
     place = owner * 16 + (rank & 15)
     place_low = jnp.where(rank < 16, place, -1)
     place_high = jnp.where(rank < 16, -1, place)
+    places_ref[0:1, :] = place_low
+    places_ref[1:2, :] = place_high
+
+    leaf = leaf_ref[...]
+    high = leaf.astype(bf16).astype(f32)
+    series = iota((1, rows), 1)
+    ones = jnp.ones((1, rows), f32)
+    known = [(fine_ref[...] & 63).astype(f32), ones, ones, (series >> 7).astype(f32), (series & 127).astype(f32)]
+    ext = jnp.concatenate([high] + known + [jnp.zeros((3, rows), f32), leaf - high], axis=0).astype(bf16)
     at = 0
-    for place, height in ((place_low, owners * 16), (place_high, owners * 16), (mid_ref[...], owners * 8), (top_ref[...], TOP_ROWS)):
-        chunk = min(64, height)
+    for ids, out_ref, height in (
+        (place_low, slots_ref, owners * 16), (place_high, slots_ref, owners * 16),
+        (mid_ref[...], nodes_ref, owners * 8), (top_ref[...], nodes_ref, TOP_ROWS),
+    ):
+        chunk = min(256, height)
         for start in range(0, height, chunk):
-            hits_ref[at:at + chunk, :] = ones_where(iota((chunk, rows), 0) + start == place)
+            sums = dot_nt(ext, ones_where(iota((chunk, rows), 0) + start == ids))
+            tail = jnp.concatenate([sums[days + 8:, :], jnp.zeros((8, chunk), f32)], axis=0)
+            out_ref[:, at:at + chunk] = sums[:days + 8, :] + tail
             at += chunk
-
-    days = base_mid_ref.shape[1]
+        if ids is place_high:
+            at = 0
+    from_ref[0, :, :] = dense_of(slots_ref[LOW + 1:LOW + 2, :]).astype(i32)
+    from_ref[1, :, :] = dense_of(slots_ref[LOW + 2:LOW + 3, :]).astype(i32)
+
+    seas = seas_ref[...]
+    season_days = days * 2
+    line = iota(seas.shape, 0)
+    own = jnp.sum(jnp.where(line == quarter_ref[0], seas, 0.0), axis=0, keepdims=True)
+    four = jnp.sum(jnp.where(line < 4, seas, 0.0), axis=0, keepdims=True)
+    known_ref[...] = dense_of(0.5 * own / season_days + 0.5 * (seas[4:5, :] - 0.5 * four) / (season_days * 4))
+
     half = days // 2
     day, lane = iota((days, 128), 0), iota((days, 128), 1)
     moves = (
@@ -114,17 +144,42 @@
     return jnp.where(iota(sums.shape, 0) == LOW, sums - high, high)
 
 
-def send_kernel(quarter_ref, leaf_ref, seas_ref, parts_ref, fine_ref, hits_ref, pay_ref, shift_ref):
-    days, rows = leaf_ref.shape
+def send_kernel(quarter_ref, parts_ref, known_ref, from_ref, slots_ref, nodes_ref, mid_ref, top_ref, pay_ref, shift_ref):
     owners = pay_ref.shape[0]
+    rows = mid_ref.shape[1]
     slots, mids = owners * 16, owners * 8
-    first, second = corrections(seas_ref[...], parts_ref[...], quarter_ref[0], days)
-    shift_ref[0:1, :] = first
-    shift_ref[1:2, :] = second
-    daily = (leaf_ref[...] + first) + second
-    local = fine_ref[...] & 63
-    ext = jnp.concatenate([daily, local.astype(f32), jnp.ones((2, rows), f32), jnp.zeros((13, rows), f32)], axis=0)
-    sums = dot_nt(ext.astype(bf16), hits_ref[...])
+    days = slots_ref.shape[0] - 8
+    season_days = days * 2
+    parts = parts_ref[...]
+    own = jnp.sum(jnp.where(iota(parts.shape, 0) >> 1 == quarter_ref[0], parts, 0.0), axis=0)
+    total = jnp.sum(parts, axis=0)
+    shift = known_ref[...] - (0.5 * own / season_days + 0.25 * total / (season_days * 4))
+    shift_row = row_of(shift)
+    shift_ref[...] = shift_row
+
+    line, lane = from_ref[0, :, :], from_ref[1, :, :]
+    moved = jnp.zeros(shift.shape, f32)
+    for at in range(shift.shape[0]):
+        taken = jnp.take_along_axis(
+            jnp.broadcast_to(shift[at:at + 1, :], shift.shape), lane, axis=1, mode="promise_in_bounds"
+        )
+        moved = jnp.where(line == at, taken, moved)
+    moved = row_of(moved)
+
+    high = shift_row.astype(bf16).astype(f32)
+    ext = jnp.concatenate([high, shift_row - high, jnp.zeros((6, rows), f32)], axis=0).astype(bf16)
+    node_sums = []
+    for ids, height in ((mid_ref[...], mids), (top_ref[...], TOP_ROWS)):
+        chunk = min(256, height)
+        for start in range(0, height, chunk):
+            hits = ones_where(iota((chunk, rows), 0) + start == ids)
+            node_sums.append(jnp.sum(dot_nt(ext, hits), axis=0, keepdims=True))
+    node_sums = jnp.concatenate(node_sums, axis=1)
+    is_day = iota((days + 8, 1), 0) < days
+    pad = jnp.zeros((8, rows + mids + TOP_ROWS), f32)
+    sums = jnp.concatenate([slots_ref[...], nodes_ref[...]], axis=1)
+    sums = sums + jnp.where(is_day, jnp.concatenate([moved, node_sums], axis=1), 0.0)
+    sums = jnp.concatenate([sums, pad], axis=0)
 
     tops = split_count(sums[:, 2 * slots + mids:]).astype(bf16)
     tops = dot(tops, ones_where(iota((TOP_ROWS, slots), 0) == iota((TOP_ROWS, slots), 1) >> 4))
@@ -183,7 +238,7 @@
     back_ref[...] = (spread + gap_rest[None]).astype(bf16)
 
 
-def finish_kernel(leaf_ref, shift_ref, hits_ref, back_ref, out_ref):
+def finish_kernel(leaf_ref, shift_ref, places_ref, mid_ref, top_ref, back_ref, out_ref):
     days, rows = leaf_ref.shape
     owners = back_ref.shape[0]
     slots, mids = owners * 16, owners * 8
@@ -197,11 +252,16 @@
     first, last = (back[:, at:at + 8, :].reshape(mids, 128).astype(bf16) for at in (0, 8))
     mid = dot_nt(ones_where((day < half) & (lane == lane_of(day))), first)
     mid = mid + dot_nt(ones_where((day >= half) & (lane == lane_of(day - half))), last)
-    gaps = jnp.concatenate([taken[:days, :], taken[days:2 * days, :], mid, tops], axis=1).astype(bf16)
+    gaps = [part.astype(bf16) for part in (taken[:days, :], taken[days:2 * days, :], mid, tops)]
     step = min(256, rows)
     for at in range(0, rows, step):
-        daily = (leaf_ref[:, at:at + step] + shift_ref[0:1, at:at + step]) + shift_ref[1:2, at:at + step]
-        out_ref[:, at:at + step] = daily + dot(gaps, hits_ref[:, at:at + step])
+        ids = (
+            places_ref[0:1, at:at + step], places_ref[1:2, at:at + step], mid_ref[:, at:at + step], top_ref[:, at:at + step]
+        )
+        out = leaf_ref[:, at:at + step] + shift_ref[:, at:at + step]
+        for gap, place in zip(gaps, ids):
+            out = out + dot(gap, ones_where(iota((gap.shape[1], step), 0) == place))
+        out_ref[:, at:at + step] = out
 
 
 def per_device(leaf, seas, fine, mid, top, base_fine, base_mid, base_top):
@@ -209,32 +269,46 @@
     owners = lax.axis_size("series")
     blocks = lax.axis_size("tm")
     quarter = (lax.axis_index("tm") // (blocks // 4)).astype(i32).reshape(1)
-    fine, mid, top = (ids.reshape(1, rows) for ids in (fine, mid, top))
-    height = owners * 40 + TOP_ROWS
-
-    sums = pl.pallas_call(
-        day_sum_kernel,
-        out_shape=jax.ShapeDtypeStruct((blocks, rows // 128, 128), f32),
-        compiler_params=PARAMS,
-        name="day_sums",
-    )(leaf)
+    any_space = pl.BlockSpec(memory_space=pl.ANY)
+    vmem = pl.BlockSpec(memory_space=pltpu.VMEM)
+    smem = pl.BlockSpec(memory_space=pltpu.SMEM)
+
+    arrays = (leaf, seas, *(ids.reshape(1, rows) for ids in (fine, mid, top)), base_mid.T, base_top.reshape(1, days))
+    *arrays, sums = pl.pallas_call(
+        start_kernel,
+        out_shape=[jax.ShapeDtypeStruct(x.shape, x.dtype) for x in arrays]
+        + [jax.ShapeDtypeStruct((blocks, rows // 128, 128), f32)],
+        in_specs=[any_space] * len(arrays),
+        scratch_shapes=[pltpu.SemaphoreType.DMA((len(arrays),))],
+        compiler_params=PARAMS,
+        name="start",
+    )(*arrays)
     parts = lax.all_to_all(sums, "tm", 0, 0, tiled=True)
-    hits, base_rest = pl.pallas_call(
-        lambda *refs: tables_kernel(owners, *refs),
-        out_shape=(jax.ShapeDtypeStruct((height, rows), bf16), jax.ShapeDtypeStruct((16, 128), f32)),
-        compiler_params=PARAMS,
-        cost_estimate=pl.CostEstimate(flops=2 * owners * rows * 256, bytes_accessed=2 * height * rows, transcendentals=0),
-        name="tables",
-    )(fine, mid, top, base_mid.T, base_top.reshape(1, days))
-
-    vmem = pl.BlockSpec(memory_space=pltpu.VMEM)
+    leaf, seas, fine, mid, top, base_mid, base_top = arrays
+    dense = (rows // 128, 128)
+    slots, nodes, places, come_from, known, base_rest = pl.pallas_call(
+        lambda *refs: sort_kernel(owners, *refs),
+        out_shape=(
+            jax.ShapeDtypeStruct((days + 8, rows), f32),
+            jax.ShapeDtypeStruct((days + 8, owners * 8 + TOP_ROWS), f32),
+            jax.ShapeDtypeStruct((2, rows), i32),
+            jax.ShapeDtypeStruct((2,) + dense, i32),
+            jax.ShapeDtypeStruct(dense, f32),
+            jax.ShapeDtypeStruct((16, 128), f32),
+        ),
+        in_specs=[smem] + [vmem] * 7,
+        compiler_params=PARAMS,
+        cost_estimate=pl.CostEstimate(flops=2 * 104 * owners * 42 * rows, bytes_accessed=4 * days * rows, transcendentals=0),
+        name="sort",
+    )(quarter, *arrays)
+
     payload, shift = pl.pallas_call(
         send_kernel,
-        out_shape=(jax.ShapeDtypeStruct((owners, 16, 128), bf16), jax.ShapeDtypeStruct((2, rows), f32)),
-        in_specs=[pl.BlockSpec(memory_space=pltpu.SMEM)] + [vmem] * 5,
+        out_shape=(jax.ShapeDtypeStruct((owners, 16, 128), bf16), jax.ShapeDtypeStruct((1, rows), f32)),
+        in_specs=[smem] + [vmem] * 7,
         compiler_params=PARAMS,
         name="pack",
-    )(quarter, leaf, seas, parts, fine, hits)
+    )(quarter, parts, known, come_from, slots, nodes, mid, top)
     got = lax.all_to_all(payload, "series", 0, 0, tiled=True)
     back = pl.pallas_call(
         owner_kernel,
@@ -248,7 +322,7 @@
         out_shape=jax.ShapeDtypeStruct((days, rows), f32),
         compiler_params=PARAMS,
         name="finish",
-    )(leaf, shift, hits, back)
+    )(leaf, shift, places, mid, top, back)
 
 
 def solution(mesh):

time: 82.3 us -> 70.6 us (0.86)
  local copies, waits for them, and re-layouts: 15.3 us -> 4.62 us
  Pallas kernels: 11.4 us -> 10.5 us
    unnamed x28 -> x16, local copies, waits for them, and re-layouts: 15.3 us -> 4.62 us
    pallas_call x1, Pallas kernels: 4.03 us -> 1.43 us  [per_device(): pl.pallas_call(send_kernel, out_shape=(jax.ShapeDtypeStruct((owners, 16,...]
    pallas_call x2, Pallas kernels: 3.36 us -> 4.97 us  [the longest x1 3.94 us: per_device(): pl.pallas_call(lambda *refs: sort_kernel(owners, *refs), out_shape=(jax.S...]
  transfers between devices with their start and end apart: 1 -> 1, of which waited for: 0 -> 0; matrix products, arithmetic and copies ran while one was open for 0% -> 0% of each run, Pallas kernels for 3% -> 6%
where the time goes in v6:
time: 70.6 us; the launch traced here: 70.1 us
  blocking collectives  45.8 us (65%)
  Pallas kernels  10.5 us (15%)
  starting transfers between devices  9.15 us (13%)
  local copies, waits for them, and re-layouts  4.62 us (7%)
    all_to_all x1, blocking collectives, per_device(): got = lax.all_to_all(payload, 'series', 0, 0, tiled=True)  27.3 us
    all_to_all x1, blocking collectives, per_device(): back = lax.all_to_all(back, 'series', 0, 0, tiled=True)  18.5 us
    all_to_all x1, starting transfers between devices, per_device(): parts = lax.all_to_all(sums, 'tm', 0, 0, tiled=True)  9.15 us
    unnamed x16, local copies, waits for them, and re-layouts  4.62 us
    pallas_call x1, Pallas kernels, per_device(): pl.pallas_call(lambda *refs: sort_kernel(owners, *refs), out_shape=(jax.S...  3.94 us
    pallas_call x1, Pallas kernels, per_device(): pl.pallas_call(finish_kernel, out_shape=jax.ShapeDtypeStruct((days, rows)...  3.24 us
    pallas_call x1, Pallas kernels, per_device(): pl.pallas_call(send_kernel, out_shape=(jax.ShapeDtypeStruct((owners, 16,...  1.43 us
  transfers between devices with their start and end apart: 1, of which 0 were waited for; matrix products, arithmetic and copies ran while one was open for 0% of the time, Pallas kernels for 6%

profile of v6, /device:TPU:6, one launch (start us, length us, event | category | flops | bytes accessed | tf_op | source)
XLA Modules:
  0.0 70.1 jit_solution(8643503423674444384)
XLA Ops:
  0.0 0.0 copy-start.3
  0.0 0.0 copy-start.7
  0.0 0.7 copy-done.3
  0.7 0.0 copy-done.7
  0.7 0.0 copy-start
  0.7 1.0 %copy-done = f32[48,2048]{1,0:T(8,128)S(1)} copy-done((f32[48,2048]{1,0:T(8,128)S(1)}, f32[48,2048]{1,0:T(8,128)}, u32[]{:S(2)}) %copy-start) | copy-done | bytes 393240
  1.7 0.0 copy-start.1
  1.7 0.8 %copy-done.1 = f32[5,2048]{1,0:T(8,128)S(1)} copy-done((f32[5,2048]{1,0:T(8,128)S(1)}, f32[5,2048]{1,0:T(8,128)}, u32[]{:S(2)}) %copy-start.1) | copy-done | bytes 40984
  2.5 0.0 copy-start.4
  2.5 0.7 copy-done.4
  3.2 0.0 copy-start.5
  3.2 0.7 copy-done.5
  3.9 0.0 copy-start.6
  3.9 0.7 copy-done.6
  4.6 1.0 %start.1 = (f32[48,2048]{1,0:T(8,128)S(1)}, f32[5,2048]{1,0:T(8,128)S(1)}, s32[1,2048]{1,0:T(1,128)S(1)}, s32[1,2048]{1,0:T(1,128)S(1)}, s32[1,2048]{1,0:T(1,128...) custom-call(f32[48,2048]{1,0:T(8,128)S(1)} %copy-done, f32[5,2048]{1,0:T(8,128)S(1)} %copy-done.1, ...), custom_call_target="tpu_custom_call" | custom-call | tf_op jit(solution)/shard_map/start/pallas_call | solution.py:277
  5.7 9.2 %all-to-all-start = ((f32[8,16,128]{2,1,0:T(8,128)}), f32[8,16,128]{2,1,0:T(8,128)S(1)}, u32[]{:S(2)}, u32[]{:S(2)}) async-start(f32[8,16,128]{2,1,0:T(8,128)} %get-tuple-element.22), calls=%async_computation | async-start | bytes 131072 | tf_op jit(solution)/shard_map/all_to_all | solution.py:286
  14.8 3.9 %sort.1 = (f32[56,2048]{1,0:T(8,128)S(1)}, f32[56,640]{1,0:T(8,128)S(1)}, s32[2,2048]{1,0:T(2,128)S(1)}, s32[2,16,128]{2,1,0:T(8,128)S(1)}, f32[16,128]{1,0:T(8,128)S(1)}, /*index=5*/f32[16,128]{1,0:T(8,128)S(1)}) custom-call(s32[1]{0:T(128)} %bitcast.5.refs_0_.quarter_ref, f32[48,2048]{1,0:T(8,128)S(1)} %get-tuple-element.21.refs_1_.leaf_ref, ...), custom_call_target="tpu_custom_call" | custom-call | flops 1145044992 | bytes 393216 | tf_op jit(solution)/shard_map/sort/pallas_call | solution.py:289
  18.8 0.0 all-to-all-done.parts_ref
  18.8 1.4 %pack.1 = (bf16[64,16,128]{2,1,0:T(8,128)(2,1)S(1)}, f32[1,2048]{1,0:T(1,128)S(1)}) custom-call(s32[1]{0:T(128)} %bitcast.5.refs_0_.quarter_ref, f32[8,16,128]{2,1,0:T(8,128)S(1)} %all-to-all-done.parts_ref, f32[16,128]{1,0:T(8,128)S(1)} %get-tuple-element.29.known_ref, s32[2,16,128]{2,1,0:T(8,128)S(1)} %get-tuple-element.30.from_ref, ...), custom_call_target="tpu_custom_call" | custom-call | tf_op jit(solution)/shard_map/pack/pallas_call | solution.py:305
  20.2 0.0 copy-start.2
  20.2 27.3 %all_to_all.15.got_ref = bf16[64,16,128]{2,1,0:T(8,128)(2,1)S(1)} all-to-all(bf16[64,16,128]{2,1,0:T(8,128)(2,1)S(1)} %get-tuple-element.35), channel_id=1, replica_groups=mesh['tm'=8,'series'=64] {'series'}, dimensions={0} | all-to-all | bytes 524288 | tf_op jit(solution)/shard_map/all_to_all | solution.py:312
  47.5 0.0 copy-done.2
  47.5 0.8 %gaps.1 = bf16[64,16,128]{2,1,0:T(8,128)(2,1)S(1)} custom-call(bf16[64,16,128]{2,1,0:T(8,128)(2,1)S(1)} %all_to_all.15.got_ref, f32[48,64]{1,0:T(8,128)S(1)} %copy-done.2, f32[16,128]{1,0:T(8,128)S(1)} %get-tuple-element.36.base_rest_ref), custom_call_target="tpu_custom_call" | custom-call | tf_op jit(solution)/shard_map/gaps/pallas_call | solution.py:313
  48.4 18.5 %all_to_all.16.back_ref = bf16[64,16,128]{2,1,0:T(8,128)(2,1)S(1)} all-to-all(bf16[64,16,128]{2,1,0:T(8,128)(2,1)S(1)} %gaps.1), channel_id=1, replica_groups=mesh['tm'=8,'series'=64] {'series'}, dimensions={0} | all-to-all | bytes 524288 | tf_op jit(solution)/shard_map/all_to_all | solution.py:319
  66.9 3.2 %finish.1 = f32[48,2048]{1,0:T(8,128)} custom-call(f32[48,2048]{1,0:T(8,128)S(1)} %get-tuple-element.21.refs_1_.leaf_ref, f32[1,2048]{1,0:T(1,128)S(1)} %get-tuple-element.33.shift_ref, s32[2,2048]{1,0:T(2,128)S(1)} %get-tuple-element.34.places_ref, s32[1,2048]{1,0:T(1,128)S(1)} %get-tuple-element.25.refs_4_.mid_ref, ...), custom_call_target="tpu_custom_call" | custom-call | tf_op jit(solution)/shard_map/finish/pallas_call | solution.py:320
Async XLA Ops:
  0.0 0.7 copy-start.3
  0.0 0.7 copy-start.7
  0.7 1.0 %copy-start = (f32[48,2048]{1,0:T(8,128)S(1)}, f32[48,2048]{1,0:T(8,128)}, u32[]{:S(2)}) copy-start(f32[48,2048]{1,0:T(8,128)} %refs_0_.1) | copy-start | bytes 1179652
  1.7 0.8 %copy-start.1 = (f32[5,2048]{1,0:T(8,128)S(1)}, f32[5,2048]{1,0:T(8,128)}, u32[]{:S(2)}) copy-start(f32[5,2048]{1,0:T(8,128)} %refs_1_.1) | copy-start | bytes 122884
  2.5 0.7 copy-start.4
  3.2 0.7 copy-start.5
  3.9 0.7 copy-start.6
  5.7 13.1 %all-to-all-start = ((f32[8,16,128]{2,1,0:T(8,128)}), f32[8,16,128]{2,1,0:T(8,128)S(1)}, u32[]{:S(2)}, u32[]{:S(2)}) async-start(f32[8,16,128]{2,1,0:T(8,128)} %get-tuple-element.22), calls=%async_computation | async-start | bytes 131072 | tf_op jit(solution)/shard_map/all_to_all | solution.py:286
  20.2 27.3 %copy-start.2 = (f32[48,64]{1,0:T(8,128)S(1)}, f32[48,64]{1,0:T(8,128)}, u32[]{:S(2)}) copy-start(f32[48,64]{1,0:T(8,128)} %base_fine_ref.1) | copy-start | bytes 36868

commit v7 on v6

--- a/solution.py
+++ b/solution.py
@@ -35,6 +35,13 @@
     return jnp.where(mask, 1.0, 0.0).astype(bf16)
 
 
+def hits(ids, start, height):
+    low = jnp.where((ids >> 8) == (start >> 8), ids & 255, -1).astype(f32).astype(bf16)
+    row = iota((height, 128), 0).astype(f32).astype(bf16)
+    row = jnp.concatenate([row] * (ids.shape[1] // 128), axis=1)
+    return jnp.where(row == low, jnp.ones((), bf16), jnp.zeros((), bf16))
+
+
 def dot(a, b):
     return jnp.dot(a, b, preferred_element_type=f32)
 
@@ -55,17 +62,17 @@
     return jnp.concatenate([row[:, at:at + 128] for at in range(0, row.shape[1], 128)], axis=0)
 
 
-def start_kernel(*refs):
-    count = (len(refs) - 2) // 2
-    sources, places, sums_ref, sems = refs[:count], refs[count:2 * count], refs[-2], refs[-1]
-    copies = [pltpu.make_async_copy(src, dst, sems.at[k]) for k, (src, dst) in enumerate(zip(sources, places))]
-    for copy in copies:
-        copy.start()
-    copies[0].wait()
-    sums = dense_of(jnp.sum(places[0][...], axis=0, keepdims=True))
+def start_kernel(quarter_ref, leaf_ref, seas_ref, fine_ref, mid_ref, top_ref, sums_ref, ids_ref, known_ref):
+    sums = dense_of(jnp.sum(leaf_ref[...], axis=0, keepdims=True))
     sums_ref[...] = jnp.broadcast_to(sums[None], sums_ref.shape)
-    for copy in copies[1:]:
-        copy.wait()
+    for at, ref in enumerate((fine_ref, mid_ref, top_ref)):
+        ids_ref[at:at + 1, :] = ref[...]
+    seas = seas_ref[...]
+    season_days = leaf_ref.shape[0] * 2
+    line = iota(seas.shape, 0)
+    own = jnp.sum(jnp.where(line == quarter_ref[0], seas, 0.0), axis=0, keepdims=True)
+    four = jnp.sum(jnp.where(line < 4, seas, 0.0), axis=0, keepdims=True)
+    known_ref[...] = dense_of(0.5 * own / season_days + 0.5 * (seas[4:5, :] - 0.5 * four) / (season_days * 4))
 
 
 def ranks_of(owner, owners):
@@ -83,33 +90,33 @@
     return jnp.concatenate(ranks, axis=1).astype(i32)
 
 
-def sort_kernel(
-    owners, quarter_ref, leaf_ref, seas_ref, fine_ref, mid_ref, top_ref, base_mid_ref, base_top_ref,
-    slots_ref, nodes_ref, places_ref, from_ref, known_ref, base_ref,
-):
+def sort_kernel(owners, leaf_ref, ids_ref, slots_ref, nodes_ref, places_ref, from_ref):
     days, rows = leaf_ref.shape
-    owner = fine_ref[...] >> 6
+    fine, mid, top = (ids_ref[at:at + 1, :] for at in range(3))
+    owner = fine >> 6
     rank = ranks_of(owner, owners)
     place = owner * 16 + (rank & 15)
     place_low = jnp.where(rank < 16, place, -1)
     place_high = jnp.where(rank < 16, -1, place)
     places_ref[0:1, :] = place_low
     places_ref[1:2, :] = place_high
+    places_ref[2:3, :] = mid
+    places_ref[3:4, :] = top
 
     leaf = leaf_ref[...]
     high = leaf.astype(bf16).astype(f32)
     series = iota((1, rows), 1)
     ones = jnp.ones((1, rows), f32)
-    known = [(fine_ref[...] & 63).astype(f32), ones, ones, (series >> 7).astype(f32), (series & 127).astype(f32)]
+    known = [(fine & 63).astype(f32), ones, ones, (series >> 7).astype(f32), (series & 127).astype(f32)]
     ext = jnp.concatenate([high] + known + [jnp.zeros((3, rows), f32), leaf - high], axis=0).astype(bf16)
     at = 0
     for ids, out_ref, height in (
         (place_low, slots_ref, owners * 16), (place_high, slots_ref, owners * 16),
-        (mid_ref[...], nodes_ref, owners * 8), (top_ref[...], nodes_ref, TOP_ROWS),
+        (mid, nodes_ref, owners * 8), (top, nodes_ref, TOP_ROWS),
     ):
         chunk = min(256, height)
         for start in range(0, height, chunk):
-            sums = dot_nt(ext, ones_where(iota((chunk, rows), 0) + start == ids))
+            sums = dot_nt(ext, hits(ids, start, chunk))
             tail = jnp.concatenate([sums[days + 8:, :], jnp.zeros((8, chunk), f32)], axis=0)
             out_ref[:, at:at + chunk] = sums[:days + 8, :] + tail
             at += chunk
@@ -118,13 +125,9 @@
     from_ref[0, :, :] = dense_of(slots_ref[LOW + 1:LOW + 2, :]).astype(i32)
     from_ref[1, :, :] = dense_of(slots_ref[LOW + 2:LOW + 3, :]).astype(i32)
 
-    seas = seas_ref[...]
-    season_days = days * 2
-    line = iota(seas.shape, 0)
-    own = jnp.sum(jnp.where(line == quarter_ref[0], seas, 0.0), axis=0, keepdims=True)
-    four = jnp.sum(jnp.where(line < 4, seas, 0.0), axis=0, keepdims=True)
-    known_ref[...] = dense_of(0.5 * own / season_days + 0.5 * (seas[4:5, :] - 0.5 * four) / (season_days * 4))
-
+
+def rest_in_lanes(base_mid, base_top):
+    days = base_mid.shape[1]
     half = days // 2
     day, lane = iota((days, 128), 0), iota((days, 128), 1)
     moves = (
@@ -133,10 +136,10 @@
         lane == top_lane(day),
     )
     moves = [jnp.where(move, 1.0, 0.0) for move in moves]
-    top = jnp.where(iota((16, days), 1) // 3 == iota((16, days), 0), base_top_ref[...], 0.0)
+    top = jnp.where(iota((16, days), 1) // 3 == iota((16, days), 0), base_top, 0.0)
     exact = lax.Precision.HIGHEST
-    mids = [jnp.dot(base_mid_ref[...], move, precision=exact, preferred_element_type=f32) for move in moves[:2]]
-    base_ref[...] = jnp.concatenate(mids, axis=0) + jnp.dot(top, moves[2], precision=exact, preferred_element_type=f32)
+    mids = [jnp.dot(base_mid, move, precision=exact, preferred_element_type=f32) for move in moves[:2]]
+    return jnp.concatenate(mids, axis=0) + jnp.dot(top, moves[2], precision=exact, preferred_element_type=f32)
 
 
 def split_count(sums):
@@ -144,9 +147,9 @@
     return jnp.where(iota(sums.shape, 0) == LOW, sums - high, high)
 
 
-def send_kernel(quarter_ref, parts_ref, known_ref, from_ref, slots_ref, nodes_ref, mid_ref, top_ref, pay_ref, shift_ref):
+def send_kernel(quarter_ref, parts_ref, known_ref, from_ref, slots_ref, nodes_ref, places_ref, pay_ref, shift_ref):
     owners = pay_ref.shape[0]
-    rows = mid_ref.shape[1]
+    rows = places_ref.shape[1]
     slots, mids = owners * 16, owners * 8
     days = slots_ref.shape[0] - 8
     season_days = days * 2
@@ -169,11 +172,10 @@
     high = shift_row.astype(bf16).astype(f32)
     ext = jnp.concatenate([high, shift_row - high, jnp.zeros((6, rows), f32)], axis=0).astype(bf16)
     node_sums = []
-    for ids, height in ((mid_ref[...], mids), (top_ref[...], TOP_ROWS)):
+    for ids, height in ((places_ref[2:3, :], mids), (places_ref[3:4, :], TOP_ROWS)):
         chunk = min(256, height)
         for start in range(0, height, chunk):
-            hits = ones_where(iota((chunk, rows), 0) + start == ids)
-            node_sums.append(jnp.sum(dot_nt(ext, hits), axis=0, keepdims=True))
+            node_sums.append(jnp.sum(dot_nt(ext, hits(ids, start, chunk)), axis=0, keepdims=True))
     node_sums = jnp.concatenate(node_sums, axis=1)
     is_day = iota((days + 8, 1), 0) < days
     pad = jnp.zeros((8, rows + mids + TOP_ROWS), f32)
@@ -213,7 +215,7 @@
         pay_ref[g * group:(g + 1) * group, :, :] = (tile.reshape(group, 16, 128) + extra).astype(bf16)
 
 
-def owner_kernel(got_ref, base_fine_ref, base_rest_ref, back_ref):
+def owner_kernel(got_ref, base_fine_ref, base_mid_ref, base_top_ref, back_ref):
     owners = got_ref.shape[0]
     days, nodes = base_fine_ref.shape
     got = got_ref[...].astype(f32)
@@ -233,12 +235,12 @@
     pair = rest + jnp.concatenate([rest[8:16, :], rest[0:8, :]], axis=0)
     of_top = iota(rest.shape, 1) > MID_COUNT
     count = jnp.where(of_top, pair[:, TOP_COUNT:TOP_COUNT + 1], pair[:, MID_COUNT:MID_COUNT + 1])
-    gap_rest = jnp.where(slot_lanes(rest.shape, 1), 0.0, (base_rest_ref[...] - rest) / (count + 1.0))
+    gap_rest = jnp.where(slot_lanes(rest.shape, 1), 0.0, (rest_in_lanes(base_mid_ref[...], base_top_ref[...]) - rest) / (count + 1.0))
     spread = jnp.where(slot_lanes(flat.shape, 1), spread, 0.0).reshape(owners, 16, 128)
     back_ref[...] = (spread + gap_rest[None]).astype(bf16)
 
 
-def finish_kernel(leaf_ref, shift_ref, places_ref, mid_ref, top_ref, back_ref, out_ref):
+def finish_kernel(leaf_ref, shift_ref, places_ref, back_ref, out_ref):
     days, rows = leaf_ref.shape
     owners = back_ref.shape[0]
     slots, mids = owners * 16, owners * 8
@@ -255,12 +257,13 @@
     gaps = [part.astype(bf16) for part in (taken[:days, :], taken[days:2 * days, :], mid, tops)]
     step = min(256, rows)
     for at in range(0, rows, step):
-        ids = (
-            places_ref[0:1, at:at + step], places_ref[1:2, at:at + step], mid_ref[:, at:at + step], top_ref[:, at:at + step]
-        )
+        ids = [places_ref[k:k + 1, at:at + step] for k in range(4)]
         out = leaf_ref[:, at:at + step] + shift_ref[:, at:at + step]
         for gap, place in zip(gaps, ids):
-            out = out + dot(gap, ones_where(iota((gap.shape[1], step), 0) == place))
+            height = gap.shape[1]
+            chunk = min(256, height)
+            blocks = [hits(place, start, chunk) for start in range(0, height, chunk)]
+            out = out + dot(gap, jnp.concatenate(blocks, axis=0))
         out_ref[:, at:at + step] = out
 
 
@@ -269,60 +272,56 @@
     owners = lax.axis_size("series")
     blocks = lax.axis_size("tm")
     quarter = (lax.axis_index("tm") // (blocks // 4)).astype(i32).reshape(1)
-    any_space = pl.BlockSpec(memory_space=pl.ANY)
     vmem = pl.BlockSpec(memory_space=pltpu.VMEM)
     smem = pl.BlockSpec(memory_space=pltpu.SMEM)
-
-    arrays = (leaf, seas, *(ids.reshape(1, rows) for ids in (fine, mid, top)), base_mid.T, base_top.reshape(1, days))
-    *arrays, sums = pl.pallas_call(
+    dense = (rows // 128, 128)
+
+    sums, ids, known = pl.pallas_call(
         start_kernel,
-        out_shape=[jax.ShapeDtypeStruct(x.shape, x.dtype) for x in arrays]
-        + [jax.ShapeDtypeStruct((blocks, rows // 128, 128), f32)],
-        in_specs=[any_space] * len(arrays),
-        scratch_shapes=[pltpu.SemaphoreType.DMA((len(arrays),))],
+        out_shape=(
+            jax.ShapeDtypeStruct((blocks,) + dense, f32),
+            jax.ShapeDtypeStruct((3, rows), i32),
+            jax.ShapeDtypeStruct(dense, f32),
+        ),
+        in_specs=[smem] + [vmem] * 5,
         compiler_params=PARAMS,
         name="start",
-    )(*arrays)
+    )(quarter, leaf, seas, *(ids.reshape(1, rows) for ids in (fine, mid, top)))
     parts = lax.all_to_all(sums, "tm", 0, 0, tiled=True)
-    leaf, seas, fine, mid, top, base_mid, base_top = arrays
-    dense = (rows // 128, 128)
-    slots, nodes, places, come_from, known, base_rest = pl.pallas_call(
+    slots, nodes, places, come_from = pl.pallas_call(
         lambda *refs: sort_kernel(owners, *refs),
         out_shape=(
             jax.ShapeDtypeStruct((days + 8, rows), f32),
             jax.ShapeDtypeStruct((days + 8, owners * 8 + TOP_ROWS), f32),
-            jax.ShapeDtypeStruct((2, rows), i32),
+            jax.ShapeDtypeStruct((4, rows), i32),
             jax.ShapeDtypeStruct((2,) + dense, i32),
-            jax.ShapeDtypeStruct(dense, f32),
-            jax.ShapeDtypeStruct((16, 128), f32),
         ),
-        in_specs=[smem] + [vmem] * 7,
         compiler_params=PARAMS,
         cost_estimate=pl.CostEstimate(flops=2 * 104 * owners * 42 * rows, bytes_accessed=4 * days * rows, transcendentals=0),
         name="sort",
-    )(quarter, *arrays)
+    )(leaf, ids)
 
     payload, shift = pl.pallas_call(
         send_kernel,
         out_shape=(jax.ShapeDtypeStruct((owners, 16, 128), bf16), jax.ShapeDtypeStruct((1, rows), f32)),
-        in_specs=[smem] + [vmem] * 7,
+        in_specs=[smem] + [vmem] * 6,
         compiler_params=PARAMS,
         name="pack",
-    )(quarter, parts, known, come_from, slots, nodes, mid, top)
+    )(quarter, parts, known, come_from, slots, nodes, places)
     got = lax.all_to_all(payload, "series", 0, 0, tiled=True)
     back = pl.pallas_call(
         owner_kernel,
         out_shape=jax.ShapeDtypeStruct((owners, 16, 128), bf16),
         compiler_params=PARAMS,
         name="gaps",
-    )(got, base_fine, base_rest)
+    )(got, base_fine, base_mid.T, base_top.reshape(1, days))
     back = lax.all_to_all(back, "series", 0, 0, tiled=True)
     return pl.pallas_call(
         finish_kernel,
         out_shape=jax.ShapeDtypeStruct((days, rows), f32),
         compiler_params=PARAMS,
         name="finish",
-    )(leaf, shift, places, mid, top, back)
+    )(leaf, shift, places, back)
 
 
 def solution(mesh):

time: 70.6 us -> 68.7 us (0.973)
  local copies, waits for them, and re-layouts: 4.62 us -> 3.22 us
    unnamed x16 -> x18, local copies, waits for them, and re-layouts: 4.62 us -> 3.22 us
where the time goes in v7:
time: 68.7 us; the launch traced here: 68.2 us
  blocking collectives  45.8 us (67%)
  Pallas kernels  10 us (15%)
  starting transfers between devices  9.14 us (13%)
  local copies, waits for them, and re-layouts  3.22 us (5%)
    all_to_all x1, blocking collectives, per_device(): got = lax.all_to_all(payload, 'series', 0, 0, tiled=True)  27.3 us
    all_to_all x1, blocking collectives, per_device(): back = lax.all_to_all(back, 'series', 0, 0, tiled=True)  18.5 us
    all_to_all x1, starting transfers between devices, per_device(): parts = lax.all_to_all(sums, 'tm', 0, 0, tiled=True)  9.14 us
    pallas_call x1, Pallas kernels, per_device(): pl.pallas_call(lambda *refs: sort_kernel(owners, *refs), out_shape=(jax.S...  3.82 us
    unnamed x18, local copies, waits for them, and re-layouts  3.22 us
    pallas_call x1, Pallas kernels, per_device(): pl.pallas_call(finish_kernel, out_shape=jax.ShapeDtypeStruct((days, rows)...  3.14 us
    pallas_call x1, Pallas kernels, per_device(): pl.pallas_call(send_kernel, out_shape=(jax.ShapeDtypeStruct((owners, 16,...  1.44 us
  transfers between devices with their start and end apart: 1, of which 0 were waited for; matrix products, arithmetic and copies ran while one was open for 0% of the time, Pallas kernels for 6%

profile of v7, /device:TPU:6, one launch (start us, length us, event | category | flops | bytes accessed | tf_op | source)
XLA Modules:
  0.0 68.2 jit_solution(7337653618785781795)
XLA Ops:
  0.0 0.0 copy-start.6
  0.0 0.0 copy-start.5
  0.0 0.0 copy-start.4
  0.0 0.7 copy-done.6
  0.7 0.0 copy-done.5
  0.7 0.0 copy-done.4
  0.7 0.0 copy-start
  0.7 1.0 %copy-done = f32[48,2048]{1,0:T(8,128)S(1)} copy-done((f32[48,2048]{1,0:T(8,128)S(1)}, f32[48,2048]{1,0:T(8,128)}, u32[]{:S(2)}) %copy-start) | copy-done | bytes 393240
  1.7 0.0 copy-start.2
  1.7 0.8 %copy-done.2 = f32[5,2048]{1,0:T(8,128)S(1)} copy-done((f32[5,2048]{1,0:T(8,128)S(1)}, f32[5,2048]{1,0:T(8,128)}, u32[]{:S(2)}) %copy-start.2) | copy-done | bytes 40984
  2.6 0.0 copy-start.1
  2.6 0.7 start.1
  3.2 9.1 %all-to-all-start = ((f32[8,16,128]{2,1,0:T(8,128)}), f32[8,16,128]{2,1,0:T(8,128)S(1)}, u32[]{:S(2)}, u32[]{:S(2)}) async-start(f32[8,16,128]{2,1,0:T(8,128)} %get-tuple-element.14), calls=%async_computation | async-start | bytes 131072 | tf_op jit(solution)/shard_map/all_to_all | solution.py:290
  12.4 0.0 copy-done.1
  12.4 3.8 %sort.1 = (f32[56,2048]{1,0:T(8,128)S(1)}, f32[56,640]{1,0:T(8,128)S(1)}, s32[4,2048]{1,0:T(4,128)S(1)}, s32[2,16,128]{2,1,0:T(8,128)S(1)}) custom-call(f32[48,2048]{1,0:T(8,128)S(1)} %copy-done.1, s32[3,2048]{1,0:T(4,128)S(1)} %get-tuple-element.16.refs_1_), custom_call_target="tpu_custom_call" | custom-call | flops 1145044992 | bytes 393216 | tf_op jit(solution)/shard_map/sort/pallas_call | solution.py:291
  16.2 0.0 all-to-all-done.parts_ref
  16.2 1.4 %pack.1 = (bf16[64,16,128]{2,1,0:T(8,128)(2,1)S(1)}, f32[1,2048]{1,0:T(1,128)S(1)}) custom-call(s32[1]{0:T(128)} %bitcast.quarter_ref, f32[8,16,128]{2,1,0:T(8,128)S(1)} %all-to-all-done.parts_ref, f32[16,128]{1,0:T(8,128)S(1)} %get-tuple-element.15.known_ref, s32[2,16,128]{2,1,0:T(8,128)S(1)} %get-tuple-element.17.from_ref, ...), custom_call_target="tpu_custom_call" | custom-call | tf_op jit(solution)/shard_map/pack/pallas_call | solution.py:304
  17.7 0.0 copy-start.3
  17.7 0.0 copy-start.7
  17.7 27.3 %all_to_all.15.got_ref = bf16[64,16,128]{2,1,0:T(8,128)(2,1)S(1)} all-to-all(bf16[64,16,128]{2,1,0:T(8,128)(2,1)S(1)} %get-tuple-element.22), channel_id=1, replica_groups=mesh['tm'=8,'series'=64] {'series'}, dimensions={0} | all-to-all | bytes 524288 | tf_op jit(solution)/shard_map/all_to_all | solution.py:311
  45.0 0.0 copy-start.8
  45.0 0.0 copy-done.3
  45.0 0.0 copy-done.7
  45.0 0.6 copy-done.8
  45.6 1.0 %gaps.1 = bf16[64,16,128]{2,1,0:T(8,128)(2,1)S(1)} custom-call(bf16[64,16,128]{2,1,0:T(8,128)(2,1)S(1)} %all_to_all.15.got_ref, f32[48,64]{1,0:T(8,128)S(1)} %copy-done.3, f32[8,48]{1,0:T(8,128)S(1)} %bitcast.9, f32[1,48]{1,0:T(1,128)S(1)} %bitcast.10), custom_call_target="tpu_custom_call" | custom-call | tf_op jit(solution)/shard_map/gaps/pallas_call | solution.py:312
  46.6 18.5 %all_to_all.16.back_ref = bf16[64,16,128]{2,1,0:T(8,128)(2,1)S(1)} all-to-all(bf16[64,16,128]{2,1,0:T(8,128)(2,1)S(1)} %gaps.1), channel_id=1, replica_groups=mesh['tm'=8,'series'=64] {'series'}, dimensions={0} | all-to-all | bytes 524288 | tf_op jit(solution)/shard_map/all_to_all | solution.py:318
  65.1 3.1 %finish.1 = f32[48,2048]{1,0:T(8,128)} custom-call(f32[48,2048]{1,0:T(8,128)S(1)} %copy-done.1, f32[1,2048]{1,0:T(1,128)S(1)} %get-tuple-element.21.shift_ref, s32[4,2048]{1,0:T(4,128)S(1)} %get-tuple-element.20.places_ref, bf16[64,16,128]{2,1,0:T(8,128)(2,1)S(1)} %all_to_all.16.back_ref), custom_call_target="tpu_custom_call" | custom-call | tf_op jit(solution)/shard_map/finish/pallas_call | solution.py:319
Async XLA Ops:
  0.0 0.7 %copy-start.6 = (s32[2048,1]{0,1:T(1,128)S(1)}, s32[2048,1]{0,1:T(1,128)}, u32[]{:S(2)}) copy-start(s32[2048,1]{0,1:T(1,128)} %param.12) | copy-start | bytes 24580
  0.0 0.7 %copy-start.5 = (s32[2048,1]{0,1:T(1,128)S(1)}, s32[2048,1]{0,1:T(1,128)}, u32[]{:S(2)}) copy-start(s32[2048,1]{0,1:T(1,128)} %param.11) | copy-start | bytes 24580
  0.0 0.7 %copy-start.4 = (s32[2048,1]{0,1:T(1,128)S(1)}, s32[2048,1]{0,1:T(1,128)}, u32[]{:S(2)}) copy-start(s32[2048,1]{0,1:T(1,128)} %param.10) | copy-start | bytes 24580
  0.7 1.0 %copy-start = (f32[48,2048]{1,0:T(8,128)S(1)}, f32[48,2048]{1,0:T(8,128)}, u32[]{:S(2)}) copy-start(f32[48,2048]{1,0:T(8,128)} %leaf_ref.3) | copy-start | bytes 1179652
  1.7 0.8 %copy-start.2 = (f32[5,2048]{1,0:T(8,128)S(1)}, f32[5,2048]{1,0:T(8,128)}, u32[]{:S(2)}) copy-start(f32[5,2048]{1,0:T(8,128)} %seas_ref.1) | copy-start | bytes 122884
  2.6 9.8 %copy-start.1 = (f32[48,2048]{1,0:T(8,128)S(1)}, f32[48,2048]{1,0:T(8,128)}, u32[]{:S(2)}) copy-start(f32[48,2048]{1,0:T(8,128)} %leaf_ref.3) | copy-start | bytes 1179652
  3.2 13.0 %all-to-all-start = ((f32[8,16,128]{2,1,0:T(8,128)}), f32[8,16,128]{2,1,0:T(8,128)S(1)}, u32[]{:S(2)}, u32[]{:S(2)}) async-start(f32[8,16,128]{2,1,0:T(8,128)} %get-tuple-element.14), calls=%async_computation | async-start | bytes 131072 | tf_op jit(solution)/shard_map/all_to_all | solution.py:290
  17.7 27.3 %copy-start.3 = (f32[48,64]{1,0:T(8,128)S(1)}, f32[48,64]{1,0:T(8,128)}, u32[]{:S(2)}) copy-start(f32[48,64]{1,0:T(8,128)} %base_fine_ref.1) | copy-start | bytes 36868
  17.7 27.3 %copy-start.7 = (f32[48,8]{0,1:T(8,128)S(1)}, f32[48,8]{0,1:T(8,128)}, u32[]{:S(2)}) copy-start(f32[48,8]{0,1:T(8,128)} %param.14) | copy-start | bytes 4612
  45.0 0.7 copy-start.8

commit v8 on v7

--- a/solution.py
+++ b/solution.py
@@ -35,11 +35,18 @@
     return jnp.where(mask, 1.0, 0.0).astype(bf16)
 
 
-def hits(ids, start, height):
-    low = jnp.where((ids >> 8) == (start >> 8), ids & 255, -1).astype(f32).astype(bf16)
+def hits(codes, height):
     row = iota((height, 128), 0).astype(f32).astype(bf16)
-    row = jnp.concatenate([row] * (ids.shape[1] // 128), axis=1)
-    return jnp.where(row == low, jnp.ones((), bf16), jnp.zeros((), bf16))
+    row = jnp.concatenate([row] * (codes.shape[1] // 128), axis=1)
+    return jnp.where(row == codes.astype(f32).astype(bf16), jnp.ones((), bf16), jnp.zeros((), bf16))
+
+
+def node_hits(mid, top, width):
+    return jnp.concatenate([hits(mid & (width - 1), width), hits(top, TOP_ROWS)], axis=0)
+
+
+def by_group(rows, group, count):
+    return jnp.concatenate([rows * ones_where(group == g) for g in range(count)], axis=0)
 
 
 def dot(a, b):
@@ -62,17 +69,13 @@
     return jnp.concatenate([row[:, at:at + 128] for at in range(0, row.shape[1], 128)], axis=0)
 
 
-def start_kernel(quarter_ref, leaf_ref, seas_ref, fine_ref, mid_ref, top_ref, sums_ref, ids_ref, known_ref):
+def start_kernel(leaf_ref, fine_ref, mid_ref, top_ref, base_mid_ref, base_top_ref, sums_ref, ids_ref, base_ref):
     sums = dense_of(jnp.sum(leaf_ref[...], axis=0, keepdims=True))
     sums_ref[...] = jnp.broadcast_to(sums[None], sums_ref.shape)
     for at, ref in enumerate((fine_ref, mid_ref, top_ref)):
         ids_ref[at:at + 1, :] = ref[...]
-    seas = seas_ref[...]
-    season_days = leaf_ref.shape[0] * 2
-    line = iota(seas.shape, 0)
-    own = jnp.sum(jnp.where(line == quarter_ref[0], seas, 0.0), axis=0, keepdims=True)
-    four = jnp.sum(jnp.where(line < 4, seas, 0.0), axis=0, keepdims=True)
-    known_ref[...] = dense_of(0.5 * own / season_days + 0.5 * (seas[4:5, :] - 0.5 * four) / (season_days * 4))
+    base_ref[0:8, :] = base_mid_ref[...]
+    base_ref[8:9, :] = base_top_ref[...]
 
 
 def ranks_of(owner, owners):
@@ -95,33 +98,37 @@
     fine, mid, top = (ids_ref[at:at + 1, :] for at in range(3))
     owner = fine >> 6
     rank = ranks_of(owner, owners)
-    place = owner * 16 + (rank & 15)
-    place_low = jnp.where(rank < 16, place, -1)
-    place_high = jnp.where(rank < 16, -1, place)
-    places_ref[0:1, :] = place_low
-    places_ref[1:2, :] = place_high
-    places_ref[2:3, :] = mid
-    places_ref[3:4, :] = top
+    place = (rank >> 4) * (owners * 16) + owner * 16 + (rank & 15)
+    places_ref[0:1, :] = place
+    places_ref[1:2, :] = mid
+    places_ref[2:3, :] = top
 
     leaf = leaf_ref[...]
     high = leaf.astype(bf16).astype(f32)
     series = iota((1, rows), 1)
     ones = jnp.ones((1, rows), f32)
     known = [(fine & 63).astype(f32), ones, ones, (series >> 7).astype(f32), (series & 127).astype(f32)]
-    ext = jnp.concatenate([high] + known + [jnp.zeros((3, rows), f32), leaf - high], axis=0).astype(bf16)
-    at = 0
-    for ids, out_ref, height in (
-        (place_low, slots_ref, owners * 16), (place_high, slots_ref, owners * 16),
-        (mid, nodes_ref, owners * 8), (top, nodes_ref, TOP_ROWS),
-    ):
-        chunk = min(256, height)
-        for start in range(0, height, chunk):
-            sums = dot_nt(ext, hits(ids, start, chunk))
-            tail = jnp.concatenate([sums[days + 8:, :], jnp.zeros((8, chunk), f32)], axis=0)
-            out_ref[:, at:at + chunk] = sums[:days + 8, :] + tail
-            at += chunk
-        if ids is place_high:
-            at = 0
+    zeros = [jnp.zeros((3, rows), f32), jnp.zeros((8, rows), f32)]
+    ext = jnp.concatenate([high] + known + [zeros[0], leaf - high, zeros[1]], axis=0).astype(bf16)
+    height = days + 8
+
+    def add_low(part):
+        return part[:height, :] + jnp.concatenate([part[height:height + days, :], jnp.zeros((8, part.shape[1]), f32)], axis=0)
+
+    count = rows // 256
+    sums = dot_nt(by_group(ext, place >> 8, count), hits(place & 255, 256))
+    for g in range(count):
+        slots_ref[:, g * 256:(g + 1) * 256] = add_low(sums[g * 2 * height:(g + 1) * 2 * height, :])
+    mids = owners * 8
+    width = min(128, mids)
+    count = mids // width
+    sums = dot_nt(by_group(ext, mid // width, count), node_hits(mid, top, width))
+    tops = jnp.zeros((height, TOP_ROWS), f32)
+    for g in range(count):
+        part = add_low(sums[g * 2 * height:(g + 1) * 2 * height, :])
+        nodes_ref[:, g * width:(g + 1) * width] = part[:, :width]
+        tops = tops + part[:, width:]
+    nodes_ref[:, mids:] = tops
     from_ref[0, :, :] = dense_of(slots_ref[LOW + 1:LOW + 2, :]).astype(i32)
     from_ref[1, :, :] = dense_of(slots_ref[LOW + 2:LOW + 3, :]).astype(i32)
 
@@ -147,7 +154,7 @@
     return jnp.where(iota(sums.shape, 0) == LOW, sums - high, high)
 
 
-def send_kernel(quarter_ref, parts_ref, known_ref, from_ref, slots_ref, nodes_ref, places_ref, pay_ref, shift_ref):
+def send_kernel(quarter_ref, parts_ref, seas_ref, from_ref, slots_ref, nodes_ref, places_ref, pay_ref, shift_ref):
     owners = pay_ref.shape[0]
     rows = places_ref.shape[1]
     slots, mids = owners * 16, owners * 8
@@ -156,7 +163,12 @@
     parts = parts_ref[...]
     own = jnp.sum(jnp.where(iota(parts.shape, 0) >> 1 == quarter_ref[0], parts, 0.0), axis=0)
     total = jnp.sum(parts, axis=0)
-    shift = known_ref[...] - (0.5 * own / season_days + 0.25 * total / (season_days * 4))
+    seas = seas_ref[...]
+    line = iota(seas.shape, 0)
+    seas_own = jnp.sum(jnp.where(line == quarter_ref[0], seas, 0.0), axis=0, keepdims=True)
+    seas_four = jnp.sum(jnp.where(line < 4, seas, 0.0), axis=0, keepdims=True)
+    known = dense_of(0.5 * seas_own / season_days + 0.5 * (seas[4:5, :] - 0.5 * seas_four) / (season_days * 4))
+    shift = known - (0.5 * own / season_days + 0.25 * total / (season_days * 4))
     shift_row = row_of(shift)
     shift_ref[...] = shift_row
 
@@ -170,13 +182,13 @@
     moved = row_of(moved)
 
     high = shift_row.astype(bf16).astype(f32)
-    ext = jnp.concatenate([high, shift_row - high, jnp.zeros((6, rows), f32)], axis=0).astype(bf16)
-    node_sums = []
-    for ids, height in ((places_ref[2:3, :], mids), (places_ref[3:4, :], TOP_ROWS)):
-        chunk = min(256, height)
-        for start in range(0, height, chunk):
-            node_sums.append(jnp.sum(dot_nt(ext, hits(ids, start, chunk)), axis=0, keepdims=True))
-    node_sums = jnp.concatenate(node_sums, axis=1)
+    ext = jnp.concatenate([high, shift_row - high, jnp.zeros((14, rows), f32)], axis=0).astype(bf16)
+    mid, top = places_ref[1:2, :], places_ref[2:3, :]
+    width = min(128, mids)
+    count = mids // width
+    found = dot_nt(by_group(ext, mid // width, count), node_hits(mid, top, width))
+    found = [jnp.sum(found[g * 16:(g + 1) * 16, :], axis=0, keepdims=True) for g in range(count)]
+    node_sums = jnp.concatenate([part[:, :width] for part in found] + [sum(part[:, width:] for part in found)], axis=1)
     is_day = iota((days + 8, 1), 0) < days
     pad = jnp.zeros((8, rows + mids + TOP_ROWS), f32)
     sums = jnp.concatenate([slots_ref[...], nodes_ref[...]], axis=1)
@@ -215,7 +227,7 @@
         pay_ref[g * group:(g + 1) * group, :, :] = (tile.reshape(group, 16, 128) + extra).astype(bf16)
 
 
-def owner_kernel(got_ref, base_fine_ref, base_mid_ref, base_top_ref, back_ref):
+def owner_kernel(got_ref, base_fine_ref, base_ref, back_ref):
     owners = got_ref.shape[0]
     days, nodes = base_fine_ref.shape
     got = got_ref[...].astype(f32)
@@ -235,7 +247,7 @@
     pair = rest + jnp.concatenate([rest[8:16, :], rest[0:8, :]], axis=0)
     of_top = iota(rest.shape, 1) > MID_COUNT
     count = jnp.where(of_top, pair[:, TOP_COUNT:TOP_COUNT + 1], pair[:, MID_COUNT:MID_COUNT + 1])
-    gap_rest = jnp.where(slot_lanes(rest.shape, 1), 0.0, (rest_in_lanes(base_mid_ref[...], base_top_ref[...]) - rest) / (count + 1.0))
+    gap_rest = jnp.where(slot_lanes(rest.shape, 1), 0.0, (rest_in_lanes(base_ref[0:8, :], base_ref[8:9, :]) - rest) / (count + 1.0))
     spread = jnp.where(slot_lanes(flat.shape, 1), spread, 0.0).reshape(owners, 16, 128)
     back_ref[...] = (spread + gap_rest[None]).astype(bf16)
 
@@ -254,16 +266,25 @@
     first, last = (back[:, at:at + 8, :].reshape(mids, 128).astype(bf16) for at in (0, 8))
     mid = dot_nt(ones_where((day < half) & (lane == lane_of(day))), first)
     mid = mid + dot_nt(ones_where((day >= half) & (lane == lane_of(day - half))), last)
-    gaps = [part.astype(bf16) for part in (taken[:days, :], taken[days:2 * days, :], mid, tops)]
-    step = min(256, rows)
+    slot_count, width = rows // 256, min(128, mids)
+    mid_count = mids // width
+    taken = jnp.concatenate([taken[:days, :], taken[days:2 * days, :]], axis=1)
+    slot_gaps = jnp.concatenate([taken[:, g * 256:(g + 1) * 256] for g in range(slot_count)], axis=0).astype(bf16)
+    node_gaps = [jnp.concatenate([mid[:, g * width:(g + 1) * width], tops], axis=1) for g in range(mid_count)]
+    node_gaps = jnp.concatenate(node_gaps, axis=0).astype(bf16)
+    step = min(512, rows)
     for at in range(0, rows, step):
-        ids = [places_ref[k:k + 1, at:at + step] for k in range(4)]
+        place, mid, top = (places_ref[k:k + 1, at:at + step] for k in range(3))
         out = leaf_ref[:, at:at + step] + shift_ref[:, at:at + step]
-        for gap, place in zip(gaps, ids):
-            height = gap.shape[1]
-            chunk = min(256, height)
-            blocks = [hits(place, start, chunk) for start in range(0, height, chunk)]
-            out = out + dot(gap, jnp.concatenate(blocks, axis=0))
+        for gaps, hit, group, count in (
+            (slot_gaps, hits(place & 255, 256), place >> 8, slot_count),
+            (node_gaps, node_hits(mid, top, width), mid // width, mid_count),
+        ):
+            found = dot(gaps, hit)
+            chosen = found[:days, :]
+            for g in range(1, count):
+                chosen = jnp.where(group == g, found[g * days:(g + 1) * days, :], chosen)
+            out = out + chosen
         out_ref[:, at:at + step] = out
 
 
@@ -276,24 +297,23 @@
     smem = pl.BlockSpec(memory_space=pltpu.SMEM)
     dense = (rows // 128, 128)
 
-    sums, ids, known = pl.pallas_call(
+    sums, ids, base = pl.pallas_call(
         start_kernel,
         out_shape=(
             jax.ShapeDtypeStruct((blocks,) + dense, f32),
             jax.ShapeDtypeStruct((3, rows), i32),
-            jax.ShapeDtypeStruct(dense, f32),
+            jax.ShapeDtypeStruct((16, days), f32),
         ),
-        in_specs=[smem] + [vmem] * 5,
         compiler_params=PARAMS,
         name="start",
-    )(quarter, leaf, seas, *(ids.reshape(1, rows) for ids in (fine, mid, top)))
+    )(leaf, *(ids.reshape(1, rows) for ids in (fine, mid, top)), base_mid.T, base_top.reshape(1, days))
     parts = lax.all_to_all(sums, "tm", 0, 0, tiled=True)
     slots, nodes, places, come_from = pl.pallas_call(
         lambda *refs: sort_kernel(owners, *refs),
         out_shape=(
             jax.ShapeDtypeStruct((days + 8, rows), f32),
             jax.ShapeDtypeStruct((days + 8, owners * 8 + TOP_ROWS), f32),
-            jax.ShapeDtypeStruct((4, rows), i32),
+            jax.ShapeDtypeStruct((3, rows), i32),
             jax.ShapeDtypeStruct((2,) + dense, i32),
         ),
         compiler_params=PARAMS,
@@ -307,14 +327,14 @@
         in_specs=[smem] + [vmem] * 6,
         compiler_params=PARAMS,
         name="pack",
-    )(quarter, parts, known, come_from, slots, nodes, places)
+    )(quarter, parts, seas, come_from, slots, nodes, places)
     got = lax.all_to_all(payload, "series", 0, 0, tiled=True)
     back = pl.pallas_call(
         owner_kernel,
         out_shape=jax.ShapeDtypeStruct((owners, 16, 128), bf16),
         compiler_params=PARAMS,
         name="gaps",
-    )(got, base_fine, base_mid.T, base_top.reshape(1, days))
+    )(got, base_fine, base)
     back = lax.all_to_all(back, "series", 0, 0, tiled=True)
     return pl.pallas_call(
         finish_kernel,

time: 68.7 us -> 67.7 us (0.985)
  Pallas kernels: 10 us -> 6.63 us
  waiting for transfers between devices: 0.01 us -> 1.62 us
    pallas_call x1, Pallas kernels: 3.82 us -> 1.9 us  [per_device(): pl.pallas_call(lambda *refs: sort_kernel(owners, *refs), out_shape=(jax.S...]
    all_to_all x1, waiting for transfers between devices: 0.01 us -> 1.62 us  [per_device(): parts = lax.all_to_all(sums, 'tm', 0, 0, tiled=True)]
    pallas_call x1, Pallas kernels: 3.14 us -> 1.9 us  [per_device(): pl.pallas_call(finish_kernel, out_shape=jax.ShapeDtypeStruct((days, rows)...]
  transfers between devices with their start and end apart: 1 -> 1, of which waited for: 0 -> 1; matrix products, arithmetic and copies ran while one was open for 0% -> 0% of each run, Pallas kernels for 6% -> 3%
where the time goes in v8:
time: 67.7 us; the launch traced here: 66.6 us
  blocking collectives  45.4 us (67%)
  starting transfers between devices  9.14 us (14%)
  Pallas kernels  6.63 us (10%)
  local copies, waits for them, and re-layouts  3.79 us (6%)
  waiting for transfers between devices  1.62 us (2%)
    all_to_all x1, blocking collectives, per_device(): got = lax.all_to_all(payload, 'series', 0, 0, tiled=True)  27 us
    all_to_all x1, blocking collectives, per_device(): back = lax.all_to_all(back, 'series', 0, 0, tiled=True)  18.4 us
    all_to_all x1, starting transfers between devices, per_device(): parts = lax.all_to_all(sums, 'tm', 0, 0, tiled=True)  9.14 us
    unnamed x18, local copies, waits for them, and re-layouts  3.79 us
    pallas_call x1, Pallas kernels, per_device(): pl.pallas_call(finish_kernel, out_shape=jax.ShapeDtypeStruct((days, rows)...  1.9 us
    pallas_call x1, Pallas kernels, per_device(): pl.pallas_call(lambda *refs: sort_kernel(owners, *refs), out_shape=(jax.S...  1.9 us
    all_to_all x1, waiting for transfers between devices, per_device(): parts = lax.all_to_all(sums, 'tm', 0, 0, tiled=True)  1.62 us
  transfers between devices with their start and end apart: 1, of which 1 were waited for; matrix products, arithmetic and copies ran while one was open for 0% of the time, Pallas kernels for 3%

profile of v8, /device:TPU:6, one launch (start us, length us, event | category | flops | bytes accessed | tf_op | source)
XLA Modules:
  0.0 66.6 jit_solution(4724254492064705812)
XLA Ops:
  0.0 0.0 copy-start.4
  0.0 0.0 copy-start.8
  0.0 0.7 %copy-done.4 = s32[2048,1]{0,1:T(1,128)S(1)} copy-done((s32[2048,1]{0,1:T(1,128)S(1)}, s32[2048,1]{0,1:T(1,128)}, u32[]{:S(2)}) %copy-start.4) | copy-done | bytes 8216
  0.7 0.0 copy-done.8
  0.7 0.0 copy-start
  0.7 1.0 %copy-done = f32[48,2048]{1,0:T(8,128)S(1)} copy-done((f32[48,2048]{1,0:T(8,128)S(1)}, f32[48,2048]{1,0:T(8,128)}, u32[]{:S(2)}) %copy-start) | copy-done | bytes 393240
  1.7 0.0 copy-start.5
  1.7 0.7 %copy-done.5 = s32[2048,1]{0,1:T(1,128)S(1)} copy-done((s32[2048,1]{0,1:T(1,128)S(1)}, s32[2048,1]{0,1:T(1,128)}, u32[]{:S(2)}) %copy-start.5) | copy-done | bytes 8216
  2.4 0.0 copy-start.6
  2.4 0.7 %copy-done.6 = s32[2048,1]{0,1:T(1,128)S(1)} copy-done((s32[2048,1]{0,1:T(1,128)S(1)}, s32[2048,1]{0,1:T(1,128)}, u32[]{:S(2)}) %copy-start.6) | copy-done | bytes 8216
  3.1 0.0 copy-start.7
  3.1 0.7 %copy-done.7 = f32[48,8]{0,1:T(8,128)S(1)} copy-done((f32[48,8]{0,1:T(8,128)S(1)}, f32[48,8]{0,1:T(8,128)}, u32[]{:S(2)}) %copy-start.7) | copy-done | bytes 1560
  3.8 0.0 copy-start.1
  3.8 0.7 start.1
  4.4 9.1 %all-to-all-start = ((f32[8,16,128]{2,1,0:T(8,128)}), f32[8,16,128]{2,1,0:T(8,128)S(1)}, u32[]{:S(2)}, u32[]{:S(2)}) async-start(f32[8,16,128]{2,1,0:T(8,128)} %get-tuple-element.14), calls=%async_computation | async-start | bytes 131072 | tf_op jit(solution)/shard_map/all_to_all | solution.py:310
  13.6 0.0 copy-done.1
  13.6 0.0 copy-start.2
  13.6 1.9 %sort.1 = (f32[56,2048]{1,0:T(8,128)S(1)}, f32[56,640]{1,0:T(8,128)S(1)}, s32[3,2048]{1,0:T(4,128)S(1)}, s32[2,16,128]{2,1,0:T(8,128)S(1)}) custom-call(f32[48,2048]{1,0:T(8,128)S(1)} %copy-done.1, s32[3,2048]{1,0:T(4,128)S(1)} %get-tuple-element.15.refs_1_), custom_call_target="tpu_custom_call" | custom-call | flops 1145044992 | bytes 393216 | tf_op jit(solution)/shard_map/sort/pallas_call | solution.py:311
  15.5 1.6 %all-to-all-done.parts_ref = f32[8,16,128]{2,1,0:T(8,128)S(1)} async-done(((f32[8,16,128]{2,1,0:T(8,128)}), f32[8,16,128]{2,1,0:T(8,128)S(1)}, u32[]{:S(2)}, u32[]{:S(2)}) %all-to-all-start) | async-done | bytes 65568 | tf_op jit(solution)/shard_map/all_to_all | solution.py:310
  17.1 0.0 copy-done.2
  17.1 1.2 %pack.1 = (bf16[64,16,128]{2,1,0:T(8,128)(2,1)S(1)}, f32[1,2048]{1,0:T(1,128)S(1)}) custom-call(s32[1]{0:T(128)} %bitcast.quarter_ref, f32[8,16,128]{2,1,0:T(8,128)S(1)} %all-to-all-done.parts_ref, f32[5,2048]{1,0:T(8,128)S(1)} %copy-done.2, s32[2,16,128]{2,1,0:T(8,128)S(1)} %get-tuple-element.16.from_ref, f32[56,2048]{1,0:T(8,128)S(1)} %get-tuple-element.17.slots_ref, ...), custom_call_target="tpu_custom_call" | custom-call | tf_op jit(solution)/shard_map/pack/pallas_call | solution.py:324
  18.3 0.0 copy-start.3
  18.3 27.0 %all_to_all.15.got_ref = bf16[64,16,128]{2,1,0:T(8,128)(2,1)S(1)} all-to-all(bf16[64,16,128]{2,1,0:T(8,128)(2,1)S(1)} %get-tuple-element.21), channel_id=1, replica_groups=mesh['tm'=8,'series'=64] {'series'}, dimensions={0} | all-to-all | bytes 524288 | tf_op jit(solution)/shard_map/all_to_all | solution.py:331
  45.3 0.0 copy-done.3
  45.3 1.0 %gaps.1 = bf16[64,16,128]{2,1,0:T(8,128)(2,1)S(1)} custom-call(bf16[64,16,128]{2,1,0:T(8,128)(2,1)S(1)} %all_to_all.15.got_ref, f32[48,64]{1,0:T(8,128)S(1)} %copy-done.3, f32[16,48]{1,0:T(8,128)S(1)} %get-tuple-element.22.base_ref), custom_call_target="tpu_custom_call" | custom-call | tf_op jit(solution)/shard_map/gaps/pallas_call | solution.py:332
  46.3 18.4 %all_to_all.16.back_ref = bf16[64,16,128]{2,1,0:T(8,128)(2,1)S(1)} all-to-all(bf16[64,16,128]{2,1,0:T(8,128)(2,1)S(1)} %gaps.1), channel_id=1, replica_groups=mesh['tm'=8,'series'=64] {'series'}, dimensions={0} | all-to-all | bytes 524288 | tf_op jit(solution)/shard_map/all_to_all | solution.py:338
  64.7 1.9 %finish.1 = f32[48,2048]{1,0:T(8,128)} custom-call(f32[48,2048]{1,0:T(8,128)S(1)} %copy-done.1, f32[1,2048]{1,0:T(1,128)S(1)} %get-tuple-element.20.shift_ref, s32[3,2048]{1,0:T(4,128)S(1)} %get-tuple-element.19.places_ref, bf16[64,16,128]{2,1,0:T(8,128)(2,1)S(1)} %all_to_all.16.back_ref), custom_call_target="tpu_custom_call" | custom-call | tf_op jit(solution)/shard_map/finish/pallas_call | solution.py:339
Async XLA Ops:
  0.0 0.7 %copy-start.4 = (s32[2048,1]{0,1:T(1,128)S(1)}, s32[2048,1]{0,1:T(1,128)}, u32[]{:S(2)}) copy-start(s32[2048,1]{0,1:T(1,128)} %param.10) | copy-start | bytes 24580
  0.0 0.7 %copy-start.8 = (f32[48,1]{0,1:T(1,128)S(1)}, f32[48,1]{0,1:T(1,128)}, u32[]{:S(2)}) copy-start(f32[48,1]{0,1:T(1,128)} %param.15) | copy-start | bytes 580
  0.7 1.0 %copy-start = (f32[48,2048]{1,0:T(8,128)S(1)}, f32[48,2048]{1,0:T(8,128)}, u32[]{:S(2)}) copy-start(f32[48,2048]{1,0:T(8,128)} %leaf_ref.3) | copy-start | bytes 1179652
  1.7 0.7 %copy-start.5 = (s32[2048,1]{0,1:T(1,128)S(1)}, s32[2048,1]{0,1:T(1,128)}, u32[]{:S(2)}) copy-start(s32[2048,1]{0,1:T(1,128)} %param.11) | copy-start | bytes 24580
  2.4 0.7 %copy-start.6 = (s32[2048,1]{0,1:T(1,128)S(1)}, s32[2048,1]{0,1:T(1,128)}, u32[]{:S(2)}) copy-start(s32[2048,1]{0,1:T(1,128)} %param.12) | copy-start | bytes 24580
  3.1 0.7 %copy-start.7 = (f32[48,8]{0,1:T(8,128)S(1)}, f32[48,8]{0,1:T(8,128)}, u32[]{:S(2)}) copy-start(f32[48,8]{0,1:T(8,128)} %param.14) | copy-start | bytes 4612
  3.8 9.8 %copy-start.1 = (f32[48,2048]{1,0:T(8,128)S(1)}, f32[48,2048]{1,0:T(8,128)}, u32[]{:S(2)}) copy-start(f32[48,2048]{1,0:T(8,128)} %leaf_ref.3) | copy-start | bytes 1179652
  4.4 12.7 %all-to-all-start = ((f32[8,16,128]{2,1,0:T(8,128)}), f32[8,16,128]{2,1,0:T(8,128)S(1)}, u32[]{:S(2)}, u32[]{:S(2)}) async-start(f32[8,16,128]{2,1,0:T(8,128)} %get-tuple-element.14), calls=%async_computation | async-start | bytes 131072 | tf_op jit(solution)/shard_map/all_to_all | solution.py:310
  13.6 3.5 %copy-start.2 = (f32[5,2048]{1,0:T(8,128)S(1)}, f32[5,2048]{1,0:T(8,128)}, u32[]{:S(2)}) copy-start(f32[5,2048]{1,0:T(8,128)} %seas_ref.1) | copy-start | bytes 122884
  18.3 27.0 %copy-start.3 = (f32[48,64]{1,0:T(8,128)S(1)}, f32[48,64]{1,0:T(8,128)}, u32[]{:S(2)}) copy-start(f32[48,64]{1,0:T(8,128)} %base_fine_ref.1) | copy-start | bytes 36868

commit v9 on v8

--- a/solution.py
+++ b/solution.py
@@ -69,11 +69,12 @@
     return jnp.concatenate([row[:, at:at + 128] for at in range(0, row.shape[1], 128)], axis=0)
 
 
-def start_kernel(leaf_ref, fine_ref, mid_ref, top_ref, base_mid_ref, base_top_ref, sums_ref, ids_ref, base_ref):
+def start_kernel(quarter_ref, leaf_ref, fine_ref, mid_ref, top_ref, base_mid_ref, base_top_ref, sums_ref, ids_ref, base_ref):
     sums = dense_of(jnp.sum(leaf_ref[...], axis=0, keepdims=True))
     sums_ref[...] = jnp.broadcast_to(sums[None], sums_ref.shape)
     for at, ref in enumerate((fine_ref, mid_ref, top_ref)):
         ids_ref[at:at + 1, :] = ref[...]
+    ids_ref[3:4, :] = jnp.zeros_like(fine_ref[...]) + quarter_ref[0]
     base_ref[0:8, :] = base_mid_ref[...]
     base_ref[8:9, :] = base_top_ref[...]
 
@@ -93,15 +94,14 @@
     return jnp.concatenate(ranks, axis=1).astype(i32)
 
 
-def sort_kernel(owners, leaf_ref, ids_ref, slots_ref, nodes_ref, places_ref, from_ref):
+def sort_kernel(owners, leaf_ref, ids_ref, base_ref, slots_ref, nodes_ref, places_ref, from_ref, rest_ref):
     days, rows = leaf_ref.shape
     fine, mid, top = (ids_ref[at:at + 1, :] for at in range(3))
     owner = fine >> 6
     rank = ranks_of(owner, owners)
     place = (rank >> 4) * (owners * 16) + owner * 16 + (rank & 15)
     places_ref[0:1, :] = place
-    places_ref[1:2, :] = mid
-    places_ref[2:3, :] = top
+    places_ref[1:4, :] = ids_ref[1:4, :]
 
     leaf = leaf_ref[...]
     high = leaf.astype(bf16).astype(f32)
@@ -131,6 +131,7 @@
     nodes_ref[:, mids:] = tops
     from_ref[0, :, :] = dense_of(slots_ref[LOW + 1:LOW + 2, :]).astype(i32)
     from_ref[1, :, :] = dense_of(slots_ref[LOW + 2:LOW + 3, :]).astype(i32)
+    rest_ref[...] = rest_in_lanes(base_ref[0:8, :], base_ref[8:9, :])
 
 
 def rest_in_lanes(base_mid, base_top):
@@ -154,18 +155,19 @@
     return jnp.where(iota(sums.shape, 0) == LOW, sums - high, high)
 
 
-def send_kernel(quarter_ref, parts_ref, seas_ref, from_ref, slots_ref, nodes_ref, places_ref, pay_ref, shift_ref):
+def send_kernel(parts_ref, seas_ref, from_ref, slots_ref, nodes_ref, places_ref, pay_ref, shift_ref):
     owners = pay_ref.shape[0]
     rows = places_ref.shape[1]
     slots, mids = owners * 16, owners * 8
     days = slots_ref.shape[0] - 8
     season_days = days * 2
     parts = parts_ref[...]
-    own = jnp.sum(jnp.where(iota(parts.shape, 0) >> 1 == quarter_ref[0], parts, 0.0), axis=0)
+    quarter = places_ref[3:4, 0:128]
+    own = jnp.sum(jnp.where(iota(parts.shape, 0) >> 1 == quarter[None], parts, 0.0), axis=0)
     total = jnp.sum(parts, axis=0)
     seas = seas_ref[...]
     line = iota(seas.shape, 0)
-    seas_own = jnp.sum(jnp.where(line == quarter_ref[0], seas, 0.0), axis=0, keepdims=True)
+    seas_own = jnp.sum(jnp.where(line == places_ref[3:4, :], seas, 0.0), axis=0, keepdims=True)
     seas_four = jnp.sum(jnp.where(line < 4, seas, 0.0), axis=0, keepdims=True)
     known = dense_of(0.5 * seas_own / season_days + 0.5 * (seas[4:5, :] - 0.5 * seas_four) / (season_days * 4))
     shift = known - (0.5 * own / season_days + 0.25 * total / (season_days * 4))
@@ -227,7 +229,7 @@
         pay_ref[g * group:(g + 1) * group, :, :] = (tile.reshape(group, 16, 128) + extra).astype(bf16)
 
 
-def owner_kernel(got_ref, base_fine_ref, base_ref, back_ref):
+def owner_kernel(got_ref, base_fine_ref, base_rest_ref, back_ref):
     owners = got_ref.shape[0]
     days, nodes = base_fine_ref.shape
     got = got_ref[...].astype(f32)
@@ -247,12 +249,12 @@
     pair = rest + jnp.concatenate([rest[8:16, :], rest[0:8, :]], axis=0)
     of_top = iota(rest.shape, 1) > MID_COUNT
     count = jnp.where(of_top, pair[:, TOP_COUNT:TOP_COUNT + 1], pair[:, MID_COUNT:MID_COUNT + 1])
-    gap_rest = jnp.where(slot_lanes(rest.shape, 1), 0.0, (rest_in_lanes(base_ref[0:8, :], base_ref[8:9, :]) - rest) / (count + 1.0))
+    gap_rest = jnp.where(slot_lanes(rest.shape, 1), 0.0, (base_rest_ref[...] - rest) / (count + 1.0))
     spread = jnp.where(slot_lanes(flat.shape, 1), spread, 0.0).reshape(owners, 16, 128)
     back_ref[...] = (spread + gap_rest[None]).astype(bf16)
 
 
-def finish_kernel(leaf_ref, shift_ref, places_ref, back_ref, out_ref):
+def finish_kernel(leaf_ref, shift_ref, places_ref, back_ref, out_ref, done_ref, sems):
     days, rows = leaf_ref.shape
     owners = back_ref.shape[0]
     slots, mids = owners * 16, owners * 8
@@ -273,6 +275,7 @@
     node_gaps = [jnp.concatenate([mid[:, g * width:(g + 1) * width], tops], axis=1) for g in range(mid_count)]
     node_gaps = jnp.concatenate(node_gaps, axis=0).astype(bf16)
     step = min(512, rows)
+    copies = []
     for at in range(0, rows, step):
         place, mid, top = (places_ref[k:k + 1, at:at + step] for k in range(3))
         out = leaf_ref[:, at:at + step] + shift_ref[:, at:at + step]
@@ -285,7 +288,11 @@
             for g in range(1, count):
                 chosen = jnp.where(group == g, found[g * days:(g + 1) * days, :], chosen)
             out = out + chosen
-        out_ref[:, at:at + step] = out
+        done_ref[:, at:at + step] = out
+        copies.append(pltpu.make_async_copy(done_ref.at[:, at:at + step], out_ref.at[:, at:at + step], sems.at[at // step]))
+        copies[-1].start()
+    for copy in copies:
+        copy.wait()
 
 
 def per_device(leaf, seas, fine, mid, top, base_fine, base_mid, base_top):
@@ -301,44 +308,48 @@
         start_kernel,
         out_shape=(
             jax.ShapeDtypeStruct((blocks,) + dense, f32),
-            jax.ShapeDtypeStruct((3, rows), i32),
+            jax.ShapeDtypeStruct((4, rows), i32),
             jax.ShapeDtypeStruct((16, days), f32),
         ),
+        in_specs=[smem] + [vmem] * 6,
         compiler_params=PARAMS,
         name="start",
-    )(leaf, *(ids.reshape(1, rows) for ids in (fine, mid, top)), base_mid.T, base_top.reshape(1, days))
+    )(quarter, leaf, *(ids.reshape(1, rows) for ids in (fine, mid, top)), base_mid.T, base_top.reshape(1, days))
     parts = lax.all_to_all(sums, "tm", 0, 0, tiled=True)
-    slots, nodes, places, come_from = pl.pallas_call(
+    slots, nodes, places, come_from, base_rest = pl.pallas_call(
         lambda *refs: sort_kernel(owners, *refs),
         out_shape=(
             jax.ShapeDtypeStruct((days + 8, rows), f32),
             jax.ShapeDtypeStruct((days + 8, owners * 8 + TOP_ROWS), f32),
-            jax.ShapeDtypeStruct((3, rows), i32),
+            jax.ShapeDtypeStruct((4, rows), i32),
             jax.ShapeDtypeStruct((2,) + dense, i32),
+            jax.ShapeDtypeStruct((16, 128), f32),
         ),
         compiler_params=PARAMS,
         cost_estimate=pl.CostEstimate(flops=2 * 104 * owners * 42 * rows, bytes_accessed=4 * days * rows, transcendentals=0),
         name="sort",
-    )(leaf, ids)
+    )(leaf, ids, base)
 
     payload, shift = pl.pallas_call(
         send_kernel,
         out_shape=(jax.ShapeDtypeStruct((owners, 16, 128), bf16), jax.ShapeDtypeStruct((1, rows), f32)),
-        in_specs=[smem] + [vmem] * 6,
         compiler_params=PARAMS,
         name="pack",
-    )(quarter, parts, seas, come_from, slots, nodes, places)
+    )(parts, seas, come_from, slots, nodes, places)
     got = lax.all_to_all(payload, "series", 0, 0, tiled=True)
     back = pl.pallas_call(
         owner_kernel,
         out_shape=jax.ShapeDtypeStruct((owners, 16, 128), bf16),
         compiler_params=PARAMS,
         name="gaps",
-    )(got, base_fine, base)
+    )(got, base_fine, base_rest)
     back = lax.all_to_all(back, "series", 0, 0, tiled=True)
     return pl.pallas_call(
         finish_kernel,
         out_shape=jax.ShapeDtypeStruct((days, rows), f32),
+        in_specs=[vmem] * 4,
+        out_specs=pl.BlockSpec(memory_space=pl.ANY),
+        scratch_shapes=[pltpu.VMEM((days, rows), f32), pltpu.SemaphoreType.DMA((max(1, rows // 512),))],
         compiler_params=PARAMS,
         name="finish",
     )(leaf, shift, places, back)

time: 67.7 us -> 65.4 us (0.966)
  local copies, waits for them, and re-layouts: 3.79 us -> 1.73 us
    unnamed x18, local copies, waits for them, and re-layouts: 3.79 us -> 1.73 us
where the time goes in v9:
time: 65.4 us; the launch traced here: 64.4 us
  blocking collectives  45.4 us (69%)
  starting transfers between devices  9.14 us (14%)
  Pallas kernels  6.52 us (10%)
  local copies, waits for them, and re-layouts  1.73 us (3%)
  waiting for transfers between devices  1.55 us (2%)
    all_to_all x1, blocking collectives, per_device(): got = lax.all_to_all(payload, 'series', 0, 0, tiled=True)  27 us
    all_to_all x1, blocking collectives, per_device(): back = lax.all_to_all(back, 'series', 0, 0, tiled=True)  18.4 us
    all_to_all x1, starting transfers between devices, per_device(): parts = lax.all_to_all(sums, 'tm', 0, 0, tiled=True)  9.14 us
    pallas_call x1, Pallas kernels, per_device(): pl.pallas_call(lambda *refs: sort_kernel(owners, *refs), out_shape=(jax.S...  1.97 us
    pallas_call x1, Pallas kernels, per_device(): pl.pallas_call(finish_kernel, out_shape=jax.ShapeDtypeStruct((days, rows)...  1.83 us
    unnamed x18, local copies, waits for them, and re-layouts  1.73 us
    all_to_all x1, waiting for transfers between devices, per_device(): parts = lax.all_to_all(sums, 'tm', 0, 0, tiled=True)  1.55 us
  transfers between devices with their start and end apart: 1, of which 1 were waited for; matrix products, arithmetic and copies ran while one was open for 0% of the time, Pallas kernels for 3%

profile of v9, /device:TPU:6, one launch (start us, length us, event | category | flops | bytes accessed | tf_op | source)
XLA Modules:
  0.0 64.4 jit_solution(16174106606966404434)
XLA Ops:
  0.0 0.0 copy-start.7
  0.0 0.0 copy-start.6
  0.0 0.0 copy-start.5
  0.0 0.0 copy-start.4
  0.0 0.0 copy-start.8
  0.0 0.7 %copy-done.7 = f32[48,8]{0,1:T(8,128)S(1)} copy-done((f32[48,8]{0,1:T(8,128)S(1)}, f32[48,8]{0,1:T(8,128)}, u32[]{:S(2)}) %copy-start.7) | copy-done | bytes 1560
  0.7 0.0 copy-done.6
  0.7 0.0 copy-done.5
  0.7 0.0 copy-done.4
  0.7 0.0 copy-done.8
  0.7 0.0 copy-start
  0.8 1.0 %copy-done = f32[48,2048]{1,0:T(8,128)S(1)} copy-done((f32[48,2048]{1,0:T(8,128)S(1)}, f32[48,2048]{1,0:T(8,128)}, u32[]{:S(2)}) %copy-start) | copy-done | bytes 393240
  1.7 0.0 copy-start.1
  1.7 0.7 %start.1 = (f32[8,16,128]{2,1,0:T(8,128)}, s32[4,2048]{1,0:T(4,128)S(1)}, f32[16,48]{1,0:T(8,128)S(1)}) custom-call(s32[1]{0:T(128)} %bitcast.quarter_ref, f32[48,2048]{1,0:T(8,128)S(1)} %copy-done, s32[1,2048]{1,0:T(1,128)S(1)} %bitcast.6, s32[1,2048]{1,0:T(1,128)S(1)} %bitcast.7, s32[1,2048]{1,0:T(1,128)S(1)} %bitcast.8, f32[8,48]{1,0:T(8,128)S(1)} %bitcast.9, ...), custom_call_target="tpu_custom_call" | custom-call | tf_op jit(solution)/shard_map/start/pallas_call | solution.py:307
  2.4 9.1 %all-to-all-start = ((f32[8,16,128]{2,1,0:T(8,128)}), f32[8,16,128]{2,1,0:T(8,128)S(1)}, u32[]{:S(2)}, u32[]{:S(2)}) async-start(f32[8,16,128]{2,1,0:T(8,128)} %get-tuple-element.15), calls=%async_computation | async-start | bytes 131072 | tf_op jit(solution)/shard_map/all_to_all | solution.py:318
  11.6 0.0 copy-done.1
  11.6 0.0 copy-start.2
  11.6 2.0 %sort.1 = (f32[56,2048]{1,0:T(8,128)S(1)}, f32[56,640]{1,0:T(8,128)S(1)}, s32[4,2048]{1,0:T(4,128)S(1)}, s32[2,16,128]{2,1,0:T(8,128)S(1)}, f32[16,128]{1,0:T(8,128)S(1)}) custom-call(f32[48,2048]{1,0:T(8,128)S(1)} %copy-done.1, s32[4,2048]{1,0:T(4,128)S(1)} %get-tuple-element.16.refs_1_, f32[16,48]{1,0:T(8,128)S(1)} %get-tuple-element.17.refs_2_), custom_call_target="tpu_custom_call" | custom-call | flops 1145044992 | bytes 393216 | tf_op jit(solution)/shard_map/sort/pallas_call | solution.py:319
  13.5 1.6 %all-to-all-done.parts_ref = f32[8,16,128]{2,1,0:T(8,128)S(1)} async-done(((f32[8,16,128]{2,1,0:T(8,128)}), f32[8,16,128]{2,1,0:T(8,128)S(1)}, u32[]{:S(2)}, u32[]{:S(2)}) %all-to-all-start) | async-done | bytes 65568 | tf_op jit(solution)/shard_map/all_to_all | solution.py:318
  15.1 0.0 copy-done.2
  15.1 1.2 %pack.1 = (bf16[64,16,128]{2,1,0:T(8,128)(2,1)S(1)}, f32[1,2048]{1,0:T(1,128)S(1)}) custom-call(f32[8,16,128]{2,1,0:T(8,128)S(1)} %all-to-all-done.parts_ref, f32[5,2048]{1,0:T(8,128)S(1)} %copy-done.2, s32[2,16,128]{2,1,0:T(8,128)S(1)} %get-tuple-element.18.from_ref, f32[56,2048]{1,0:T(8,128)S(1)} %get-tuple-element.19.slots_ref, ...), custom_call_target="tpu_custom_call" | custom-call | tf_op jit(solution)/shard_map/pack/pallas_call | solution.py:333
  16.3 0.0 copy-start.3
  16.3 27.0 %all_to_all.15.got_ref = bf16[64,16,128]{2,1,0:T(8,128)(2,1)S(1)} all-to-all(bf16[64,16,128]{2,1,0:T(8,128)(2,1)S(1)} %get-tuple-element.23), channel_id=1, replica_groups=mesh['tm'=8,'series'=64] {'series'}, dimensions={0} | all-to-all | bytes 524288 | tf_op jit(solution)/shard_map/all_to_all | solution.py:339
  43.3 0.0 copy-done.3
  43.3 0.8 %gaps.1 = bf16[64,16,128]{2,1,0:T(8,128)(2,1)S(1)} custom-call(bf16[64,16,128]{2,1,0:T(8,128)(2,1)S(1)} %all_to_all.15.got_ref, f32[48,64]{1,0:T(8,128)S(1)} %copy-done.3, f32[16,128]{1,0:T(8,128)S(1)} %get-tuple-element.24.base_rest_ref), custom_call_target="tpu_custom_call" | custom-call | tf_op jit(solution)/shard_map/gaps/pallas_call | solution.py:340
  44.1 18.4 %all_to_all.16.back_ref = bf16[64,16,128]{2,1,0:T(8,128)(2,1)S(1)} all-to-all(bf16[64,16,128]{2,1,0:T(8,128)(2,1)S(1)} %gaps.1), channel_id=1, replica_groups=mesh['tm'=8,'series'=64] {'series'}, dimensions={0} | all-to-all | bytes 524288 | tf_op jit(solution)/shard_map/all_to_all | solution.py:346
  62.5 1.8 %finish.1 = f32[48,2048]{1,0:T(8,128)} custom-call(f32[48,2048]{1,0:T(8,128)S(1)} %copy-done.1, f32[1,2048]{1,0:T(1,128)S(1)} %get-tuple-element.22.shift_ref, s32[4,2048]{1,0:T(4,128)S(1)} %get-tuple-element.21.places_ref, bf16[64,16,128]{2,1,0:T(8,128)(2,1)S(1)} %all_to_all.16.back_ref), custom_call_target="tpu_custom_call" | custom-call | tf_op jit(solution)/shard_map/finish/pallas_call | solution.py:347
Async XLA Ops:
  0.0 0.7 %copy-start.7 = (f32[48,8]{0,1:T(8,128)S(1)}, f32[48,8]{0,1:T(8,128)}, u32[]{:S(2)}) copy-start(f32[48,8]{0,1:T(8,128)} %param.14) | copy-start | bytes 4612
  0.0 0.7 %copy-start.6 = (s32[2048,1]{0,1:T(1,128)S(1)}, s32[2048,1]{0,1:T(1,128)}, u32[]{:S(2)}) copy-start(s32[2048,1]{0,1:T(1,128)} %param.12) | copy-start | bytes 24580
  0.0 0.7 %copy-start.5 = (s32[2048,1]{0,1:T(1,128)S(1)}, s32[2048,1]{0,1:T(1,128)}, u32[]{:S(2)}) copy-start(s32[2048,1]{0,1:T(1,128)} %param.11) | copy-start | bytes 24580
  0.0 0.7 %copy-start.4 = (s32[2048,1]{0,1:T(1,128)S(1)}, s32[2048,1]{0,1:T(1,128)}, u32[]{:S(2)}) copy-start(s32[2048,1]{0,1:T(1,128)} %param.10) | copy-start | bytes 24580
  0.0 0.7 %copy-start.8 = (f32[48,1]{0,1:T(1,128)S(1)}, f32[48,1]{0,1:T(1,128)}, u32[]{:S(2)}) copy-start(f32[48,1]{0,1:T(1,128)} %param.15) | copy-start | bytes 580
  0.7 1.0 %copy-start = (f32[48,2048]{1,0:T(8,128)S(1)}, f32[48,2048]{1,0:T(8,128)}, u32[]{:S(2)}) copy-start(f32[48,2048]{1,0:T(8,128)} %leaf_ref.3) | copy-start | bytes 1179652
  1.7 9.8 %copy-start.1 = (f32[48,2048]{1,0:T(8,128)S(1)}, f32[48,2048]{1,0:T(8,128)}, u32[]{:S(2)}) copy-start(f32[48,2048]{1,0:T(8,128)} %leaf_ref.3) | copy-start | bytes 1179652
  2.4 12.7 %all-to-all-start = ((f32[8,16,128]{2,1,0:T(8,128)}), f32[8,16,128]{2,1,0:T(8,128)S(1)}, u32[]{:S(2)}, u32[]{:S(2)}) async-start(f32[8,16,128]{2,1,0:T(8,128)} %get-tuple-element.15), calls=%async_computation | async-start | bytes 131072 | tf_op jit(solution)/shard_map/all_to_all | solution.py:318
  11.6 3.5 %copy-start.2 = (f32[5,2048]{1,0:T(8,128)S(1)}, f32[5,2048]{1,0:T(8,128)}, u32[]{:S(2)}) copy-start(f32[5,2048]{1,0:T(8,128)} %seas_ref.1) | copy-start | bytes 122884
  16.3 27.0 %copy-start.3 = (f32[48,64]{1,0:T(8,128)S(1)}, f32[48,64]{1,0:T(8,128)}, u32[]{:S(2)}) copy-start(f32[48,64]{1,0:T(8,128)} %base_fine_ref.1) | copy-start | bytes 36868

commit v10 on v9

--- a/solution.py
+++ b/solution.py
@@ -57,6 +57,16 @@
     return lax.dot_general(a, b, (((1,), (1,)), ((), ())), precision=precision, preferred_element_type=f32)
 
 
+def dot_tn(a, b):
+    return lax.dot_general(a, b, (((0,), (0,)), ((), ())), preferred_element_type=f32)
+
+
+def spread_row(row, lanes):
+    high = row.astype(bf16).astype(f32)
+    parts = jnp.concatenate([high, row - high, jnp.zeros((14, row.shape[1]), f32)], axis=0).astype(bf16)
+    return dot_tn(parts, ones_where(lanes & (iota(lanes.shape, 0) < 2)))
+
+
 def slot_lanes(shape, dim):
     return (iota(shape, dim) & 63) <= ID
 
@@ -69,14 +79,9 @@
     return jnp.concatenate([row[:, at:at + 128] for at in range(0, row.shape[1], 128)], axis=0)
 
 
-def start_kernel(quarter_ref, leaf_ref, fine_ref, mid_ref, top_ref, base_mid_ref, base_top_ref, sums_ref, ids_ref, base_ref):
+def start_kernel(leaf_ref, sums_ref):
     sums = dense_of(jnp.sum(leaf_ref[...], axis=0, keepdims=True))
     sums_ref[...] = jnp.broadcast_to(sums[None], sums_ref.shape)
-    for at, ref in enumerate((fine_ref, mid_ref, top_ref)):
-        ids_ref[at:at + 1, :] = ref[...]
-    ids_ref[3:4, :] = jnp.zeros_like(fine_ref[...]) + quarter_ref[0]
-    base_ref[0:8, :] = base_mid_ref[...]
-    base_ref[8:9, :] = base_top_ref[...]
 
 
 def ranks_of(owner, owners):
@@ -94,14 +99,19 @@
     return jnp.concatenate(ranks, axis=1).astype(i32)
 
 
-def sort_kernel(owners, leaf_ref, ids_ref, base_ref, slots_ref, nodes_ref, places_ref, from_ref, rest_ref):
+def sort_kernel(
+    owners, quarter_ref, fine_ref, mid_ref, top_ref, base_mid_ref, base_top_ref, leaf_ref,
+    tiles_ref, mids_ref, tops_ref, places_ref, from_ref, rest_ref,
+):
     days, rows = leaf_ref.shape
-    fine, mid, top = (ids_ref[at:at + 1, :] for at in range(3))
+    fine, mid, top = fine_ref[...], mid_ref[...], top_ref[...]
     owner = fine >> 6
     rank = ranks_of(owner, owners)
     place = (rank >> 4) * (owners * 16) + owner * 16 + (rank & 15)
     places_ref[0:1, :] = place
-    places_ref[1:4, :] = ids_ref[1:4, :]
+    places_ref[1:2, :] = mid
+    places_ref[2:3, :] = top
+    places_ref[3:4, :] = jnp.zeros_like(mid) + quarter_ref[0]
 
     leaf = leaf_ref[...]
     high = leaf.astype(bf16).astype(f32)
@@ -115,23 +125,30 @@
     def add_low(part):
         return part[:height, :] + jnp.concatenate([part[height:height + days, :], jnp.zeros((8, part.shape[1]), f32)], axis=0)
 
+    def turned(part):
+        part = jnp.concatenate([part, jnp.zeros((64 - height, part.shape[1]), f32)], axis=0)
+        step = min(128, part.shape[1])
+        return jnp.concatenate([jnp.transpose(part[:, at:at + step]) for at in range(0, part.shape[1], step)], axis=0)
+
     count = rows // 256
+    half = rows // 2
     sums = dot_nt(by_group(ext, place >> 8, count), hits(place & 255, 256))
-    for g in range(count):
-        slots_ref[:, g * 256:(g + 1) * 256] = add_low(sums[g * 2 * height:(g + 1) * 2 * height, :])
+    sums = jnp.concatenate([add_low(sums[g * 2 * height:(g + 1) * 2 * height, :]) for g in range(count)], axis=1)
+    pad = jnp.zeros((64 - height, rows), f32)
+    both = jnp.concatenate([sums, pad], axis=0)
+    both = jnp.concatenate([both[:, :half], both[:, half:]], axis=0)
+    tiles_ref[...] = jnp.concatenate([jnp.transpose(both[:, at:at + 128]) for at in range(0, half, 128)], axis=0)
+    from_ref[0, :, :] = dense_of(sums[LOW + 1:LOW + 2, :]).astype(i32)
+    from_ref[1, :, :] = dense_of(sums[LOW + 2:LOW + 3, :]).astype(i32)
+
     mids = owners * 8
     width = min(128, mids)
     count = mids // width
     sums = dot_nt(by_group(ext, mid // width, count), node_hits(mid, top, width))
-    tops = jnp.zeros((height, TOP_ROWS), f32)
-    for g in range(count):
-        part = add_low(sums[g * 2 * height:(g + 1) * 2 * height, :])
-        nodes_ref[:, g * width:(g + 1) * width] = part[:, :width]
-        tops = tops + part[:, width:]
-    nodes_ref[:, mids:] = tops
-    from_ref[0, :, :] = dense_of(slots_ref[LOW + 1:LOW + 2, :]).astype(i32)
-    from_ref[1, :, :] = dense_of(slots_ref[LOW + 2:LOW + 3, :]).astype(i32)
-    rest_ref[...] = rest_in_lanes(base_ref[0:8, :], base_ref[8:9, :])
+    sums = [add_low(sums[g * 2 * height:(g + 1) * 2 * height, :]) for g in range(count)]
+    mids_ref[...] = turned(jnp.concatenate([part[:, :width] for part in sums], axis=1))
+    tops_ref[...] = turned(sum(part[:, width:] for part in sums))
+    rest_ref[...] = rest_in_lanes(base_mid_ref[...], base_top_ref[...])
 
 
 def rest_in_lanes(base_mid, base_top):
@@ -152,14 +169,14 @@
 
 def split_count(sums):
     high = sums.astype(bf16).astype(f32)
-    return jnp.where(iota(sums.shape, 0) == LOW, sums - high, high)
-
-
-def send_kernel(parts_ref, seas_ref, from_ref, slots_ref, nodes_ref, places_ref, pay_ref, shift_ref):
+    return jnp.where(iota(sums.shape, 1) == LOW, sums - high, high).astype(bf16)
+
+
+def send_kernel(parts_ref, seas_ref, from_ref, tiles_ref, mids_ref, tops_ref, places_ref, pay_ref, shift_ref):
     owners = pay_ref.shape[0]
     rows = places_ref.shape[1]
     slots, mids = owners * 16, owners * 8
-    days = slots_ref.shape[0] - 8
+    days = 48
     season_days = days * 2
     parts = parts_ref[...]
     quarter = places_ref[3:4, 0:128]
@@ -190,43 +207,29 @@
     count = mids // width
     found = dot_nt(by_group(ext, mid // width, count), node_hits(mid, top, width))
     found = [jnp.sum(found[g * 16:(g + 1) * 16, :], axis=0, keepdims=True) for g in range(count)]
-    node_sums = jnp.concatenate([part[:, :width] for part in found] + [sum(part[:, width:] for part in found)], axis=1)
-    is_day = iota((days + 8, 1), 0) < days
-    pad = jnp.zeros((8, rows + mids + TOP_ROWS), f32)
-    sums = jnp.concatenate([slots_ref[...], nodes_ref[...]], axis=1)
-    sums = sums + jnp.where(is_day, jnp.concatenate([moved, node_sums], axis=1), 0.0)
-    sums = jnp.concatenate([sums, pad], axis=0)
-
-    tops = split_count(sums[:, 2 * slots + mids:]).astype(bf16)
-    tops = dot(tops, ones_where(iota((TOP_ROWS, slots), 0) == iota((TOP_ROWS, slots), 1) >> 4))
-    row, column = iota((64, slots), 0), iota((64, slots), 1) & 15
-    keep = (
-        ((row < days) & (row // 3 == column))
-        | ((row == ONE) & (column < 8))
-        | ((row == LOW) & (column >= 8))
-    )
-    tops = jnp.where(keep, tops, 0.0).astype(bf16)
-    lane, day = iota((128, 64), 0), iota((128, 64), 1)
-    top_move = ((day < days) & (lane == top_lane(day))) | (((day == ONE) | (day == LOW)) & (lane == TOP_COUNT))
-    tops = dot(ones_where(top_move), tops)
-    tiles = jnp.concatenate([sums[:, :slots], sums[:, slots:2 * slots]], axis=0)
-    tiles = jnp.where(slot_lanes((128, slots), 0), tiles, tops)
-
+    lane = iota((16, 128), 1)
+    is_day = iota((16, 64), 1) < days
+    mid_sums = mids_ref[...] + spread_row(jnp.concatenate([part[:, :width] for part in found], axis=1), is_day)
+    top_sums = tops_ref[...] + spread_row(sum(part[:, width:] for part in found), is_day)
+    tiles = tiles_ref[...] + spread_row(moved[:, :slots], lane < days)
+    tiles = tiles + spread_row(moved[:, slots:], (lane >= 64) & (lane < 64 + days))
+
+    row, day = iota((slots, 64), 0) & 15, iota((slots, 64), 1)
+    keep = ((day < days) & (day // 3 == row)) | ((day == ONE) & (row < 8)) | ((day == LOW) & (row >= 8))
+    owner = ones_where(iota((slots, TOP_ROWS), 0) >> 4 == iota((slots, TOP_ROWS), 1))
+    top = jnp.where(keep, dot(owner, split_count(top_sums)), 0.0).astype(bf16)
     half = days // 2
-    mid_sums = split_count(sums[:, 2 * slots:2 * slots + mids])
     day, lane = iota((64, 128), 0), iota((64, 128), 1)
     moves = (
         ((day < half) & (lane == lane_of(day))) | ((day == ONE) & (lane == MID_COUNT)),
         ((day >= half) & (day < days) & (lane == lane_of(day - half))) | ((day == LOW) & (lane == MID_COUNT)),
+        ((day < days) & (lane == top_lane(day))) | (((day == ONE) | (day == LOW)) & (lane == TOP_COUNT)),
     )
     moves = [ones_where(move) for move in moves]
-    group = min(16, owners)
-    for g in range(owners // group):
-        own = jnp.transpose(mid_sums[:, g * group * 8:(g + 1) * group * 8]).astype(bf16)
-        extra = jnp.concatenate([dot(own, move).reshape(group, 8, 128) for move in moves], axis=1)
-        start, stop = g * group * 16, (g + 1) * group * 16
-        tile = jnp.concatenate([jnp.transpose(tiles[:, at:at + 128]) for at in range(start, stop, 128)], axis=0)
-        pay_ref[g * group:(g + 1) * group, :, :] = (tile.reshape(group, 16, 128) + extra).astype(bf16)
+    own = split_count(mid_sums)
+    extra = jnp.concatenate([dot(own, move).reshape(owners, 8, 128) for move in moves[:2]], axis=1)
+    tiles = jnp.where(slot_lanes((slots, 128), 1), tiles, dot(top, moves[2]))
+    pay_ref[...] = (tiles.reshape(owners, 16, 128) + extra).astype(bf16)
 
 
 def owner_kernel(got_ref, base_fine_ref, base_rest_ref, back_ref):
@@ -304,38 +307,32 @@
     smem = pl.BlockSpec(memory_space=pltpu.SMEM)
     dense = (rows // 128, 128)
 
-    sums, ids, base = pl.pallas_call(
-        start_kernel,
-        out_shape=(
-            jax.ShapeDtypeStruct((blocks,) + dense, f32),
-            jax.ShapeDtypeStruct((4, rows), i32),
-            jax.ShapeDtypeStruct((16, days), f32),
-        ),
-        in_specs=[smem] + [vmem] * 6,
-        compiler_params=PARAMS,
-        name="start",
-    )(quarter, leaf, *(ids.reshape(1, rows) for ids in (fine, mid, top)), base_mid.T, base_top.reshape(1, days))
+    sums = pl.pallas_call(
+        start_kernel, out_shape=jax.ShapeDtypeStruct((blocks,) + dense, f32), compiler_params=PARAMS, name="day_sums"
+    )(leaf)
     parts = lax.all_to_all(sums, "tm", 0, 0, tiled=True)
-    slots, nodes, places, come_from, base_rest = pl.pallas_call(
+    tiles, mids, tops, places, come_from, base_rest = pl.pallas_call(
         lambda *refs: sort_kernel(owners, *refs),
         out_shape=(
-            jax.ShapeDtypeStruct((days + 8, rows), f32),
-            jax.ShapeDtypeStruct((days + 8, owners * 8 + TOP_ROWS), f32),
+            jax.ShapeDtypeStruct((owners * 16, 128), f32),
+            jax.ShapeDtypeStruct((owners * 8, 64), f32),
+            jax.ShapeDtypeStruct((TOP_ROWS, 64), f32),
             jax.ShapeDtypeStruct((4, rows), i32),
             jax.ShapeDtypeStruct((2,) + dense, i32),
             jax.ShapeDtypeStruct((16, 128), f32),
         ),
+        in_specs=[smem] + [vmem] * 6,
         compiler_params=PARAMS,
         cost_estimate=pl.CostEstimate(flops=2 * 104 * owners * 42 * rows, bytes_accessed=4 * days * rows, transcendentals=0),
         name="sort",
-    )(leaf, ids, base)
+    )(quarter, *(ids.reshape(1, rows) for ids in (fine, mid, top)), base_mid.T, base_top.reshape(1, days), leaf)
 
     payload, shift = pl.pallas_call(
         send_kernel,
         out_shape=(jax.ShapeDtypeStruct((owners, 16, 128), bf16), jax.ShapeDtypeStruct((1, rows), f32)),
         compiler_params=PARAMS,
         name="pack",
-    )(parts, seas, come_from, slots, nodes, places)
+    )(parts, seas, come_from, tiles, mids, tops, places)
     got = lax.all_to_all(payload, "series", 0, 0, tiled=True)
     back = pl.pallas_call(
         owner_kernel,

time: 65.4 us -> 65.2 us (level)
  waiting for transfers between devices: 1.55 us -> 0.67 us
  Pallas kernels: 6.52 us -> 7.19 us
    all_to_all x1, waiting for transfers between devices: 1.55 us -> 0.67 us  [per_device(): parts = lax.all_to_all(sums, 'tm', 0, 0, tiled=True)]
where the time goes in v10:
time: 65.2 us; the launch traced here: 64.1 us
  blocking collectives  45.4 us (70%)
  starting transfers between devices  9.14 us (14%)
  Pallas kernels  7.19 us (11%)
  local copies, waits for them, and re-layouts  1.72 us (3%)
  waiting for transfers between devices  0.67 us (1%)
    all_to_all x1, blocking collectives, per_device(): got = lax.all_to_all(payload, 'series', 0, 0, tiled=True)  27 us
    all_to_all x1, blocking collectives, per_device(): back = lax.all_to_all(back, 'series', 0, 0, tiled=True)  18.4 us
    all_to_all x1, starting transfers between devices, per_device(): parts = lax.all_to_all(sums, 'tm', 0, 0, tiled=True)  9.14 us
    pallas_call x1, Pallas kernels, per_device(): pl.pallas_call(lambda *refs: sort_kernel(owners, *refs), out_shape=(jax.S...  2.11 us
    pallas_call x1, Pallas kernels, per_device(): pl.pallas_call(finish_kernel, out_shape=jax.ShapeDtypeStruct((days, rows)...  1.83 us
    pallas_call x1, Pallas kernels, per_device(): pl.pallas_call(send_kernel, out_shape=(jax.ShapeDtypeStruct((owners, 16,...  1.76 us
    unnamed x18, local copies, waits for them, and re-layouts  1.72 us
  transfers between devices with their start and end apart: 1, of which 1 were waited for; matrix products, arithmetic and copies ran while one was open for 0% of the time, Pallas kernels for 3%

profile of v10, /device:TPU:6, one launch (start us, length us, event | category | flops | bytes accessed | tf_op | source)
XLA Modules:
  0.0 64.1 jit_solution(7788480593310259409)
XLA Ops:
  0.0 0.0 copy-start
  0.0 1.0 %copy-done = f32[48,2048]{1,0:T(8,128)S(1)} copy-done((f32[48,2048]{1,0:T(8,128)S(1)}, f32[48,2048]{1,0:T(8,128)}, u32[]{:S(2)}) %copy-start) | copy-done | bytes 393240
  1.0 0.0 copy-start.1
  1.0 0.7 %day_sums.1 = f32[8,16,128]{2,1,0:T(8,128)} custom-call(f32[48,2048]{1,0:T(8,128)S(1)} %copy-done), custom_call_target="tpu_custom_call" | custom-call | tf_op jit(solution)/shard_map/day_sums/pallas_call | solution.py:310
  1.7 9.1 %all-to-all-start = ((f32[8,16,128]{2,1,0:T(8,128)}), f32[8,16,128]{2,1,0:T(8,128)S(1)}, u32[]{:S(2)}, u32[]{:S(2)}) async-start(f32[8,16,128]{2,1,0:T(8,128)} %day_sums.1), calls=%async_computation | async-start | bytes 131072 | tf_op jit(solution)/shard_map/all_to_all | solution.py:313
  10.8 0.0 copy-start.6
  10.8 0.0 copy-start.7
  10.8 0.0 copy-start.5
  10.8 0.0 copy-start.4
  10.8 0.0 copy-start.8
  10.8 0.0 copy-done.1
  10.9 0.6 %copy-done.6 = s32[2048,1]{0,1:T(1,128)S(1)} copy-done((s32[2048,1]{0,1:T(1,128)S(1)}, s32[2048,1]{0,1:T(1,128)}, u32[]{:S(2)}) %copy-start.6) | copy-done | bytes 8216
  11.5 0.0 copy-done.7
  11.5 0.0 copy-done.5
  11.5 0.0 copy-done.4
  11.5 0.0 copy-done.8
  11.6 0.0 copy-start.2
  11.6 2.1 %sort.1 = (f32[1024,128]{1,0:T(8,128)S(1)}, f32[512,64]{1,0:T(8,128)S(1)}, f32[128,64]{1,0:T(8,128)S(1)}, s32[4,2048]{1,0:T(4,128)S(1)}, s32[2,16,128]{2,1,0:T(8,128)S(1)}, /*index=5*/f32[16,128]{1,0:T(8,128)S(1)}) custom-call(s32[1]{0:T(128)} %bitcast.refs_0_, s32[1,2048]{1,0:T(1,128)S(1)} %bitcast.6, s32[1,2048]{1,0:T(1,128)S(1)} %bitcast.7, ...), custom_call_target="tpu_custom_call" | custom-call | flops 1145044992 | bytes 393216 | tf_op jit(solution)/shard_map/sort/pallas_call | solution.py:314
  13.7 0.7 %all-to-all-done.parts_ref = f32[8,16,128]{2,1,0:T(8,128)S(1)} async-done(((f32[8,16,128]{2,1,0:T(8,128)}), f32[8,16,128]{2,1,0:T(8,128)S(1)}, u32[]{:S(2)}, u32[]{:S(2)}) %all-to-all-start) | async-done | bytes 65568 | tf_op jit(solution)/shard_map/all_to_all | solution.py:313
  14.3 0.0 copy-done.2
  14.3 1.8 %pack.1 = (bf16[64,16,128]{2,1,0:T(8,128)(2,1)S(1)}, f32[1,2048]{1,0:T(1,128)S(1)}) custom-call(f32[8,16,128]{2,1,0:T(8,128)S(1)} %all-to-all-done.parts_ref, f32[5,2048]{1,0:T(8,128)S(1)} %copy-done.2, s32[2,16,128]{2,1,0:T(8,128)S(1)} %get-tuple-element.13.from_ref, f32[1024,128]{1,0:T(8,128)S(1)} %get-tuple-element.14.tiles_ref, ...), custom_call_target="tpu_custom_call" | custom-call | tf_op jit(solution)/shard_map/pack/pallas_call | solution.py:330
  16.1 0.0 copy-start.3
  16.1 27.0 %all_to_all.15.got_ref = bf16[64,16,128]{2,1,0:T(8,128)(2,1)S(1)} all-to-all(bf16[64,16,128]{2,1,0:T(8,128)(2,1)S(1)} %get-tuple-element.19), channel_id=1, replica_groups=mesh['tm'=8,'series'=64] {'series'}, dimensions={0} | all-to-all | bytes 524288 | tf_op jit(solution)/shard_map/all_to_all | solution.py:336
  43.1 0.0 copy-done.3
  43.1 0.8 %gaps.1 = bf16[64,16,128]{2,1,0:T(8,128)(2,1)S(1)} custom-call(bf16[64,16,128]{2,1,0:T(8,128)(2,1)S(1)} %all_to_all.15.got_ref, f32[48,64]{1,0:T(8,128)S(1)} %copy-done.3, f32[16,128]{1,0:T(8,128)S(1)} %get-tuple-element.20.base_rest_ref), custom_call_target="tpu_custom_call" | custom-call | tf_op jit(solution)/shard_map/gaps/pallas_call | solution.py:337
  43.9 18.4 %all_to_all.16.back_ref = bf16[64,16,128]{2,1,0:T(8,128)(2,1)S(1)} all-to-all(bf16[64,16,128]{2,1,0:T(8,128)(2,1)S(1)} %gaps.1), channel_id=1, replica_groups=mesh['tm'=8,'series'=64] {'series'}, dimensions={0} | all-to-all | bytes 524288 | tf_op jit(solution)/shard_map/all_to_all | solution.py:343
  62.3 1.8 %finish.1 = f32[48,2048]{1,0:T(8,128)} custom-call(f32[48,2048]{1,0:T(8,128)S(1)} %copy-done.1, f32[1,2048]{1,0:T(1,128)S(1)} %get-tuple-element.18.shift_ref, s32[4,2048]{1,0:T(4,128)S(1)} %get-tuple-element.17.places_ref, bf16[64,16,128]{2,1,0:T(8,128)(2,1)S(1)} %all_to_all.16.back_ref), custom_call_target="tpu_custom_call" | custom-call | tf_op jit(solution)/shard_map/finish/pallas_call | solution.py:344
Async XLA Ops:
  0.0 1.0 %copy-start = (f32[48,2048]{1,0:T(8,128)S(1)}, f32[48,2048]{1,0:T(8,128)}, u32[]{:S(2)}) copy-start(f32[48,2048]{1,0:T(8,128)} %leaf_ref.3) | copy-start | bytes 1179652
  1.0 9.8 %copy-start.1 = (f32[48,2048]{1,0:T(8,128)S(1)}, f32[48,2048]{1,0:T(8,128)}, u32[]{:S(2)}) copy-start(f32[48,2048]{1,0:T(8,128)} %leaf_ref.3) | copy-start | bytes 1179652
  1.7 12.7 %all-to-all-start = ((f32[8,16,128]{2,1,0:T(8,128)}), f32[8,16,128]{2,1,0:T(8,128)S(1)}, u32[]{:S(2)}, u32[]{:S(2)}) async-start(f32[8,16,128]{2,1,0:T(8,128)} %day_sums.1), calls=%async_computation | async-start | bytes 131072 | tf_op jit(solution)/shard_map/all_to_all | solution.py:313
  10.8 0.7 %copy-start.6 = (s32[2048,1]{0,1:T(1,128)S(1)}, s32[2048,1]{0,1:T(1,128)}, u32[]{:S(2)}) copy-start(s32[2048,1]{0,1:T(1,128)} %param.12) | copy-start | bytes 24580
  10.8 0.7 %copy-start.7 = (f32[48,8]{0,1:T(8,128)S(1)}, f32[48,8]{0,1:T(8,128)}, u32[]{:S(2)}) copy-start(f32[48,8]{0,1:T(8,128)} %param.14) | copy-start | bytes 4612
  10.8 0.7 %copy-start.5 = (s32[2048,1]{0,1:T(1,128)S(1)}, s32[2048,1]{0,1:T(1,128)}, u32[]{:S(2)}) copy-start(s32[2048,1]{0,1:T(1,128)} %param.11) | copy-start | bytes 24580
  10.8 0.7 %copy-start.4 = (s32[2048,1]{0,1:T(1,128)S(1)}, s32[2048,1]{0,1:T(1,128)}, u32[]{:S(2)}) copy-start(s32[2048,1]{0,1:T(1,128)} %param.10) | copy-start | bytes 24580
  10.8 0.7 %copy-start.8 = (f32[48,1]{0,1:T(1,128)S(1)}, f32[48,1]{0,1:T(1,128)}, u32[]{:S(2)}) copy-start(f32[48,1]{0,1:T(1,128)} %param.15) | copy-start | bytes 580
  11.6 2.8 %copy-start.2 = (f32[5,2048]{1,0:T(8,128)S(1)}, f32[5,2048]{1,0:T(8,128)}, u32[]{:S(2)}) copy-start(f32[5,2048]{1,0:T(8,128)} %seas_ref.1) | copy-start | bytes 122884
  16.1 27.0 %copy-start.3 = (f32[48,64]{1,0:T(8,128)S(1)}, f32[48,64]{1,0:T(8,128)}, u32[]{:S(2)}) copy-start(f32[48,64]{1,0:T(8,128)} %base_fine_ref.1) | copy-start | bytes 36868

commit v11 on v9

--- a/solution.py
+++ b/solution.py
@@ -69,14 +69,9 @@
     return jnp.concatenate([row[:, at:at + 128] for at in range(0, row.shape[1], 128)], axis=0)
 
 
-def start_kernel(quarter_ref, leaf_ref, fine_ref, mid_ref, top_ref, base_mid_ref, base_top_ref, sums_ref, ids_ref, base_ref):
+def start_kernel(leaf_ref, sums_ref):
     sums = dense_of(jnp.sum(leaf_ref[...], axis=0, keepdims=True))
     sums_ref[...] = jnp.broadcast_to(sums[None], sums_ref.shape)
-    for at, ref in enumerate((fine_ref, mid_ref, top_ref)):
-        ids_ref[at:at + 1, :] = ref[...]
-    ids_ref[3:4, :] = jnp.zeros_like(fine_ref[...]) + quarter_ref[0]
-    base_ref[0:8, :] = base_mid_ref[...]
-    base_ref[8:9, :] = base_top_ref[...]
 
 
 def ranks_of(owner, owners):
@@ -94,14 +89,19 @@
     return jnp.concatenate(ranks, axis=1).astype(i32)
 
 
-def sort_kernel(owners, leaf_ref, ids_ref, base_ref, slots_ref, nodes_ref, places_ref, from_ref, rest_ref):
+def sort_kernel(
+    owners, quarter_ref, fine_ref, mid_ref, top_ref, base_mid_ref, base_top_ref, seas_ref, leaf_ref,
+    slots_ref, nodes_ref, places_ref, from_ref, rest_ref, known_ref,
+):
     days, rows = leaf_ref.shape
-    fine, mid, top = (ids_ref[at:at + 1, :] for at in range(3))
+    fine, mid, top = fine_ref[...], mid_ref[...], top_ref[...]
     owner = fine >> 6
     rank = ranks_of(owner, owners)
     place = (rank >> 4) * (owners * 16) + owner * 16 + (rank & 15)
     places_ref[0:1, :] = place
-    places_ref[1:4, :] = ids_ref[1:4, :]
+    places_ref[1:2, :] = mid
+    places_ref[2:3, :] = top
+    places_ref[3:4, :] = jnp.zeros_like(mid) + quarter_ref[0]
 
     leaf = leaf_ref[...]
     high = leaf.astype(bf16).astype(f32)
@@ -131,7 +131,13 @@
     nodes_ref[:, mids:] = tops
     from_ref[0, :, :] = dense_of(slots_ref[LOW + 1:LOW + 2, :]).astype(i32)
     from_ref[1, :, :] = dense_of(slots_ref[LOW + 2:LOW + 3, :]).astype(i32)
-    rest_ref[...] = rest_in_lanes(base_ref[0:8, :], base_ref[8:9, :])
+    seas = seas_ref[...]
+    season_days = days * 2
+    line = iota(seas.shape, 0)
+    seas_own = jnp.sum(jnp.where(line == quarter_ref[0], seas, 0.0), axis=0, keepdims=True)
+    seas_four = jnp.sum(jnp.where(line < 4, seas, 0.0), axis=0, keepdims=True)
+    known_ref[...] = dense_of(0.5 * seas_own / season_days + 0.5 * (seas[4:5, :] - 0.5 * seas_four) / (season_days * 4))
+    rest_ref[...] = rest_in_lanes(base_mid_ref[...], base_top_ref[...])
 
 
 def rest_in_lanes(base_mid, base_top):
@@ -155,7 +161,7 @@
     return jnp.where(iota(sums.shape, 0) == LOW, sums - high, high)
 
 
-def send_kernel(parts_ref, seas_ref, from_ref, slots_ref, nodes_ref, places_ref, pay_ref, shift_ref):
+def send_kernel(parts_ref, known_ref, from_ref, slots_ref, nodes_ref, places_ref, pay_ref, shift_ref):
     owners = pay_ref.shape[0]
     rows = places_ref.shape[1]
     slots, mids = owners * 16, owners * 8
@@ -165,12 +171,7 @@
     quarter = places_ref[3:4, 0:128]
     own = jnp.sum(jnp.where(iota(parts.shape, 0) >> 1 == quarter[None], parts, 0.0), axis=0)
     total = jnp.sum(parts, axis=0)
-    seas = seas_ref[...]
-    line = iota(seas.shape, 0)
-    seas_own = jnp.sum(jnp.where(line == places_ref[3:4, :], seas, 0.0), axis=0, keepdims=True)
-    seas_four = jnp.sum(jnp.where(line < 4, seas, 0.0), axis=0, keepdims=True)
-    known = dense_of(0.5 * seas_own / season_days + 0.5 * (seas[4:5, :] - 0.5 * seas_four) / (season_days * 4))
-    shift = known - (0.5 * own / season_days + 0.25 * total / (season_days * 4))
+    shift = known_ref[...] - (0.5 * own / season_days + 0.25 * total / (season_days * 4))
     shift_row = row_of(shift)
     shift_ref[...] = shift_row
 
@@ -304,19 +305,11 @@
     smem = pl.BlockSpec(memory_space=pltpu.SMEM)
     dense = (rows // 128, 128)
 
-    sums, ids, base = pl.pallas_call(
-        start_kernel,
-        out_shape=(
-            jax.ShapeDtypeStruct((blocks,) + dense, f32),
-            jax.ShapeDtypeStruct((4, rows), i32),
-            jax.ShapeDtypeStruct((16, days), f32),
-        ),
-        in_specs=[smem] + [vmem] * 6,
-        compiler_params=PARAMS,
-        name="start",
-    )(quarter, leaf, *(ids.reshape(1, rows) for ids in (fine, mid, top)), base_mid.T, base_top.reshape(1, days))
+    sums = pl.pallas_call(
+        start_kernel, out_shape=jax.ShapeDtypeStruct((blocks,) + dense, f32), compiler_params=PARAMS, name="day_sums"
+    )(leaf)
     parts = lax.all_to_all(sums, "tm", 0, 0, tiled=True)
-    slots, nodes, places, come_from, base_rest = pl.pallas_call(
+    slots, nodes, places, come_from, base_rest, known = pl.pallas_call(
         lambda *refs: sort_kernel(owners, *refs),
         out_shape=(
             jax.ShapeDtypeStruct((days + 8, rows), f32),
@@ -324,18 +317,20 @@
             jax.ShapeDtypeStruct((4, rows), i32),
             jax.ShapeDtypeStruct((2,) + dense, i32),
             jax.ShapeDtypeStruct((16, 128), f32),
+            jax.ShapeDtypeStruct(dense, f32),
         ),
+        in_specs=[smem] + [vmem] * 7,
         compiler_params=PARAMS,
         cost_estimate=pl.CostEstimate(flops=2 * 104 * owners * 42 * rows, bytes_accessed=4 * days * rows, transcendentals=0),
         name="sort",
-    )(leaf, ids, base)
+    )(quarter, *(ids.reshape(1, rows) for ids in (fine, mid, top)), base_mid.T, base_top.reshape(1, days), seas, leaf)
 
     payload, shift = pl.pallas_call(
         send_kernel,
         out_shape=(jax.ShapeDtypeStruct((owners, 16, 128), bf16), jax.ShapeDtypeStruct((1, rows), f32)),
         compiler_params=PARAMS,
         name="pack",
-    )(parts, seas, come_from, slots, nodes, places)
+    )(parts, known, come_from, slots, nodes, places)
     got = lax.all_to_all(payload, "series", 0, 0, tiled=True)
     back = pl.pallas_call(
         owner_kernel,

time: 65.4 us -> 64.8 us (level)
  waiting for transfers between devices: 1.55 us -> 0.8 us
    all_to_all x1, waiting for transfers between devices: 1.55 us -> 0.8 us  [per_device(): parts = lax.all_to_all(sums, 'tm', 0, 0, tiled=True)]
where the time goes in v11:
time: 64.8 us; the launch traced here: 63.7 us
  blocking collectives  45.4 us (70%)
  starting transfers between devices  9.27 us (14%)
  Pallas kernels  6.47 us (10%)
  local copies, waits for them, and re-layouts  1.71 us (3%)
  waiting for transfers between devices  0.8 us (1%)
    all_to_all x1, blocking collectives, per_device(): got = lax.all_to_all(payload, 'series', 0, 0, tiled=True)  27 us
    all_to_all x1, blocking collectives, per_device(): back = lax.all_to_all(back, 'series', 0, 0, tiled=True)  18.4 us
    all_to_all x1, starting transfers between devices, per_device(): parts = lax.all_to_all(sums, 'tm', 0, 0, tiled=True)  9.27 us
    pallas_call x1, Pallas kernels, per_device(): pl.pallas_call(lambda *refs: sort_kernel(owners, *refs), out_shape=(jax.S...  1.97 us
    pallas_call x1, Pallas kernels, per_device(): pl.pallas_call(finish_kernel, out_shape=jax.ShapeDtypeStruct((days, rows)...  1.83 us
    unnamed x18, local copies, waits for them, and re-layouts  1.71 us
  transfers between devices with their start and end apart: 1, of which 1 were waited for; matrix products, arithmetic and copies ran while one was open for 0% of the time, Pallas kernels for 3%

profile of v11, /device:TPU:6, one launch (start us, length us, event | category | flops | bytes accessed | tf_op | source)
XLA Modules:
  0.0 63.7 jit_solution(12175443941272253893)
XLA Ops:
  0.0 0.0 copy-start
  0.0 1.0 %copy-done = f32[48,2048]{1,0:T(8,128)S(1)} copy-done((f32[48,2048]{1,0:T(8,128)S(1)}, f32[48,2048]{1,0:T(8,128)}, u32[]{:S(2)}) %copy-start) | copy-done | bytes 393240
  1.0 0.0 copy-start.1
  1.0 0.7 %day_sums.1 = f32[8,16,128]{2,1,0:T(8,128)} custom-call(f32[48,2048]{1,0:T(8,128)S(1)} %copy-done), custom_call_target="tpu_custom_call" | custom-call | tf_op jit(solution)/shard_map/day_sums/pallas_call | solution.py:308
  1.7 0.0 copy-start.3
  1.7 9.3 %all-to-all-start = ((f32[8,16,128]{2,1,0:T(8,128)}), f32[8,16,128]{2,1,0:T(8,128)S(1)}, u32[]{:S(2)}, u32[]{:S(2)}) async-start(f32[8,16,128]{2,1,0:T(8,128)} %day_sums.1), calls=%async_computation | async-start | bytes 131072 | tf_op jit(solution)/shard_map/all_to_all | solution.py:311
  10.9 0.0 copy-start.6
  10.9 0.0 copy-start.7
  10.9 0.0 copy-start.5
  10.9 0.0 copy-start.4
  11.0 0.0 copy-start.8
  11.0 0.0 copy-done.1
  11.0 0.0 copy-done.3
  11.0 0.6 copy-done.6
  11.6 0.0 copy-done.7
  11.6 0.0 copy-done.5
  11.7 0.0 copy-done.4
  11.7 0.0 copy-done.8
  11.7 2.0 %sort.1 = (f32[56,2048]{1,0:T(8,128)S(1)}, f32[56,640]{1,0:T(8,128)S(1)}, s32[4,2048]{1,0:T(4,128)S(1)}, s32[2,16,128]{2,1,0:T(8,128)S(1)}, f32[16,128]{1,0:T(8,128)S(1)}, /*index=5*/f32[16,128]{1,0:T(8,128)S(1)}) custom-call(s32[1]{0:T(128)} %bitcast.refs_0_, s32[1,2048]{1,0:T(1,128)S(1)} %bitcast.6, s32[1,2048]{1,0:T(1,128)S(1)} %bitcast.7, ...), custom_call_target="tpu_custom_call" | custom-call | flops 1145044992 | bytes 393216 | tf_op jit(solution)/shard_map/sort/pallas_call | solution.py:312
  13.7 0.8 %all-to-all-done.parts_ref = f32[8,16,128]{2,1,0:T(8,128)S(1)} async-done(((f32[8,16,128]{2,1,0:T(8,128)}), f32[8,16,128]{2,1,0:T(8,128)S(1)}, u32[]{:S(2)}, u32[]{:S(2)}) %all-to-all-start) | async-done | bytes 65568 | tf_op jit(solution)/shard_map/all_to_all | solution.py:311
  14.5 1.2 %pack.1 = (bf16[64,16,128]{2,1,0:T(8,128)(2,1)S(1)}, f32[1,2048]{1,0:T(1,128)S(1)}) custom-call(f32[8,16,128]{2,1,0:T(8,128)S(1)} %all-to-all-done.parts_ref, f32[16,128]{1,0:T(8,128)S(1)} %get-tuple-element.13.known_ref, s32[2,16,128]{2,1,0:T(8,128)S(1)} %get-tuple-element.14.from_ref, f32[56,2048]{1,0:T(8,128)S(1)} %get-tuple-element.15.slots_ref, ...), custom_call_target="tpu_custom_call" | custom-call | tf_op jit(solution)/shard_map/pack/pallas_call | solution.py:328
  15.7 0.0 copy-start.2
  15.7 27.0 %all_to_all.15.got_ref = bf16[64,16,128]{2,1,0:T(8,128)(2,1)S(1)} all-to-all(bf16[64,16,128]{2,1,0:T(8,128)(2,1)S(1)} %get-tuple-element.19), channel_id=1, replica_groups=mesh['tm'=8,'series'=64] {'series'}, dimensions={0} | all-to-all | bytes 524288 | tf_op jit(solution)/shard_map/all_to_all | solution.py:334
  42.6 0.0 copy-done.2
  42.6 0.8 %gaps.1 = bf16[64,16,128]{2,1,0:T(8,128)(2,1)S(1)} custom-call(bf16[64,16,128]{2,1,0:T(8,128)(2,1)S(1)} %all_to_all.15.got_ref, f32[48,64]{1,0:T(8,128)S(1)} %copy-done.2, f32[16,128]{1,0:T(8,128)S(1)} %get-tuple-element.20.base_rest_ref), custom_call_target="tpu_custom_call" | custom-call | tf_op jit(solution)/shard_map/gaps/pallas_call | solution.py:335
  43.5 18.4 %all_to_all.16.back_ref = bf16[64,16,128]{2,1,0:T(8,128)(2,1)S(1)} all-to-all(bf16[64,16,128]{2,1,0:T(8,128)(2,1)S(1)} %gaps.1), channel_id=1, replica_groups=mesh['tm'=8,'series'=64] {'series'}, dimensions={0} | all-to-all | bytes 524288 | tf_op jit(solution)/shard_map/all_to_all | solution.py:341
  61.9 1.8 %finish.1 = f32[48,2048]{1,0:T(8,128)} custom-call(f32[48,2048]{1,0:T(8,128)S(1)} %copy-done.1, f32[1,2048]{1,0:T(1,128)S(1)} %get-tuple-element.18.shift_ref, s32[4,2048]{1,0:T(4,128)S(1)} %get-tuple-element.17.places_ref, bf16[64,16,128]{2,1,0:T(8,128)(2,1)S(1)} %all_to_all.16.back_ref), custom_call_target="tpu_custom_call" | custom-call | tf_op jit(solution)/shard_map/finish/pallas_call | solution.py:342
Async XLA Ops:
  0.0 1.0 %copy-start = (f32[48,2048]{1,0:T(8,128)S(1)}, f32[48,2048]{1,0:T(8,128)}, u32[]{:S(2)}) copy-start(f32[48,2048]{1,0:T(8,128)} %leaf_ref.3) | copy-start | bytes 1179652
  1.0 10.0 %copy-start.1 = (f32[48,2048]{1,0:T(8,128)S(1)}, f32[48,2048]{1,0:T(8,128)}, u32[]{:S(2)}) copy-start(f32[48,2048]{1,0:T(8,128)} %leaf_ref.3) | copy-start | bytes 1179652
  1.7 9.3 %copy-start.3 = (f32[5,2048]{1,0:T(8,128)S(1)}, f32[5,2048]{1,0:T(8,128)}, u32[]{:S(2)}) copy-start(f32[5,2048]{1,0:T(8,128)} %refs_6_.1) | copy-start | bytes 122884
  1.7 12.8 %all-to-all-start = ((f32[8,16,128]{2,1,0:T(8,128)}), f32[8,16,128]{2,1,0:T(8,128)S(1)}, u32[]{:S(2)}, u32[]{:S(2)}) async-start(f32[8,16,128]{2,1,0:T(8,128)} %day_sums.1), calls=%async_computation | async-start | bytes 131072 | tf_op jit(solution)/shard_map/all_to_all | solution.py:311
  10.9 0.7 %copy-start.6 = (s32[2048,1]{0,1:T(1,128)S(1)}, s32[2048,1]{0,1:T(1,128)}, u32[]{:S(2)}) copy-start(s32[2048,1]{0,1:T(1,128)} %param.12) | copy-start | bytes 24580
  10.9 0.7 %copy-start.7 = (f32[48,8]{0,1:T(8,128)S(1)}, f32[48,8]{0,1:T(8,128)}, u32[]{:S(2)}) copy-start(f32[48,8]{0,1:T(8,128)} %param.14) | copy-start | bytes 4612
  10.9 0.7 %copy-start.5 = (s32[2048,1]{0,1:T(1,128)S(1)}, s32[2048,1]{0,1:T(1,128)}, u32[]{:S(2)}) copy-start(s32[2048,1]{0,1:T(1,128)} %param.11) | copy-start | bytes 24580
  10.9 0.7 %copy-start.4 = (s32[2048,1]{0,1:T(1,128)S(1)}, s32[2048,1]{0,1:T(1,128)}, u32[]{:S(2)}) copy-start(s32[2048,1]{0,1:T(1,128)} %param.10) | copy-start | bytes 24580
  11.0 0.7 %copy-start.8 = (f32[48,1]{0,1:T(1,128)S(1)}, f32[48,1]{0,1:T(1,128)}, u32[]{:S(2)}) copy-start(f32[48,1]{0,1:T(1,128)} %param.15) | copy-start | bytes 580
  15.7 27.0 %copy-start.2 = (f32[48,64]{1,0:T(8,128)S(1)}, f32[48,64]{1,0:T(8,128)}, u32[]{:S(2)}) copy-start(f32[48,64]{1,0:T(8,128)} %base_fine_ref.1) | copy-start | bytes 36868

commit v12 on v11

--- a/solution.py
+++ b/solution.py
@@ -91,7 +91,7 @@
 
 def sort_kernel(
     owners, quarter_ref, fine_ref, mid_ref, top_ref, base_mid_ref, base_top_ref, seas_ref, leaf_ref,
-    slots_ref, nodes_ref, places_ref, from_ref, rest_ref, known_ref,
+    parts_ref, slots_ref, nodes_ref, places_ref, from_ref, rest_ref, known_ref,
 ):
     days, rows = leaf_ref.shape
     fine, mid, top = fine_ref[...], mid_ref[...], top_ref[...]
@@ -136,7 +136,11 @@
     line = iota(seas.shape, 0)
     seas_own = jnp.sum(jnp.where(line == quarter_ref[0], seas, 0.0), axis=0, keepdims=True)
     seas_four = jnp.sum(jnp.where(line < 4, seas, 0.0), axis=0, keepdims=True)
-    known_ref[...] = dense_of(0.5 * seas_own / season_days + 0.5 * (seas[4:5, :] - 0.5 * seas_four) / (season_days * 4))
+    parts = parts_ref[...]
+    own = jnp.sum(jnp.where(iota(parts.shape, 0) >> 1 == quarter_ref[0], parts, 0.0), axis=0)
+    total = jnp.sum(parts, axis=0)
+    known = dense_of(0.5 * seas_own / season_days + 0.5 * (seas[4:5, :] - 0.5 * seas_four) / (season_days * 4))
+    known_ref[...] = known - (0.5 * own / season_days + 0.25 * total / (season_days * 4))
     rest_ref[...] = rest_in_lanes(base_mid_ref[...], base_top_ref[...])
 
 
@@ -161,19 +165,14 @@
     return jnp.where(iota(sums.shape, 0) == LOW, sums - high, high)
 
 
-def send_kernel(parts_ref, known_ref, from_ref, slots_ref, nodes_ref, places_ref, pay_ref, shift_ref):
+def send_kernel(shift_ref, from_ref, slots_ref, nodes_ref, places_ref, pay_ref, row_ref):
     owners = pay_ref.shape[0]
     rows = places_ref.shape[1]
     slots, mids = owners * 16, owners * 8
     days = slots_ref.shape[0] - 8
-    season_days = days * 2
-    parts = parts_ref[...]
-    quarter = places_ref[3:4, 0:128]
-    own = jnp.sum(jnp.where(iota(parts.shape, 0) >> 1 == quarter[None], parts, 0.0), axis=0)
-    total = jnp.sum(parts, axis=0)
-    shift = known_ref[...] - (0.5 * own / season_days + 0.25 * total / (season_days * 4))
+    shift = shift_ref[...]
     shift_row = row_of(shift)
-    shift_ref[...] = shift_row
+    row_ref[...] = shift_row
 
     line, lane = from_ref[0, :, :], from_ref[1, :, :]
     moved = jnp.zeros(shift.shape, f32)
@@ -319,18 +318,18 @@
             jax.ShapeDtypeStruct((16, 128), f32),
             jax.ShapeDtypeStruct(dense, f32),
         ),
-        in_specs=[smem] + [vmem] * 7,
+        in_specs=[smem] + [vmem] * 8,
         compiler_params=PARAMS,
         cost_estimate=pl.CostEstimate(flops=2 * 104 * owners * 42 * rows, bytes_accessed=4 * days * rows, transcendentals=0),
         name="sort",
-    )(quarter, *(ids.reshape(1, rows) for ids in (fine, mid, top)), base_mid.T, base_top.reshape(1, days), seas, leaf)
+    )(quarter, *(ids.reshape(1, rows) for ids in (fine, mid, top)), base_mid.T, base_top.reshape(1, days), seas, leaf, parts)
 
     payload, shift = pl.pallas_call(
         send_kernel,
         out_shape=(jax.ShapeDtypeStruct((owners, 16, 128), bf16), jax.ShapeDtypeStruct((1, rows), f32)),
         compiler_params=PARAMS,
         name="pack",
-    )(parts, known, come_from, slots, nodes, places)
+    )(known, come_from, slots, nodes, places)
     got = lax.all_to_all(payload, "series", 0, 0, tiled=True)
     back = pl.pallas_call(
         owner_kernel,

time: 64.8 us -> 67.3 us (1.039)
  waiting for transfers between devices: 0.8 us -> 3.5 us
    all_to_all x1, waiting for transfers between devices: 0.8 us -> 3.5 us  [per_device(): parts = lax.all_to_all(sums, 'tm', 0, 0, tiled=True)]
  transfers between devices with their start and end apart: 1 -> 1, of which waited for: 1 -> 1; matrix products, arithmetic and copies ran while one was open for 0% -> 0% of each run, Pallas kernels for 3% -> 0%
where the time goes in v12:
time: 67.3 us; the launch traced here: 66.3 us
  blocking collectives  45.4 us (67%)
  starting transfers between devices  9.27 us (14%)
  Pallas kernels  6.49 us (10%)
  waiting for transfers between devices  3.5 us (5%)
  local copies, waits for them, and re-layouts  1.64 us (2%)
    all_to_all x1, blocking collectives, per_device(): got = lax.all_to_all(payload, 'series', 0, 0, tiled=True)  27 us
    all_to_all x1, blocking collectives, per_device(): back = lax.all_to_all(back, 'series', 0, 0, tiled=True)  18.4 us
    all_to_all x1, starting transfers between devices, per_device(): parts = lax.all_to_all(sums, 'tm', 0, 0, tiled=True)  9.27 us
    all_to_all x1, waiting for transfers between devices, per_device(): parts = lax.all_to_all(sums, 'tm', 0, 0, tiled=True)  3.5 us
    pallas_call x1, Pallas kernels, per_device(): pl.pallas_call(lambda *refs: sort_kernel(owners, *refs), out_shape=(jax.S...  1.98 us
    pallas_call x1, Pallas kernels, per_device(): pl.pallas_call(finish_kernel, out_shape=jax.ShapeDtypeStruct((days, rows)...  1.84 us
    unnamed x18, local copies, waits for them, and re-layouts  1.64 us
  transfers between devices with their start and end apart: 1, of which 1 were waited for; matrix products, arithmetic and copies ran while one was open for 0% of the time, Pallas kernels for 0%

profile of v12, /device:TPU:6, one launch (start us, length us, event | category | flops | bytes accessed | tf_op | source)
XLA Modules:
  0.0 66.3 jit_solution(7703425673850096929)
XLA Ops:
  0.0 0.0 copy-start
  0.0 1.0 %copy-done = f32[48,2048]{1,0:T(8,128)S(1)} copy-done((f32[48,2048]{1,0:T(8,128)S(1)}, f32[48,2048]{1,0:T(8,128)}, u32[]{:S(2)}) %copy-start) | copy-done | bytes 393240
  1.0 0.0 copy-start.1
  1.0 0.7 day_sums.1
  1.7 0.0 copy-start.3
  1.7 9.3 %all-to-all-start = ((f32[8,16,128]{2,1,0:T(8,128)}), f32[8,16,128]{2,1,0:T(8,128)S(1)}, u32[]{:S(2)}, u32[]{:S(2)}) async-start(f32[8,16,128]{2,1,0:T(8,128)} %day_sums.1), calls=%async_computation | async-start | bytes 131072 | tf_op jit(solution)/shard_map/all_to_all | solution.py:310
  10.9 0.0 copy-start.6
  10.9 0.0 copy-start.7
  10.9 0.0 copy-start.5
  10.9 0.0 copy-start.4
  11.0 3.5 %all-to-all-done.refs_8_ = f32[8,16,128]{2,1,0:T(8,128)S(1)} async-done(((f32[8,16,128]{2,1,0:T(8,128)}), f32[8,16,128]{2,1,0:T(8,128)S(1)}, u32[]{:S(2)}, u32[]{:S(2)}) %all-to-all-start) | async-done | bytes 65568 | tf_op jit(solution)/shard_map/all_to_all | solution.py:310
  14.5 0.0 copy-start.8
  14.5 0.0 copy-done.1
  14.5 0.0 copy-done.3
  14.5 0.0 copy-done.6
  14.5 0.0 copy-done.7
  14.5 0.0 copy-done.5
  14.5 0.0 copy-done.4
  14.5 0.6 copy-done.8
  15.1 2.0 %sort.1 = (f32[56,2048]{1,0:T(8,128)S(1)}, f32[56,640]{1,0:T(8,128)S(1)}, s32[4,2048]{1,0:T(4,128)S(1)}, s32[2,16,128]{2,1,0:T(8,128)S(1)}, f32[16,128]{1,0:T(8,128)S(1)}, /*index=5*/f32[16,128]{1,0:T(8,128)S(1)}) custom-call(s32[1]{0:T(128)} %bitcast.refs_0_, s32[1,2048]{1,0:T(1,128)S(1)} %bitcast.6, s32[1,2048]{1,0:T(1,128)S(1)} %bitcast.7, ...), custom_call_target="tpu_custom_call" | custom-call | flops 1145044992 | bytes 393216 | tf_op jit(solution)/shard_map/sort/pallas_call | solution.py:311
  17.1 1.2 %pack.1 = (bf16[64,16,128]{2,1,0:T(8,128)(2,1)S(1)}, f32[1,2048]{1,0:T(1,128)S(1)}) custom-call(f32[16,128]{1,0:T(8,128)S(1)} %get-tuple-element.13.shift_ref, s32[2,16,128]{2,1,0:T(8,128)S(1)} %get-tuple-element.14.from_ref, f32[56,2048]{1,0:T(8,128)S(1)} %get-tuple-element.15.slots_ref, f32[56,640]{1,0:T(8,128)S(1)} %get-tuple-element.16.nodes_ref, ...), custom_call_target="tpu_custom_call" | custom-call | tf_op jit(solution)/shard_map/pack/pallas_call | solution.py:327
  18.3 0.0 copy-start.2
  18.3 27.0 %all_to_all.15.got_ref = bf16[64,16,128]{2,1,0:T(8,128)(2,1)S(1)} all-to-all(bf16[64,16,128]{2,1,0:T(8,128)(2,1)S(1)} %get-tuple-element.19), channel_id=1, replica_groups=mesh['tm'=8,'series'=64] {'series'}, dimensions={0} | all-to-all | bytes 524288 | tf_op jit(solution)/shard_map/all_to_all | solution.py:333
  45.3 0.0 copy-done.2
  45.3 0.8 %gaps.1 = bf16[64,16,128]{2,1,0:T(8,128)(2,1)S(1)} custom-call(bf16[64,16,128]{2,1,0:T(8,128)(2,1)S(1)} %all_to_all.15.got_ref, f32[48,64]{1,0:T(8,128)S(1)} %copy-done.2, f32[16,128]{1,0:T(8,128)S(1)} %get-tuple-element.20.base_rest_ref), custom_call_target="tpu_custom_call" | custom-call | tf_op jit(solution)/shard_map/gaps/pallas_call | solution.py:334
  46.1 18.4 %all_to_all.16.back_ref = bf16[64,16,128]{2,1,0:T(8,128)(2,1)S(1)} all-to-all(bf16[64,16,128]{2,1,0:T(8,128)(2,1)S(1)} %gaps.1), channel_id=1, replica_groups=mesh['tm'=8,'series'=64] {'series'}, dimensions={0} | all-to-all | bytes 524288 | tf_op jit(solution)/shard_map/all_to_all | solution.py:340
  64.5 1.8 %finish.1 = f32[48,2048]{1,0:T(8,128)} custom-call(f32[48,2048]{1,0:T(8,128)S(1)} %copy-done.1, f32[1,2048]{1,0:T(1,128)S(1)} %get-tuple-element.18.shift_ref, s32[4,2048]{1,0:T(4,128)S(1)} %get-tuple-element.17.places_ref, bf16[64,16,128]{2,1,0:T(8,128)(2,1)S(1)} %all_to_all.16.back_ref), custom_call_target="tpu_custom_call" | custom-call | tf_op jit(solution)/shard_map/finish/pallas_call | solution.py:341
Async XLA Ops:
  0.0 1.0 %copy-start = (f32[48,2048]{1,0:T(8,128)S(1)}, f32[48,2048]{1,0:T(8,128)}, u32[]{:S(2)}) copy-start(f32[48,2048]{1,0:T(8,128)} %leaf_ref.3) | copy-start | bytes 1179652
  1.0 13.5 %copy-start.1 = (f32[48,2048]{1,0:T(8,128)S(1)}, f32[48,2048]{1,0:T(8,128)}, u32[]{:S(2)}) copy-start(f32[48,2048]{1,0:T(8,128)} %leaf_ref.3) | copy-start | bytes 1179652
  1.7 12.8 %copy-start.3 = (f32[5,2048]{1,0:T(8,128)S(1)}, f32[5,2048]{1,0:T(8,128)}, u32[]{:S(2)}) copy-start(f32[5,2048]{1,0:T(8,128)} %refs_6_.1) | copy-start | bytes 122884
  1.7 12.8 %all-to-all-start = ((f32[8,16,128]{2,1,0:T(8,128)}), f32[8,16,128]{2,1,0:T(8,128)S(1)}, u32[]{:S(2)}, u32[]{:S(2)}) async-start(f32[8,16,128]{2,1,0:T(8,128)} %day_sums.1), calls=%async_computation | async-start | bytes 131072 | tf_op jit(solution)/shard_map/all_to_all | solution.py:310
  10.9 3.5 %copy-start.6 = (s32[2048,1]{0,1:T(1,128)S(1)}, s32[2048,1]{0,1:T(1,128)}, u32[]{:S(2)}) copy-start(s32[2048,1]{0,1:T(1,128)} %param.12) | copy-start | bytes 24580
  10.9 3.5 %copy-start.7 = (f32[48,8]{0,1:T(8,128)S(1)}, f32[48,8]{0,1:T(8,128)}, u32[]{:S(2)}) copy-start(f32[48,8]{0,1:T(8,128)} %param.14) | copy-start | bytes 4612
  10.9 3.6 %copy-start.5 = (s32[2048,1]{0,1:T(1,128)S(1)}, s32[2048,1]{0,1:T(1,128)}, u32[]{:S(2)}) copy-start(s32[2048,1]{0,1:T(1,128)} %param.11) | copy-start | bytes 24580
  10.9 3.6 %copy-start.4 = (s32[2048,1]{0,1:T(1,128)S(1)}, s32[2048,1]{0,1:T(1,128)}, u32[]{:S(2)}) copy-start(s32[2048,1]{0,1:T(1,128)} %param.10) | copy-start | bytes 24580
  14.5 0.7 copy-start.8
  18.3 27.0 %copy-start.2 = (f32[48,64]{1,0:T(8,128)S(1)}, f32[48,64]{1,0:T(8,128)}, u32[]{:S(2)}) copy-start(f32[48,64]{1,0:T(8,128)} %base_fine_ref.1) | copy-start | bytes 36868

commit v13 on v11

--- a/solution.py
+++ b/solution.py
@@ -69,8 +69,18 @@
     return jnp.concatenate([row[:, at:at + 128] for at in range(0, row.shape[1], 128)], axis=0)
 
 
-def start_kernel(leaf_ref, sums_ref):
-    sums = dense_of(jnp.sum(leaf_ref[...], axis=0, keepdims=True))
+def start_kernel(leaf_ref, sums_ref, here_ref, sems):
+    strips = range(0, leaf_ref.shape[0], 8)
+    copies = [
+        pltpu.make_async_copy(leaf_ref.at[at:at + 8, :], here_ref.at[at:at + 8, :], sems.at[at // 8]) for at in strips
+    ]
+    for copy in copies:
+        copy.start()
+    total = jnp.zeros((8, leaf_ref.shape[1]), f32)
+    for at, copy in zip(strips, copies):
+        copy.wait()
+        total = total + here_ref[at:at + 8, :]
+    sums = dense_of(jnp.sum(total, axis=0, keepdims=True))
     sums_ref[...] = jnp.broadcast_to(sums[None], sums_ref.shape)
 
 
@@ -239,7 +249,8 @@
     node = iota((owners * 16, nodes), 1).astype(f32)
     pick_low = ones_where(flat[:, ID:ID + 1] == node)
     pick_high = ones_where(flat[:, 64 + ID:65 + ID] == node)
-    turned = jnp.transpose(jnp.where((lanes & 63) == ONE, 1.0, flat)).astype(bf16)
+    same = ones_where(iota((128, 128), 0) == iota((128, 128), 1))
+    turned = dot_nt(same, jnp.where((lanes & 63) == ONE, 1.0, flat).astype(bf16)).astype(bf16)
     totals = dot(turned[0:64, :], pick_low) + dot(turned[64:128, :], pick_high)
     gap = (base_fine_ref[...] - totals[0:days, :]) / (totals[ONE:ONE + 1, :] + 1.0)
     gap = jnp.concatenate([gap, jnp.zeros((64 - days, nodes), f32)], axis=0)
@@ -306,7 +317,12 @@
     dense = (rows // 128, 128)
 
     sums = pl.pallas_call(
-        start_kernel, out_shape=jax.ShapeDtypeStruct((blocks,) + dense, f32), compiler_params=PARAMS, name="day_sums"
+        start_kernel,
+        out_shape=jax.ShapeDtypeStruct((blocks,) + dense, f32),
+        in_specs=[pl.BlockSpec(memory_space=pltpu.HBM)],
+        scratch_shapes=[pltpu.VMEM((days, rows), f32), pltpu.SemaphoreType.DMA((days // 8,))],
+        compiler_params=pltpu.CompilerParams(vmem_limit_bytes=66900000),
+        name="day_sums",
     )(leaf)
     parts = lax.all_to_all(sums, "tm", 0, 0, tiled=True)
     slots, nodes, places, come_from, base_rest, known = pl.pallas_call(

time: 64.8 us -> 65 us (level)
  Pallas kernels: 6.47 us -> 7.51 us
  waiting for transfers between devices: 0.8 us -> 0.01 us
    pallas_call x1, Pallas kernels: 0.66 us -> 1.7 us  [per_device(): pl.pallas_call(start_kernel, out_shape=jax.ShapeDtypeStruct((blocks,) + d...]
    all_to_all x1, waiting for transfers between devices: 0.8 us -> 0.01 us  [per_device(): parts = lax.all_to_all(sums, 'tm', 0, 0, tiled=True)]
  transfers between devices with their start and end apart: 1 -> 1, of which waited for: 1 -> 0; matrix products, arithmetic and copies ran while one was open for 0% -> 0% of each run, Pallas kernels for 3% -> 3%
where the time goes in v13:
time: 65 us; the launch traced here: 64.5 us
  blocking collectives  45.9 us (71%)
  starting transfers between devices  9.28 us (14%)
  Pallas kernels  7.51 us (12%)
  local copies, waits for them, and re-layouts  1.72 us (3%)
    all_to_all x1, blocking collectives, per_device(): got = lax.all_to_all(payload, 'series', 0, 0, tiled=True)  27.3 us
    all_to_all x1, blocking collectives, per_device(): back = lax.all_to_all(back, 'series', 0, 0, tiled=True)  18.6 us
    all_to_all x1, starting transfers between devices, per_device(): parts = lax.all_to_all(sums, 'tm', 0, 0, tiled=True)  9.28 us
    pallas_call x1, Pallas kernels, per_device(): pl.pallas_call(lambda *refs: sort_kernel(owners, *refs), out_shape=(jax.S...  1.97 us
    pallas_call x1, Pallas kernels, per_device(): pl.pallas_call(finish_kernel, out_shape=jax.ShapeDtypeStruct((days, rows)...  1.84 us
    unnamed x18, local copies, waits for them, and re-layouts  1.72 us
    pallas_call x1, Pallas kernels, per_device(): pl.pallas_call(start_kernel, out_shape=jax.ShapeDtypeStruct((blocks,) + d...  1.7 us
  transfers between devices with their start and end apart: 1, of which 0 were waited for; matrix products, arithmetic and copies ran while one was open for 0% of the time, Pallas kernels for 3%

profile of v13, /device:TPU:6, one launch (start us, length us, event | category | flops | bytes accessed | tf_op | source)
XLA Modules:
  0.0 64.5 jit_solution(14346848407148511463)
XLA Ops:
  0.0 1.7 %day_sums.1 = f32[8,16,128]{2,1,0:T(8,128)} custom-call(f32[48,2048]{1,0:T(8,128)} %leaf_ref.3), custom_call_target="tpu_custom_call" | custom-call | tf_op jit(solution)/shard_map/day_sums/pallas_call | solution.py:319
  1.7 0.0 copy-start.3
  1.7 9.3 %all-to-all-start = ((f32[8,16,128]{2,1,0:T(8,128)}), f32[8,16,128]{2,1,0:T(8,128)S(1)}, u32[]{:S(2)}, u32[]{:S(2)}) async-start(f32[8,16,128]{2,1,0:T(8,128)} %day_sums.1), calls=%async_computation | async-start | bytes 131072 | tf_op jit(solution)/shard_map/all_to_all | solution.py:327
  11.0 0.0 copy-start.6
  11.0 0.0 copy-start.7
  11.0 0.0 copy-start.5
  11.0 0.0 copy-start.4
  11.0 0.0 copy-start.8
  11.0 0.0 copy-done.3
  11.1 0.6 %copy-done.6 = s32[2048,1]{0,1:T(1,128)S(1)} copy-done((s32[2048,1]{0,1:T(1,128)S(1)}, s32[2048,1]{0,1:T(1,128)}, u32[]{:S(2)}) %copy-start.6) | copy-done | bytes 8216
  11.7 0.0 copy-done.7
  11.7 0.0 copy-done.5
  11.7 0.0 copy-done.4
  11.7 0.0 copy-done.8
  11.7 0.0 copy-start
  11.8 1.0 %copy-done = f32[48,2048]{1,0:T(8,128)S(1)} copy-done((f32[48,2048]{1,0:T(8,128)S(1)}, f32[48,2048]{1,0:T(8,128)}, u32[]{:S(2)}) %copy-start) | copy-done | bytes 393240
  12.7 2.0 %sort.1 = (f32[56,2048]{1,0:T(8,128)S(1)}, f32[56,640]{1,0:T(8,128)S(1)}, s32[4,2048]{1,0:T(4,128)S(1)}, s32[2,16,128]{2,1,0:T(8,128)S(1)}, f32[16,128]{1,0:T(8,128)S(1)}, /*index=5*/f32[16,128]{1,0:T(8,128)S(1)}) custom-call(s32[1]{0:T(128)} %bitcast.refs_0_, s32[1,2048]{1,0:T(1,128)S(1)} %bitcast.6, s32[1,2048]{1,0:T(1,128)S(1)} %bitcast.7, ...), custom_call_target="tpu_custom_call" | custom-call | flops 1145044992 | bytes 393216 | tf_op jit(solution)/shard_map/sort/pallas_call | solution.py:328
  14.7 0.0 all-to-all-done.parts_ref
  14.7 1.2 %pack.1 = (bf16[64,16,128]{2,1,0:T(8,128)(2,1)S(1)}, f32[1,2048]{1,0:T(1,128)S(1)}) custom-call(f32[8,16,128]{2,1,0:T(8,128)S(1)} %all-to-all-done.parts_ref, f32[16,128]{1,0:T(8,128)S(1)} %get-tuple-element.13.known_ref, s32[2,16,128]{2,1,0:T(8,128)S(1)} %get-tuple-element.14.from_ref, f32[56,2048]{1,0:T(8,128)S(1)} %get-tuple-element.15.slots_ref, ...), custom_call_target="tpu_custom_call" | custom-call | tf_op jit(solution)/shard_map/pack/pallas_call | solution.py:344
  15.9 0.0 copy-start.2
  15.9 27.3 %all_to_all.15.got_ref = bf16[64,16,128]{2,1,0:T(8,128)(2,1)S(1)} all-to-all(bf16[64,16,128]{2,1,0:T(8,128)(2,1)S(1)} %get-tuple-element.19), channel_id=1, replica_groups=mesh['tm'=8,'series'=64] {'series'}, dimensions={0} | all-to-all | bytes 524288 | tf_op jit(solution)/shard_map/all_to_all | solution.py:350
  43.2 0.0 copy-done.2
  43.2 0.8 %gaps.1 = bf16[64,16,128]{2,1,0:T(8,128)(2,1)S(1)} custom-call(bf16[64,16,128]{2,1,0:T(8,128)(2,1)S(1)} %all_to_all.15.got_ref, f32[48,64]{1,0:T(8,128)S(1)} %copy-done.2, f32[16,128]{1,0:T(8,128)S(1)} %get-tuple-element.20.base_rest_ref), custom_call_target="tpu_custom_call" | custom-call | tf_op jit(solution)/shard_map/gaps/pallas_call | solution.py:351
  44.1 0.0 copy-start.1
  44.1 18.6 %all_to_all.16.back_ref = bf16[64,16,128]{2,1,0:T(8,128)(2,1)S(1)} all-to-all(bf16[64,16,128]{2,1,0:T(8,128)(2,1)S(1)} %gaps.1), channel_id=1, replica_groups=mesh['tm'=8,'series'=64] {'series'}, dimensions={0} | all-to-all | bytes 524288 | tf_op jit(solution)/shard_map/all_to_all | solution.py:357
  62.7 0.0 copy-done.1
  62.7 1.8 %finish.1 = f32[48,2048]{1,0:T(8,128)} custom-call(f32[48,2048]{1,0:T(8,128)S(1)} %copy-done.1, f32[1,2048]{1,0:T(1,128)S(1)} %get-tuple-element.18.shift_ref, s32[4,2048]{1,0:T(4,128)S(1)} %get-tuple-element.17.places_ref, bf16[64,16,128]{2,1,0:T(8,128)(2,1)S(1)} %all_to_all.16.back_ref), custom_call_target="tpu_custom_call" | custom-call | tf_op jit(solution)/shard_map/finish/pallas_call | solution.py:358
Async XLA Ops:
  1.7 9.3 %copy-start.3 = (f32[5,2048]{1,0:T(8,128)S(1)}, f32[5,2048]{1,0:T(8,128)}, u32[]{:S(2)}) copy-start(f32[5,2048]{1,0:T(8,128)} %refs_6_.1) | copy-start | bytes 122884
  1.7 13.0 %all-to-all-start = ((f32[8,16,128]{2,1,0:T(8,128)}), f32[8,16,128]{2,1,0:T(8,128)S(1)}, u32[]{:S(2)}, u32[]{:S(2)}) async-start(f32[8,16,128]{2,1,0:T(8,128)} %day_sums.1), calls=%async_computation | async-start | bytes 131072 | tf_op jit(solution)/shard_map/all_to_all | solution.py:327
  11.0 0.7 %copy-start.6 = (s32[2048,1]{0,1:T(1,128)S(1)}, s32[2048,1]{0,1:T(1,128)}, u32[]{:S(2)}) copy-start(s32[2048,1]{0,1:T(1,128)} %param.12) | copy-start | bytes 24580
  11.0 0.7 %copy-start.7 = (f32[48,8]{0,1:T(8,128)S(1)}, f32[48,8]{0,1:T(8,128)}, u32[]{:S(2)}) copy-start(f32[48,8]{0,1:T(8,128)} %param.14) | copy-start | bytes 4612
  11.0 0.7 %copy-start.5 = (s32[2048,1]{0,1:T(1,128)S(1)}, s32[2048,1]{0,1:T(1,128)}, u32[]{:S(2)}) copy-start(s32[2048,1]{0,1:T(1,128)} %param.11) | copy-start | bytes 24580
  11.0 0.7 %copy-start.4 = (s32[2048,1]{0,1:T(1,128)S(1)}, s32[2048,1]{0,1:T(1,128)}, u32[]{:S(2)}) copy-start(s32[2048,1]{0,1:T(1,128)} %param.10) | copy-start | bytes 24580
  11.0 0.7 %copy-start.8 = (f32[48,1]{0,1:T(1,128)S(1)}, f32[48,1]{0,1:T(1,128)}, u32[]{:S(2)}) copy-start(f32[48,1]{0,1:T(1,128)} %param.15) | copy-start | bytes 580
  11.7 1.0 %copy-start = (f32[48,2048]{1,0:T(8,128)S(1)}, f32[48,2048]{1,0:T(8,128)}, u32[]{:S(2)}) copy-start(f32[48,2048]{1,0:T(8,128)} %leaf_ref.3) | copy-start | bytes 1179652
  15.9 27.3 %copy-start.2 = (f32[48,64]{1,0:T(8,128)S(1)}, f32[48,64]{1,0:T(8,128)}, u32[]{:S(2)}) copy-start(f32[48,64]{1,0:T(8,128)} %base_fine_ref.1) | copy-start | bytes 36868
  44.1 18.6 %copy-start.1 = (f32[48,2048]{1,0:T(8,128)S(1)}, f32[48,2048]{1,0:T(8,128)}, u32[]{:S(2)}) copy-start(f32[48,2048]{1,0:T(8,128)} %leaf_ref.3) | copy-start | bytes 1179652

commit v14 on v11

--- a/solution.py
+++ b/solution.py
@@ -3,6 +3,7 @@
 from jax import lax
 from jax.experimental import pallas as pl
 from jax.experimental.pallas import tpu as pltpu
+from jax.sharding import Mesh
 from jax.sharding import PartitionSpec as P
 
 f32 = jnp.float32
@@ -72,6 +73,11 @@
 def start_kernel(leaf_ref, sums_ref):
     sums = dense_of(jnp.sum(leaf_ref[...], axis=0, keepdims=True))
     sums_ref[...] = jnp.broadcast_to(sums[None], sums_ref.shape)
+
+
+def halves_kernel(sums_ref, parts_ref, out_ref):
+    out_ref[0, :, :] = sums_ref[0]
+    out_ref[1, :, :] = jnp.sum(parts_ref[...], axis=0)
 
 
 def ranks_of(owner, owners):
@@ -161,16 +167,14 @@
     return jnp.where(iota(sums.shape, 0) == LOW, sums - high, high)
 
 
-def send_kernel(parts_ref, known_ref, from_ref, slots_ref, nodes_ref, places_ref, pay_ref, shift_ref):
+def send_kernel(here_ref, there_ref, known_ref, from_ref, slots_ref, nodes_ref, places_ref, pay_ref, shift_ref):
     owners = pay_ref.shape[0]
     rows = places_ref.shape[1]
     slots, mids = owners * 16, owners * 8
     days = slots_ref.shape[0] - 8
     season_days = days * 2
-    parts = parts_ref[...]
-    quarter = places_ref[3:4, 0:128]
-    own = jnp.sum(jnp.where(iota(parts.shape, 0) >> 1 == quarter[None], parts, 0.0), axis=0)
-    total = jnp.sum(parts, axis=0)
+    own = here_ref[0, :, :] + there_ref[0, :, :]
+    total = here_ref[1, :, :] + there_ref[1, :, :]
     shift = known_ref[...] - (0.5 * own / season_days + 0.25 * total / (season_days * 4))
     shift_row = row_of(shift)
     shift_ref[...] = shift_row
@@ -299,16 +303,16 @@
 def per_device(leaf, seas, fine, mid, top, base_fine, base_mid, base_top):
     days, rows = leaf.shape
     owners = lax.axis_size("series")
-    blocks = lax.axis_size("tm")
-    quarter = (lax.axis_index("tm") // (blocks // 4)).astype(i32).reshape(1)
+    chips = lax.axis_size("x")
+    quarter = lax.axis_index("x").astype(i32).reshape(1)
     vmem = pl.BlockSpec(memory_space=pltpu.VMEM)
     smem = pl.BlockSpec(memory_space=pltpu.SMEM)
     dense = (rows // 128, 128)
 
     sums = pl.pallas_call(
-        start_kernel, out_shape=jax.ShapeDtypeStruct((blocks,) + dense, f32), compiler_params=PARAMS, name="day_sums"
+        start_kernel, out_shape=jax.ShapeDtypeStruct((chips,) + dense, f32), compiler_params=PARAMS, name="day_sums"
     )(leaf)
-    parts = lax.all_to_all(sums, "tm", 0, 0, tiled=True)
+    parts = lax.all_to_all(sums, "x", 0, 0, tiled=True)
     slots, nodes, places, come_from, base_rest, known = pl.pallas_call(
         lambda *refs: sort_kernel(owners, *refs),
         out_shape=(
@@ -325,12 +329,17 @@
         name="sort",
     )(quarter, *(ids.reshape(1, rows) for ids in (fine, mid, top)), base_mid.T, base_top.reshape(1, days), seas, leaf)
 
+    here = pl.pallas_call(
+        halves_kernel, out_shape=jax.ShapeDtypeStruct((2,) + dense, f32), compiler_params=PARAMS, name="halves"
+    )(sums, parts)
+    there = lax.ppermute(here, "core", [(0, 1), (1, 0)])
+
     payload, shift = pl.pallas_call(
         send_kernel,
         out_shape=(jax.ShapeDtypeStruct((owners, 16, 128), bf16), jax.ShapeDtypeStruct((1, rows), f32)),
         compiler_params=PARAMS,
         name="pack",
-    )(parts, known, come_from, slots, nodes, places)
+    )(here, there, known, come_from, slots, nodes, places)
     got = lax.all_to_all(payload, "series", 0, 0, tiled=True)
     back = pl.pallas_call(
         owner_kernel,
@@ -351,19 +360,22 @@
 
 
 def solution(mesh):
+    chips = mesh.devices.shape[0] // 2
+    mesh = Mesh(mesh.devices.reshape(chips, 2, -1), ("x", "core", "series"))
+    days = ("x", "core")
     return jax.shard_map(
         per_device,
         mesh=mesh,
         in_specs=(
-            P("tm", "series"),
+            P(days, "series"),
             P(None, "series"),
             P("series", None),
             P("series", None),
             P("series", None),
-            P("tm", "series"),
-            P("tm", "series"),
-            P("tm", "series"),
+            P(days, "series"),
+            P(days, "series"),
+            P(days, "series"),
         ),
-        out_specs=P("tm", "series"),
+        out_specs=P(days, "series"),
         check_vma=False,
     )

time: 64.8 us -> 71 us (1.096)
  waiting for transfers between devices: 0.8 us -> 3.38 us
  starting transfers between devices: 9.27 us -> 11.1 us
  blocking collectives: 45.4 us -> 46.3 us
  Pallas kernels: 6.47 us -> 7.27 us
    all_to_all x1, waiting for transfers between devices: 0.8 us -> 3.38 us  [per_device(): parts = lax.all_to_all(sums, 'x', 0, 0, tiled=True)]
    ppermute x0 -> x1, starting transfers between devices: none -> 2.04 us  [per_device(): there = lax.ppermute(here, 'core', [(0, 1), (1, 0)])]
    pallas_call x1 -> x2, Pallas kernels: 0.66 us -> 1.45 us  [the longest x1 0.8 us: per_device(): pl.pallas_call(halves_kernel, out_shape=jax.ShapeDtypeStruct((2,) + dense...]
  transfers between devices with their start and end apart: 1 -> 2, of which waited for: 1 -> 1; matrix products, arithmetic and copies ran while one was open for 0% -> 0% of each run, Pallas kernels for 3% -> 3%
where the time goes in v14:
time: 71 us; the launch traced here: 69.9 us
  blocking collectives  46.3 us (65%)
  starting transfers between devices  11.1 us (16%)
  Pallas kernels  7.27 us (10%)
  waiting for transfers between devices  3.38 us (5%)
  local copies, waits for them, and re-layouts  1.61 us (2%)
    all_to_all x1, blocking collectives, per_device(): got = lax.all_to_all(payload, 'series', 0, 0, tiled=True)  27.3 us
    all_to_all x1, blocking collectives, per_device(): back = lax.all_to_all(back, 'series', 0, 0, tiled=True)  19 us
    all_to_all x1, starting transfers between devices, per_device(): parts = lax.all_to_all(sums, 'x', 0, 0, tiled=True)  9.09 us
    all_to_all x1, waiting for transfers between devices, per_device(): parts = lax.all_to_all(sums, 'x', 0, 0, tiled=True)  3.38 us
    ppermute x1, starting transfers between devices, per_device(): there = lax.ppermute(here, 'core', [(0, 1), (1, 0)])  2.04 us
    pallas_call x1, Pallas kernels, per_device(): pl.pallas_call(lambda *refs: sort_kernel(owners, *refs), out_shape=(jax.S...  1.97 us
    pallas_call x1, Pallas kernels, per_device(): pl.pallas_call(finish_kernel, out_shape=jax.ShapeDtypeStruct((days, rows)...  1.84 us
    unnamed x18, local copies, waits for them, and re-layouts  1.61 us
  transfers between devices with their start and end apart: 2, of which 1 were waited for; matrix products, arithmetic and copies ran while one was open for 0% of the time, Pallas kernels for 3%

profile of v14, /device:TPU:6, one launch (start us, length us, event | category | flops | bytes accessed | tf_op | source)
XLA Modules:
  0.0 69.9 jit_solution(10728605016947888611)
XLA Ops:
  0.0 0.0 copy-start
  0.0 1.0 %copy-done = f32[48,2048]{1,0:T(8,128)S(1)} copy-done((f32[48,2048]{1,0:T(8,128)S(1)}, f32[48,2048]{1,0:T(8,128)}, u32[]{:S(2)}) %copy-start) | copy-done | bytes 393240
  1.0 0.0 copy-start.1
  1.0 0.6 day_sums.1.sums_ref
  1.6 9.1 %all-to-all-start = ((f32[4,16,128]{2,1,0:T(8,128)}), f32[4,16,128]{2,1,0:T(8,128)S(1)}, u32[]{:S(2)}, u32[]{:S(2)}) async-start(f32[4,16,128]{2,1,0:T(8,128)} %day_sums.1.sums_ref), calls=%async_computation | async-start | bytes 65536 | tf_op jit(solution)/shard_map/all_to_all | solution.py:315
  10.7 0.0 copy-start.3
  10.7 3.4 %all-to-all-done.parts_ref = f32[4,16,128]{2,1,0:T(8,128)S(1)} async-done(((f32[4,16,128]{2,1,0:T(8,128)}), f32[4,16,128]{2,1,0:T(8,128)S(1)}, u32[]{:S(2)}, u32[]{:S(2)}) %all-to-all-start) | async-done | bytes 32800 | tf_op jit(solution)/shard_map/all_to_all | solution.py:315
  14.1 0.0 copy-start.5
  14.1 0.0 copy-start.6
  14.1 0.0 copy-start.7
  14.1 0.8 %halves.1.here_ref = f32[2,16,128]{2,1,0:T(8,128)S(1)} custom-call(f32[4,16,128]{2,1,0:T(8,128)} %day_sums.1.sums_ref, f32[4,16,128]{2,1,0:T(8,128)S(1)} %all-to-all-done.parts_ref), custom_call_target="tpu_custom_call" | custom-call | tf_op jit(solution)/shard_map/halves/pallas_call | solution.py:332
  14.9 0.0 copy-start.4
  14.9 2.0 %collective-permute-start = (f32[2,16,128]{2,1,0:T(8,128)S(1)}, f32[2,16,128]{2,1,0:T(8,128)S(1)}, u32[]{:S(2)}, u32[]{:S(2)}) collective-permute-start(f32[2,16,128]{2,1,0:T(8,128)S(1)} %halves.1.here_ref), channel_id=1, source_target_pairs={{0,64},{64,0},{1,65},{65,1},{2,66},{66,2},{3,67},{67,3},{4,68},{68... | collective-permute-start | bytes 49160 | tf_op jit(solution)/shard_map/ppermute | solution.py:335
  17.0 0.0 copy-start.8
  17.0 0.0 copy-done.1
  17.0 0.0 copy-done.3
  17.0 0.0 copy-done.5
  17.0 0.0 copy-done.6
  17.0 0.0 copy-done.7
  17.0 0.0 copy-done.4
  17.0 0.6 copy-done.8
  17.6 2.0 %sort.1 = (f32[56,2048]{1,0:T(8,128)S(1)}, f32[56,640]{1,0:T(8,128)S(1)}, s32[4,2048]{1,0:T(4,128)S(1)}, s32[2,16,128]{2,1,0:T(8,128)S(1)}, f32[16,128]{1,0:T(8,128)S(1)}, /*index=5*/f32[16,128]{1,0:T(8,128)S(1)}) custom-call(s32[1]{0:T(128)} %bitcast.refs_0_, s32[1,2048]{1,0:T(1,128)S(1)} %bitcast.6, s32[1,2048]{1,0:T(1,128)S(1)} %bitcast.7, ...), custom_call_target="tpu_custom_call" | custom-call | flops 1145044992 | bytes 393216 | tf_op jit(solution)/shard_map/sort/pallas_call | solution.py:316
  19.6 0.0 collective-permute-done.there_ref
  19.6 1.2 %pack.1 = (bf16[64,16,128]{2,1,0:T(8,128)(2,1)S(1)}, f32[1,2048]{1,0:T(1,128)S(1)}) custom-call(f32[2,16,128]{2,1,0:T(8,128)S(1)} %halves.1.here_ref, f32[2,16,128]{2,1,0:T(8,128)S(1)} %collective-permute-done.there_ref, f32[16,128]{1,0:T(8,128)S(1)} %get-tuple-element.13.known_ref, s32[2,16,128]{2,1,0:T(8,128)S(1)} %get-tuple-element.14.from_ref, ...), custom_call_target="tpu_custom_call" | custom-call | tf_op jit(solution)/shard_map/pack/pallas_call | solution.py:337
  20.8 0.0 copy-start.2
  20.8 27.3 %all_to_all.15.got_ref = bf16[64,16,128]{2,1,0:T(8,128)(2,1)S(1)} all-to-all(bf16[64,16,128]{2,1,0:T(8,128)(2,1)S(1)} %get-tuple-element.19), channel_id=1, replica_groups=mesh['x'=4,'core'=2,'series'=64] {'series'}, dimensions={0} | all-to-all | bytes 524288 | tf_op jit(solution)/shard_map/all_to_all | solution.py:343
  48.2 0.0 copy-done.2
  48.2 0.8 %gaps.1 = bf16[64,16,128]{2,1,0:T(8,128)(2,1)S(1)} custom-call(bf16[64,16,128]{2,1,0:T(8,128)(2,1)S(1)} %all_to_all.15.got_ref, f32[48,64]{1,0:T(8,128)S(1)} %copy-done.2, f32[16,128]{1,0:T(8,128)S(1)} %get-tuple-element.20.base_rest_ref), custom_call_target="tpu_custom_call" | custom-call | tf_op jit(solution)/shard_map/gaps/pallas_call | solution.py:344
  49.0 19.0 %all_to_all.16.back_ref = bf16[64,16,128]{2,1,0:T(8,128)(2,1)S(1)} all-to-all(bf16[64,16,128]{2,1,0:T(8,128)(2,1)S(1)} %gaps.1), channel_id=1, replica_groups=mesh['x'=4,'core'=2,'series'=64] {'series'}, dimensions={0} | all-to-all | bytes 524288 | tf_op jit(solution)/shard_map/all_to_all | solution.py:350
  68.0 1.8 %finish.1 = f32[48,2048]{1,0:T(8,128)} custom-call(f32[48,2048]{1,0:T(8,128)S(1)} %copy-done.1, f32[1,2048]{1,0:T(1,128)S(1)} %get-tuple-element.18.shift_ref, s32[4,2048]{1,0:T(4,128)S(1)} %get-tuple-element.17.places_ref, bf16[64,16,128]{2,1,0:T(8,128)(2,1)S(1)} %all_to_all.16.back_ref), custom_call_target="tpu_custom_call" | custom-call | tf_op jit(solution)/shard_map/finish/pallas_call | solution.py:351
Async XLA Ops:
  0.0 1.0 %copy-start = (f32[48,2048]{1,0:T(8,128)S(1)}, f32[48,2048]{1,0:T(8,128)}, u32[]{:S(2)}) copy-start(f32[48,2048]{1,0:T(8,128)} %leaf_ref.3) | copy-start | bytes 1179652
  1.0 16.0 %copy-start.1 = (f32[48,2048]{1,0:T(8,128)S(1)}, f32[48,2048]{1,0:T(8,128)}, u32[]{:S(2)}) copy-start(f32[48,2048]{1,0:T(8,128)} %leaf_ref.3) | copy-start | bytes 1179652
  1.6 12.5 %all-to-all-start = ((f32[4,16,128]{2,1,0:T(8,128)}), f32[4,16,128]{2,1,0:T(8,128)S(1)}, u32[]{:S(2)}, u32[]{:S(2)}) async-start(f32[4,16,128]{2,1,0:T(8,128)} %day_sums.1.sums_ref), calls=%async_computation | async-start | bytes 65536 | tf_op jit(solution)/shard_map/all_to_all | solution.py:315
  10.7 6.3 %copy-start.3 = (f32[5,2048]{1,0:T(8,128)S(1)}, f32[5,2048]{1,0:T(8,128)}, u32[]{:S(2)}) copy-start(f32[5,2048]{1,0:T(8,128)} %refs_6_.1) | copy-start | bytes 122884
  14.1 2.9 %copy-start.5 = (s32[2048,1]{0,1:T(1,128)S(1)}, s32[2048,1]{0,1:T(1,128)}, u32[]{:S(2)}) copy-start(s32[2048,1]{0,1:T(1,128)} %param.11) | copy-start | bytes 24580
  14.1 2.9 %copy-start.6 = (s32[2048,1]{0,1:T(1,128)S(1)}, s32[2048,1]{0,1:T(1,128)}, u32[]{:S(2)}) copy-start(s32[2048,1]{0,1:T(1,128)} %param.12) | copy-start | bytes 24580
  14.1 2.9 %copy-start.7 = (f32[48,8]{0,1:T(8,128)S(1)}, f32[48,8]{0,1:T(8,128)}, u32[]{:S(2)}) copy-start(f32[48,8]{0,1:T(8,128)} %param.14) | copy-start | bytes 4612
  14.9 2.1 %copy-start.4 = (s32[2048,1]{0,1:T(1,128)S(1)}, s32[2048,1]{0,1:T(1,128)}, u32[]{:S(2)}) copy-start(s32[2048,1]{0,1:T(1,128)} %param.10) | copy-start | bytes 24580
  14.9 4.7 %collective-permute-start = (f32[2,16,128]{2,1,0:T(8,128)S(1)}, f32[2,16,128]{2,1,0:T(8,128)S(1)}, u32[]{:S(2)}, u32[]{:S(2)}) collective-permute-start(f32[2,16,128]{2,1,0:T(8,128)S(1)} %halves.1.here_ref), channel_id=1, source_target_pairs={{0,64},{64,0},{1,65},{65,1},{2,66},{66,2},{3,67},{67,3},{4,68},{68... | collective-permute-start | bytes 49160 | tf_op jit(solution)/shard_map/ppermute | solution.py:335
  17.0 0.7 copy-start.8
  20.8 27.4 %copy-start.2 = (f32[48,64]{1,0:T(8,128)S(1)}, f32[48,64]{1,0:T(8,128)}, u32[]{:S(2)}) copy-start(f32[48,64]{1,0:T(8,128)} %base_fine_ref.1) | copy-start | bytes 36868

commit v15 on v11

--- a/solution.py
+++ b/solution.py
@@ -262,20 +262,21 @@
     half = days // 2
     back = back_ref[...].astype(f32)
     day, lane = iota((days, 128), 0), iota((days, 128), 1)
-    take = jnp.concatenate([ones_where(lane == day), ones_where(lane == day + 64), ones_where(lane == top_lane(day))], axis=0)
-    taken = dot_nt(take, back.reshape(slots, 128).astype(bf16))
-    tops = jnp.where(iota((days, slots), 0) // 3 == (iota((days, slots), 1) & 15), taken[2 * days:, :], 0.0).astype(bf16)
+    flat = back.reshape(slots, 128)
+    turned = jnp.concatenate([jnp.transpose(flat[at:at + 128, :]) for at in range(0, slots, 128)], axis=1)
+    tops = dot(ones_where(lane == top_lane(day)), turned.astype(bf16))
+    tops = jnp.where(iota((days, slots), 0) // 3 == (iota((days, slots), 1) & 15), tops, 0.0).astype(bf16)
     tops = dot(tops, ones_where(iota((slots, TOP_ROWS), 0) >> 4 == iota((slots, TOP_ROWS), 1)))
     first, last = (back[:, at:at + 8, :].reshape(mids, 128).astype(bf16) for at in (0, 8))
     mid = dot_nt(ones_where((day < half) & (lane == lane_of(day))), first)
     mid = mid + dot_nt(ones_where((day >= half) & (lane == lane_of(day - half))), last)
     slot_count, width = rows // 256, min(128, mids)
     mid_count = mids // width
-    taken = jnp.concatenate([taken[:days, :], taken[days:2 * days, :]], axis=1)
+    taken = jnp.concatenate([turned[:days, :], turned[64:64 + days, :]], axis=1)
     slot_gaps = jnp.concatenate([taken[:, g * 256:(g + 1) * 256] for g in range(slot_count)], axis=0).astype(bf16)
     node_gaps = [jnp.concatenate([mid[:, g * width:(g + 1) * width], tops], axis=1) for g in range(mid_count)]
     node_gaps = jnp.concatenate(node_gaps, axis=0).astype(bf16)
-    step = min(512, rows)
+    step = min(256, rows)
     copies = []
     for at in range(0, rows, step):
         place, mid, top = (places_ref[k:k + 1, at:at + step] for k in range(3))
@@ -344,7 +345,7 @@
         out_shape=jax.ShapeDtypeStruct((days, rows), f32),
         in_specs=[vmem] * 4,
         out_specs=pl.BlockSpec(memory_space=pl.ANY),
-        scratch_shapes=[pltpu.VMEM((days, rows), f32), pltpu.SemaphoreType.DMA((max(1, rows // 512),))],
+        scratch_shapes=[pltpu.VMEM((days, rows), f32), pltpu.SemaphoreType.DMA((max(1, rows // 256),))],
         compiler_params=PARAMS,
         name="finish",
     )(leaf, shift, places, back)

time: 64.8 us -> 64.8 us (level)
  no operation moved by 1% of the time
where the time goes in v15:
time: 64.8 us; the launch traced here: 63.8 us
  blocking collectives  45.4 us (70%)
  starting transfers between devices  9.27 us (14%)
  Pallas kernels  6.53 us (10%)
  local copies, waits for them, and re-layouts  1.71 us (3%)
  waiting for transfers between devices  0.8 us (1%)
    all_to_all x1, blocking collectives, per_device(): got = lax.all_to_all(payload, 'series', 0, 0, tiled=True)  27 us
    all_to_all x1, blocking collectives, per_device(): back = lax.all_to_all(back, 'series', 0, 0, tiled=True)  18.4 us
    all_to_all x1, starting transfers between devices, per_device(): parts = lax.all_to_all(sums, 'tm', 0, 0, tiled=True)  9.27 us
    pallas_call x1, Pallas kernels, per_device(): pl.pallas_call(lambda *refs: sort_kernel(owners, *refs), out_shape=(jax.S...  1.97 us
    pallas_call x1, Pallas kernels, per_device(): pl.pallas_call(finish_kernel, out_shape=jax.ShapeDtypeStruct((days, rows)...  1.88 us
    unnamed x18, local copies, waits for them, and re-layouts  1.71 us
  transfers between devices with their start and end apart: 1, of which 1 were waited for; matrix products, arithmetic and copies ran while one was open for 0% of the time, Pallas kernels for 3%

profile of v15, /device:TPU:6, one launch (start us, length us, event | category | flops | bytes accessed | tf_op | source)
XLA Modules:
  0.0 63.8 jit_solution(249478514823061511)
XLA Ops:
  0.0 0.0 copy-start
  0.0 1.0 %copy-done = f32[48,2048]{1,0:T(8,128)S(1)} copy-done((f32[48,2048]{1,0:T(8,128)S(1)}, f32[48,2048]{1,0:T(8,128)}, u32[]{:S(2)}) %copy-start) | copy-done | bytes 393240
  1.0 0.0 copy-start.1
  1.0 0.7 %day_sums.1 = f32[8,16,128]{2,1,0:T(8,128)} custom-call(f32[48,2048]{1,0:T(8,128)S(1)} %copy-done), custom_call_target="tpu_custom_call" | custom-call | tf_op jit(solution)/shard_map/day_sums/pallas_call | solution.py:309
  1.7 0.0 copy-start.3
  1.7 9.3 %all-to-all-start = ((f32[8,16,128]{2,1,0:T(8,128)}), f32[8,16,128]{2,1,0:T(8,128)S(1)}, u32[]{:S(2)}, u32[]{:S(2)}) async-start(f32[8,16,128]{2,1,0:T(8,128)} %day_sums.1), calls=%async_computation | async-start | bytes 131072 | tf_op jit(solution)/shard_map/all_to_all | solution.py:312
  10.9 0.0 copy-start.6
  10.9 0.0 copy-start.7
  10.9 0.0 copy-start.5
  10.9 0.0 copy-start.4
  11.0 0.0 copy-start.8
  11.0 0.0 copy-done.1
  11.0 0.0 copy-done.3
  11.0 0.6 copy-done.6
  11.6 0.0 copy-done.7
  11.6 0.0 copy-done.5
  11.7 0.0 copy-done.4
  11.7 0.0 copy-done.8
  11.7 2.0 %sort.1 = (f32[56,2048]{1,0:T(8,128)S(1)}, f32[56,640]{1,0:T(8,128)S(1)}, s32[4,2048]{1,0:T(4,128)S(1)}, s32[2,16,128]{2,1,0:T(8,128)S(1)}, f32[16,128]{1,0:T(8,128)S(1)}, /*index=5*/f32[16,128]{1,0:T(8,128)S(1)}) custom-call(s32[1]{0:T(128)} %bitcast.refs_0_, s32[1,2048]{1,0:T(1,128)S(1)} %bitcast.6, s32[1,2048]{1,0:T(1,128)S(1)} %bitcast.7, ...), custom_call_target="tpu_custom_call" | custom-call | flops 1145044992 | bytes 393216 | tf_op jit(solution)/shard_map/sort/pallas_call | solution.py:313
  13.7 0.8 %all-to-all-done.parts_ref = f32[8,16,128]{2,1,0:T(8,128)S(1)} async-done(((f32[8,16,128]{2,1,0:T(8,128)}), f32[8,16,128]{2,1,0:T(8,128)S(1)}, u32[]{:S(2)}, u32[]{:S(2)}) %all-to-all-start) | async-done | bytes 65568 | tf_op jit(solution)/shard_map/all_to_all | solution.py:312
  14.5 1.2 %pack.1 = (bf16[64,16,128]{2,1,0:T(8,128)(2,1)S(1)}, f32[1,2048]{1,0:T(1,128)S(1)}) custom-call(f32[8,16,128]{2,1,0:T(8,128)S(1)} %all-to-all-done.parts_ref, f32[16,128]{1,0:T(8,128)S(1)} %get-tuple-element.13.known_ref, s32[2,16,128]{2,1,0:T(8,128)S(1)} %get-tuple-element.14.from_ref, f32[56,2048]{1,0:T(8,128)S(1)} %get-tuple-element.15.slots_ref, ...), custom_call_target="tpu_custom_call" | custom-call | tf_op jit(solution)/shard_map/pack/pallas_call | solution.py:329
  15.7 0.0 copy-start.2
  15.7 27.0 %all_to_all.15.got_ref = bf16[64,16,128]{2,1,0:T(8,128)(2,1)S(1)} all-to-all(bf16[64,16,128]{2,1,0:T(8,128)(2,1)S(1)} %get-tuple-element.19), channel_id=1, replica_groups=mesh['tm'=8,'series'=64] {'series'}, dimensions={0} | all-to-all | bytes 524288 | tf_op jit(solution)/shard_map/all_to_all | solution.py:335
  42.6 0.0 copy-done.2
  42.6 0.8 %gaps.1 = bf16[64,16,128]{2,1,0:T(8,128)(2,1)S(1)} custom-call(bf16[64,16,128]{2,1,0:T(8,128)(2,1)S(1)} %all_to_all.15.got_ref, f32[48,64]{1,0:T(8,128)S(1)} %copy-done.2, f32[16,128]{1,0:T(8,128)S(1)} %get-tuple-element.20.base_rest_ref), custom_call_target="tpu_custom_call" | custom-call | tf_op jit(solution)/shard_map/gaps/pallas_call | solution.py:336
  43.5 18.4 %all_to_all.16.back_ref = bf16[64,16,128]{2,1,0:T(8,128)(2,1)S(1)} all-to-all(bf16[64,16,128]{2,1,0:T(8,128)(2,1)S(1)} %gaps.1), channel_id=1, replica_groups=mesh['tm'=8,'series'=64] {'series'}, dimensions={0} | all-to-all | bytes 524288 | tf_op jit(solution)/shard_map/all_to_all | solution.py:342
  61.9 1.9 %finish.1 = f32[48,2048]{1,0:T(8,128)} custom-call(f32[48,2048]{1,0:T(8,128)S(1)} %copy-done.1, f32[1,2048]{1,0:T(1,128)S(1)} %get-tuple-element.18.shift_ref, s32[4,2048]{1,0:T(4,128)S(1)} %get-tuple-element.17.places_ref, bf16[64,16,128]{2,1,0:T(8,128)(2,1)S(1)} %all_to_all.16.back_ref), custom_call_target="tpu_custom_call" | custom-call | tf_op jit(solution)/shard_map/finish/pallas_call | solution.py:343
Async XLA Ops:
  0.0 1.0 %copy-start = (f32[48,2048]{1,0:T(8,128)S(1)}, f32[48,2048]{1,0:T(8,128)}, u32[]{:S(2)}) copy-start(f32[48,2048]{1,0:T(8,128)} %leaf_ref.3) | copy-start | bytes 1179652
  1.0 10.0 %copy-start.1 = (f32[48,2048]{1,0:T(8,128)S(1)}, f32[48,2048]{1,0:T(8,128)}, u32[]{:S(2)}) copy-start(f32[48,2048]{1,0:T(8,128)} %leaf_ref.3) | copy-start | bytes 1179652
  1.7 9.3 %copy-start.3 = (f32[5,2048]{1,0:T(8,128)S(1)}, f32[5,2048]{1,0:T(8,128)}, u32[]{:S(2)}) copy-start(f32[5,2048]{1,0:T(8,128)} %refs_6_.1) | copy-start | bytes 122884
  1.7 12.8 %all-to-all-start = ((f32[8,16,128]{2,1,0:T(8,128)}), f32[8,16,128]{2,1,0:T(8,128)S(1)}, u32[]{:S(2)}, u32[]{:S(2)}) async-start(f32[8,16,128]{2,1,0:T(8,128)} %day_sums.1), calls=%async_computation | async-start | bytes 131072 | tf_op jit(solution)/shard_map/all_to_all | solution.py:312
  10.9 0.7 %copy-start.6 = (s32[2048,1]{0,1:T(1,128)S(1)}, s32[2048,1]{0,1:T(1,128)}, u32[]{:S(2)}) copy-start(s32[2048,1]{0,1:T(1,128)} %param.12) | copy-start | bytes 24580
  10.9 0.7 %copy-start.7 = (f32[48,8]{0,1:T(8,128)S(1)}, f32[48,8]{0,1:T(8,128)}, u32[]{:S(2)}) copy-start(f32[48,8]{0,1:T(8,128)} %param.14) | copy-start | bytes 4612
  10.9 0.7 %copy-start.5 = (s32[2048,1]{0,1:T(1,128)S(1)}, s32[2048,1]{0,1:T(1,128)}, u32[]{:S(2)}) copy-start(s32[2048,1]{0,1:T(1,128)} %param.11) | copy-start | bytes 24580
  10.9 0.7 %copy-start.4 = (s32[2048,1]{0,1:T(1,128)S(1)}, s32[2048,1]{0,1:T(1,128)}, u32[]{:S(2)}) copy-start(s32[2048,1]{0,1:T(1,128)} %param.10) | copy-start | bytes 24580
  11.0 0.7 %copy-start.8 = (f32[48,1]{0,1:T(1,128)S(1)}, f32[48,1]{0,1:T(1,128)}, u32[]{:S(2)}) copy-start(f32[48,1]{0,1:T(1,128)} %param.15) | copy-start | bytes 580
  15.7 27.0 %copy-start.2 = (f32[48,64]{1,0:T(8,128)S(1)}, f32[48,64]{1,0:T(8,128)}, u32[]{:S(2)}) copy-start(f32[48,64]{1,0:T(8,128)} %base_fine_ref.1) | copy-start | bytes 36868

commit v16 on v11

--- a/solution.py
+++ b/solution.py
@@ -1,8 +1,11 @@
+import math
+
 import jax
 import jax.numpy as jnp
 from jax import lax
 from jax.experimental import pallas as pl
 from jax.experimental.pallas import tpu as pltpu
+from jax.sharding import Mesh
 from jax.sharding import PartitionSpec as P
 
 f32 = jnp.float32
@@ -94,8 +97,12 @@
     slots_ref, nodes_ref, places_ref, from_ref, rest_ref, known_ref,
 ):
     days, rows = leaf_ref.shape
+    side = math.isqrt(owners)
     fine, mid, top = fine_ref[...], mid_ref[...], top_ref[...]
-    owner = fine >> 6
+    owner, mid_owner = fine >> 6, mid >> 3
+    owner = (owner % side) * side + owner // side
+    mid = ((mid_owner % side) * side + mid_owner // side) * 8 + (mid & 7)
+    top = (top % side) * side + top // side
     rank = ranks_of(owner, owners)
     place = (rank >> 4) * (owners * 16) + owner * 16 + (rank & 15)
     places_ref[0:1, :] = place
@@ -298,7 +305,7 @@
 
 def per_device(leaf, seas, fine, mid, top, base_fine, base_mid, base_top):
     days, rows = leaf.shape
-    owners = lax.axis_size("series")
+    owners = lax.axis_size("y") * lax.axis_size("z")
     blocks = lax.axis_size("tm")
     quarter = (lax.axis_index("tm") // (blocks // 4)).astype(i32).reshape(1)
     vmem = pl.BlockSpec(memory_space=pltpu.VMEM)
@@ -331,14 +338,14 @@
         compiler_params=PARAMS,
         name="pack",
     )(parts, known, come_from, slots, nodes, places)
-    got = lax.all_to_all(payload, "series", 0, 0, tiled=True)
+    got = lax.all_to_all(payload, ("z", "y"), 0, 0, tiled=True)
     back = pl.pallas_call(
         owner_kernel,
         out_shape=jax.ShapeDtypeStruct((owners, 16, 128), bf16),
         compiler_params=PARAMS,
         name="gaps",
     )(got, base_fine, base_rest)
-    back = lax.all_to_all(back, "series", 0, 0, tiled=True)
+    back = lax.all_to_all(back, ("z", "y"), 0, 0, tiled=True)
     return pl.pallas_call(
         finish_kernel,
         out_shape=jax.ShapeDtypeStruct((days, rows), f32),
@@ -351,19 +358,23 @@
 
 
 def solution(mesh):
+    blocks, places = mesh.devices.shape
+    side = math.isqrt(places)
+    mesh = Mesh(mesh.devices.reshape(blocks, side, side), ("tm", "y", "z"))
+    series = ("y", "z")
     return jax.shard_map(
         per_device,
         mesh=mesh,
         in_specs=(
-            P("tm", "series"),
-            P(None, "series"),
-            P("series", None),
-            P("series", None),
-            P("series", None),
-            P("tm", "series"),
-            P("tm", "series"),
-            P("tm", "series"),
+            P("tm", series),
+            P(None, series),
+            P(series, None),
+            P(series, None),
+            P(series, None),
+            P("tm", series),
+            P("tm", series),
+            P("tm", series),
         ),
-        out_specs=P("tm", "series"),
+        out_specs=P("tm", series),
         check_vma=False,
     )

time: 64.8 us -> 64.7 us (level)
  the two profiles are of different devices: /device:TPU:6 before, /device:TPU:8 now
where the time goes in v16:
time: 64.7 us; the launch traced here: 64.3 us
  blocking collectives  48.7 us (75%)
  Pallas kernels  6.49 us (10%)
  starting transfers between devices  4.43 us (7%)
  waiting for transfers between devices  2.88 us (4%)
  local copies, waits for them, and re-layouts  1.69 us (3%)
    all_to_all x1, blocking collectives, per_device(): got = lax.all_to_all(payload, ('z', 'y'), 0, 0, tiled=True)  30.6 us
    all_to_all x1, blocking collectives, per_device(): back = lax.all_to_all(back, ('z', 'y'), 0, 0, tiled=True)  18.1 us
    all_to_all x1, starting transfers between devices, per_device(): parts = lax.all_to_all(sums, 'tm', 0, 0, tiled=True)  4.43 us
    all_to_all x1, waiting for transfers between devices, per_device(): parts = lax.all_to_all(sums, 'tm', 0, 0, tiled=True)  2.88 us
    pallas_call x1, Pallas kernels, per_device(): pl.pallas_call(lambda *refs: sort_kernel(owners, *refs), out_shape=(jax.S...  1.98 us
    pallas_call x1, Pallas kernels, per_device(): pl.pallas_call(finish_kernel, out_shape=jax.ShapeDtypeStruct((days, rows)...  1.83 us
    unnamed x18, local copies, waits for them, and re-layouts  1.69 us
  transfers between devices with their start and end apart: 1, of which 1 were waited for; matrix products, arithmetic and copies ran while one was open for 0% of the time, Pallas kernels for 3%

profile of v16, /device:TPU:8, one launch (start us, length us, event | category | flops | bytes accessed | tf_op | source)
XLA Modules:
  0.0 64.3 jit_solution(4082852115474795674)
XLA Ops:
  0.0 0.0 copy-start
  0.0 1.0 %copy-done = f32[48,2048]{1,0:T(8,128)S(1)} copy-done((f32[48,2048]{1,0:T(8,128)S(1)}, f32[48,2048]{1,0:T(8,128)}, u32[]{:S(2)}) %copy-start) | copy-done | bytes 393240
  1.0 0.0 copy-start.1
  1.0 0.7 %day_sums.1 = f32[8,16,128]{2,1,0:T(8,128)} custom-call(f32[48,2048]{1,0:T(8,128)S(1)} %copy-done), custom_call_target="tpu_custom_call" | custom-call | tf_op jit(solution)/shard_map/day_sums/pallas_call | solution.py:315
  1.7 0.0 copy-start.3
  1.7 4.4 %all-to-all-start = ((f32[8,16,128]{2,1,0:T(8,128)}), f32[8,16,128]{2,1,0:T(8,128)S(1)}, u32[]{:S(2)}, u32[]{:S(2)}) async-start(f32[8,16,128]{2,1,0:T(8,128)} %day_sums.1), calls=%async_computation | async-start | bytes 131072 | tf_op jit(solution)/shard_map/all_to_all | solution.py:318
  6.1 0.0 copy-start.6
  6.1 0.0 copy-start.7
  6.1 0.0 copy-start.5
  6.1 0.0 copy-start.4
  6.1 0.0 copy-start.8
  6.2 0.0 copy-done.1
  6.2 0.0 copy-done.3
  6.2 0.6 copy-done.6
  6.8 0.0 copy-done.7
  6.8 0.0 copy-done.5
  6.8 0.0 copy-done.4
  6.8 0.0 copy-done.8
  6.8 2.0 %sort.1 = (f32[56,2048]{1,0:T(8,128)S(1)}, f32[56,640]{1,0:T(8,128)S(1)}, s32[4,2048]{1,0:T(4,128)S(1)}, s32[2,16,128]{2,1,0:T(8,128)S(1)}, f32[16,128]{1,0:T(8,128)S(1)}, /*index=5*/f32[16,128]{1,0:T(8,128)S(1)}) custom-call(s32[1]{0:T(128)} %bitcast.refs_0_, s32[1,2048]{1,0:T(1,128)S(1)} %bitcast.6, s32[1,2048]{1,0:T(1,128)S(1)} %bitcast.7, ...), custom_call_target="tpu_custom_call" | custom-call | flops 1145044992 | bytes 393216 | tf_op jit(solution)/shard_map/sort/pallas_call | solution.py:319
  8.8 2.9 %all-to-all-done.parts_ref = f32[8,16,128]{2,1,0:T(8,128)S(1)} async-done(((f32[8,16,128]{2,1,0:T(8,128)}), f32[8,16,128]{2,1,0:T(8,128)S(1)}, u32[]{:S(2)}, u32[]{:S(2)}) %all-to-all-start) | async-done | bytes 65568 | tf_op jit(solution)/shard_map/all_to_all | solution.py:318
  11.7 1.2 %pack.1 = (bf16[64,16,128]{2,1,0:T(8,128)(2,1)S(1)}, f32[1,2048]{1,0:T(1,128)S(1)}) custom-call(f32[8,16,128]{2,1,0:T(8,128)S(1)} %all-to-all-done.parts_ref, f32[16,128]{1,0:T(8,128)S(1)} %get-tuple-element.13.known_ref, s32[2,16,128]{2,1,0:T(8,128)S(1)} %get-tuple-element.14.from_ref, f32[56,2048]{1,0:T(8,128)S(1)} %get-tuple-element.15.slots_ref, ...), custom_call_target="tpu_custom_call" | custom-call | tf_op jit(solution)/shard_map/pack/pallas_call | solution.py:335
  12.9 0.0 copy-start.2
  12.9 30.6 %all_to_all.15.got_ref = bf16[64,16,128]{2,1,0:T(8,128)(2,1)S(1)} all-to-all(bf16[64,16,128]{2,1,0:T(8,128)(2,1)S(1)} %get-tuple-element.19), channel_id=1, replica_groups=mesh['tm'=8,'y'=8,'z'=8] {'z','y'}, dimensions={0} | all-to-all | bytes 524288 | tf_op jit(solution)/shard_map/all_to_all | solution.py:341
  43.5 0.0 copy-done.2
  43.5 0.8 %gaps.1 = bf16[64,16,128]{2,1,0:T(8,128)(2,1)S(1)} custom-call(bf16[64,16,128]{2,1,0:T(8,128)(2,1)S(1)} %all_to_all.15.got_ref, f32[48,64]{1,0:T(8,128)S(1)} %copy-done.2, f32[16,128]{1,0:T(8,128)S(1)} %get-tuple-element.20.base_rest_ref), custom_call_target="tpu_custom_call" | custom-call | tf_op jit(solution)/shard_map/gaps/pallas_call | solution.py:342
  44.3 18.1 %all_to_all.16.back_ref = bf16[64,16,128]{2,1,0:T(8,128)(2,1)S(1)} all-to-all(bf16[64,16,128]{2,1,0:T(8,128)(2,1)S(1)} %gaps.1), channel_id=1, replica_groups=mesh['tm'=8,'y'=8,'z'=8] {'z','y'}, dimensions={0} | all-to-all | bytes 524288 | tf_op jit(solution)/shard_map/all_to_all | solution.py:348
  62.5 1.8 %finish.1 = f32[48,2048]{1,0:T(8,128)} custom-call(f32[48,2048]{1,0:T(8,128)S(1)} %copy-done.1, f32[1,2048]{1,0:T(1,128)S(1)} %get-tuple-element.18.shift_ref, s32[4,2048]{1,0:T(4,128)S(1)} %get-tuple-element.17.places_ref, bf16[64,16,128]{2,1,0:T(8,128)(2,1)S(1)} %all_to_all.16.back_ref), custom_call_target="tpu_custom_call" | custom-call | tf_op jit(solution)/shard_map/finish/pallas_call | solution.py:349
Async XLA Ops:
  0.0 1.0 %copy-start = (f32[48,2048]{1,0:T(8,128)S(1)}, f32[48,2048]{1,0:T(8,128)}, u32[]{:S(2)}) copy-start(f32[48,2048]{1,0:T(8,128)} %leaf_ref.3) | copy-start | bytes 1179652
  1.0 5.2 %copy-start.1 = (f32[48,2048]{1,0:T(8,128)S(1)}, f32[48,2048]{1,0:T(8,128)}, u32[]{:S(2)}) copy-start(f32[48,2048]{1,0:T(8,128)} %leaf_ref.3) | copy-start | bytes 1179652
  1.7 4.5 %copy-start.3 = (f32[5,2048]{1,0:T(8,128)S(1)}, f32[5,2048]{1,0:T(8,128)}, u32[]{:S(2)}) copy-start(f32[5,2048]{1,0:T(8,128)} %refs_6_.1) | copy-start | bytes 122884
  1.7 10.1 %all-to-all-start = ((f32[8,16,128]{2,1,0:T(8,128)}), f32[8,16,128]{2,1,0:T(8,128)S(1)}, u32[]{:S(2)}, u32[]{:S(2)}) async-start(f32[8,16,128]{2,1,0:T(8,128)} %day_sums.1), calls=%async_computation | async-start | bytes 131072 | tf_op jit(solution)/shard_map/all_to_all | solution.py:318
  6.1 0.7 %copy-start.6 = (s32[2048,1]{0,1:T(1,128)S(1)}, s32[2048,1]{0,1:T(1,128)}, u32[]{:S(2)}) copy-start(s32[2048,1]{0,1:T(1,128)} %param.12) | copy-start | bytes 24580
  6.1 0.7 %copy-start.7 = (f32[48,8]{0,1:T(8,128)S(1)}, f32[48,8]{0,1:T(8,128)}, u32[]{:S(2)}) copy-start(f32[48,8]{0,1:T(8,128)} %param.14) | copy-start | bytes 4612
  6.1 0.7 %copy-start.5 = (s32[2048,1]{0,1:T(1,128)S(1)}, s32[2048,1]{0,1:T(1,128)}, u32[]{:S(2)}) copy-start(s32[2048,1]{0,1:T(1,128)} %param.11) | copy-start | bytes 24580
  6.1 0.7 %copy-start.4 = (s32[2048,1]{0,1:T(1,128)S(1)}, s32[2048,1]{0,1:T(1,128)}, u32[]{:S(2)}) copy-start(s32[2048,1]{0,1:T(1,128)} %param.10) | copy-start | bytes 24580
  6.1 0.7 %copy-start.8 = (f32[48,1]{0,1:T(1,128)S(1)}, f32[48,1]{0,1:T(1,128)}, u32[]{:S(2)}) copy-start(f32[48,1]{0,1:T(1,128)} %param.15) | copy-start | bytes 580
  12.9 30.6 %copy-start.2 = (f32[48,64]{1,0:T(8,128)S(1)}, f32[48,64]{1,0:T(8,128)}, u32[]{:S(2)}) copy-start(f32[48,64]{1,0:T(8,128)} %base_fine_ref.1) | copy-start | bytes 36868

commit v17 on v16

--- a/solution.py
+++ b/solution.py
@@ -176,7 +176,7 @@
     season_days = days * 2
     parts = parts_ref[...]
     quarter = places_ref[3:4, 0:128]
-    own = jnp.sum(jnp.where(iota(parts.shape, 0) >> 1 == quarter[None], parts, 0.0), axis=0)
+    own = jnp.sum(jnp.where((iota(parts.shape, 0) & 3) == quarter[None], parts, 0.0), axis=0)
     total = jnp.sum(parts, axis=0)
     shift = known_ref[...] - (0.5 * own / season_days + 0.25 * total / (season_days * 4))
     shift_row = row_of(shift)
@@ -306,8 +306,8 @@
 def per_device(leaf, seas, fine, mid, top, base_fine, base_mid, base_top):
     days, rows = leaf.shape
     owners = lax.axis_size("y") * lax.axis_size("z")
-    blocks = lax.axis_size("tm")
-    quarter = (lax.axis_index("tm") // (blocks // 4)).astype(i32).reshape(1)
+    blocks = lax.axis_size("x") * lax.axis_size("core")
+    quarter = lax.axis_index("x").astype(i32).reshape(1)
     vmem = pl.BlockSpec(memory_space=pltpu.VMEM)
     smem = pl.BlockSpec(memory_space=pltpu.SMEM)
     dense = (rows // 128, 128)
@@ -315,7 +315,7 @@
     sums = pl.pallas_call(
         start_kernel, out_shape=jax.ShapeDtypeStruct((blocks,) + dense, f32), compiler_params=PARAMS, name="day_sums"
     )(leaf)
-    parts = lax.all_to_all(sums, "tm", 0, 0, tiled=True)
+    parts = lax.all_to_all(sums, ("core", "x"), 0, 0, tiled=True)
     slots, nodes, places, come_from, base_rest, known = pl.pallas_call(
         lambda *refs: sort_kernel(owners, *refs),
         out_shape=(
@@ -360,21 +360,22 @@
 def solution(mesh):
     blocks, places = mesh.devices.shape
     side = math.isqrt(places)
-    mesh = Mesh(mesh.devices.reshape(blocks, side, side), ("tm", "y", "z"))
+    mesh = Mesh(mesh.devices.reshape(blocks // 2, 2, side, side), ("x", "core", "y", "z"))
+    days = ("x", "core")
     series = ("y", "z")
     return jax.shard_map(
         per_device,
         mesh=mesh,
         in_specs=(
-            P("tm", series),
+            P(days, series),
             P(None, series),
             P(series, None),
             P(series, None),
             P(series, None),
-            P("tm", series),
-            P("tm", series),
-            P("tm", series),
+            P(days, series),
+            P(days, series),
+            P(days, series),
         ),
-        out_specs=P("tm", series),
+        out_specs=P(days, series),
         check_vma=False,
     )

time: 64.7 us -> 65.1 us (level)
  blocking collectives: 48.7 us -> 49.4 us
where the time goes in v17:
time: 65.1 us; the launch traced here: 64.7 us
  blocking collectives  49.4 us (76%)
  Pallas kernels  6.49 us (10%)
  starting transfers between devices  4.43 us (7%)
  waiting for transfers between devices  2.65 us (4%)
  local copies, waits for them, and re-layouts  1.67 us (3%)
    all_to_all x1, blocking collectives, per_device(): got = lax.all_to_all(payload, ('z', 'y'), 0, 0, tiled=True)  31 us
    all_to_all x1, blocking collectives, per_device(): back = lax.all_to_all(back, ('z', 'y'), 0, 0, tiled=True)  18.4 us
    all_to_all x1, starting transfers between devices, per_device(): parts = lax.all_to_all(sums, ('core', 'x'), 0, 0, tiled=True)  4.43 us
    all_to_all x1, waiting for transfers between devices, per_device(): parts = lax.all_to_all(sums, ('core', 'x'), 0, 0, tiled=True)  2.65 us
    pallas_call x1, Pallas kernels, per_device(): pl.pallas_call(lambda *refs: sort_kernel(owners, *refs), out_shape=(jax.S...  1.98 us
    pallas_call x1, Pallas kernels, per_device(): pl.pallas_call(finish_kernel, out_shape=jax.ShapeDtypeStruct((days, rows)...  1.83 us
    unnamed x18, local copies, waits for them, and re-layouts  1.67 us
  transfers between devices with their start and end apart: 1, of which 1 were waited for; matrix products, arithmetic and copies ran while one was open for 0% of the time, Pallas kernels for 3%

profile of v17, /device:TPU:8, one launch (start us, length us, event | category | flops | bytes accessed | tf_op | source)
XLA Modules:
  0.0 64.7 jit_solution(8732841692711308504)
XLA Ops:
  0.0 0.0 copy-start
  0.0 1.0 %copy-done = f32[48,2048]{1,0:T(8,128)S(1)} copy-done((f32[48,2048]{1,0:T(8,128)S(1)}, f32[48,2048]{1,0:T(8,128)}, u32[]{:S(2)}) %copy-start) | copy-done | bytes 393240
  1.0 0.0 copy-start.1
  1.0 0.7 %day_sums.1 = f32[8,16,128]{2,1,0:T(8,128)} custom-call(f32[48,2048]{1,0:T(8,128)S(1)} %copy-done), custom_call_target="tpu_custom_call" | custom-call | tf_op jit(solution)/shard_map/day_sums/pallas_call | solution.py:315
  1.7 0.0 copy-start.3
  1.7 0.0 copy-start.6
  1.7 0.0 copy-start.7
  1.7 4.4 %all-to-all-start = ((f32[8,16,128]{2,1,0:T(8,128)}), f32[8,16,128]{2,1,0:T(8,128)S(1)}, u32[]{:S(2)}, u32[]{:S(2)}) async-start(f32[8,16,128]{2,1,0:T(8,128)} %day_sums.1), calls=%async_computation | async-start | bytes 131072 | tf_op jit(solution)/shard_map/all_to_all | solution.py:318
  6.1 0.0 copy-start.5
  6.1 0.0 copy-start.4
  6.1 0.0 copy-start.8
  6.1 0.0 copy-done.1
  6.1 0.0 copy-done.3
  6.2 0.0 copy-done.6
  6.2 0.0 copy-done.7
  6.2 0.6 copy-done.5
  6.8 0.0 copy-done.4
  6.8 0.0 copy-done.8
  6.8 2.0 %sort.1 = (f32[56,2048]{1,0:T(8,128)S(1)}, f32[56,640]{1,0:T(8,128)S(1)}, s32[4,2048]{1,0:T(4,128)S(1)}, s32[2,16,128]{2,1,0:T(8,128)S(1)}, f32[16,128]{1,0:T(8,128)S(1)}, /*index=5*/f32[16,128]{1,0:T(8,128)S(1)}) custom-call(s32[1]{0:T(128)} %bitcast.refs_0_, s32[1,2048]{1,0:T(1,128)S(1)} %bitcast.6, s32[1,2048]{1,0:T(1,128)S(1)} %bitcast.7, ...), custom_call_target="tpu_custom_call" | custom-call | flops 1145044992 | bytes 393216 | tf_op jit(solution)/shard_map/sort/pallas_call | solution.py:319
  8.8 2.7 %all-to-all-done.parts_ref = f32[8,16,128]{2,1,0:T(8,128)S(1)} async-done(((f32[8,16,128]{2,1,0:T(8,128)}), f32[8,16,128]{2,1,0:T(8,128)S(1)}, u32[]{:S(2)}, u32[]{:S(2)}) %all-to-all-start) | async-done | bytes 65568 | tf_op jit(solution)/shard_map/all_to_all | solution.py:318
  11.5 1.2 %pack.1 = (bf16[64,16,128]{2,1,0:T(8,128)(2,1)S(1)}, f32[1,2048]{1,0:T(1,128)S(1)}) custom-call(f32[8,16,128]{2,1,0:T(8,128)S(1)} %all-to-all-done.parts_ref, f32[16,128]{1,0:T(8,128)S(1)} %get-tuple-element.13.known_ref, s32[2,16,128]{2,1,0:T(8,128)S(1)} %get-tuple-element.14.from_ref, f32[56,2048]{1,0:T(8,128)S(1)} %get-tuple-element.15.slots_ref, ...), custom_call_target="tpu_custom_call" | custom-call | tf_op jit(solution)/shard_map/pack/pallas_call | solution.py:335
  12.6 0.0 copy-start.2
  12.7 31.0 %all_to_all.15.got_ref = bf16[64,16,128]{2,1,0:T(8,128)(2,1)S(1)} all-to-all(bf16[64,16,128]{2,1,0:T(8,128)(2,1)S(1)} %get-tuple-element.19), channel_id=1, replica_groups=mesh['x'=4,'core'=2,'y'=8,'z'=8] {'z','y'}, dimensions={0} | all-to-all | bytes 524288 | tf_op jit(solution)/shard_map/all_to_all | solution.py:341
  43.6 0.0 copy-done.2
  43.6 0.8 %gaps.1 = bf16[64,16,128]{2,1,0:T(8,128)(2,1)S(1)} custom-call(bf16[64,16,128]{2,1,0:T(8,128)(2,1)S(1)} %all_to_all.15.got_ref, f32[48,64]{1,0:T(8,128)S(1)} %copy-done.2, f32[16,128]{1,0:T(8,128)S(1)} %get-tuple-element.20.base_rest_ref), custom_call_target="tpu_custom_call" | custom-call | tf_op jit(solution)/shard_map/gaps/pallas_call | solution.py:342
  44.5 18.4 %all_to_all.16.back_ref = bf16[64,16,128]{2,1,0:T(8,128)(2,1)S(1)} all-to-all(bf16[64,16,128]{2,1,0:T(8,128)(2,1)S(1)} %gaps.1), channel_id=1, replica_groups=mesh['x'=4,'core'=2,'y'=8,'z'=8] {'z','y'}, dimensions={0} | all-to-all | bytes 524288 | tf_op jit(solution)/shard_map/all_to_all | solution.py:348
  62.9 1.8 %finish.1 = f32[48,2048]{1,0:T(8,128)} custom-call(f32[48,2048]{1,0:T(8,128)S(1)} %copy-done.1, f32[1,2048]{1,0:T(1,128)S(1)} %get-tuple-element.18.shift_ref, s32[4,2048]{1,0:T(4,128)S(1)} %get-tuple-element.17.places_ref, bf16[64,16,128]{2,1,0:T(8,128)(2,1)S(1)} %all_to_all.16.back_ref), custom_call_target="tpu_custom_call" | custom-call | tf_op jit(solution)/shard_map/finish/pallas_call | solution.py:349
Async XLA Ops:
  0.0 1.0 %copy-start = (f32[48,2048]{1,0:T(8,128)S(1)}, f32[48,2048]{1,0:T(8,128)}, u32[]{:S(2)}) copy-start(f32[48,2048]{1,0:T(8,128)} %leaf_ref.3) | copy-start | bytes 1179652
  1.0 5.1 %copy-start.1 = (f32[48,2048]{1,0:T(8,128)S(1)}, f32[48,2048]{1,0:T(8,128)}, u32[]{:S(2)}) copy-start(f32[48,2048]{1,0:T(8,128)} %leaf_ref.3) | copy-start | bytes 1179652
  1.7 4.5 %copy-start.3 = (f32[5,2048]{1,0:T(8,128)S(1)}, f32[5,2048]{1,0:T(8,128)}, u32[]{:S(2)}) copy-start(f32[5,2048]{1,0:T(8,128)} %refs_6_.1) | copy-start | bytes 122884
  1.7 4.5 %copy-start.6 = (s32[2048,1]{0,1:T(1,128)S(1)}, s32[2048,1]{0,1:T(1,128)}, u32[]{:S(2)}) copy-start(s32[2048,1]{0,1:T(1,128)} %param.12) | copy-start | bytes 24580
  1.7 4.5 %copy-start.7 = (f32[48,8]{0,1:T(8,128)S(1)}, f32[48,8]{0,1:T(8,128)}, u32[]{:S(2)}) copy-start(f32[48,8]{0,1:T(8,128)} %param.14) | copy-start | bytes 4612
  1.7 9.8 %all-to-all-start = ((f32[8,16,128]{2,1,0:T(8,128)}), f32[8,16,128]{2,1,0:T(8,128)S(1)}, u32[]{:S(2)}, u32[]{:S(2)}) async-start(f32[8,16,128]{2,1,0:T(8,128)} %day_sums.1), calls=%async_computation | async-start | bytes 131072 | tf_op jit(solution)/shard_map/all_to_all | solution.py:318
  6.1 0.7 %copy-start.5 = (s32[2048,1]{0,1:T(1,128)S(1)}, s32[2048,1]{0,1:T(1,128)}, u32[]{:S(2)}) copy-start(s32[2048,1]{0,1:T(1,128)} %param.11) | copy-start | bytes 24580
  6.1 0.7 %copy-start.4 = (s32[2048,1]{0,1:T(1,128)S(1)}, s32[2048,1]{0,1:T(1,128)}, u32[]{:S(2)}) copy-start(s32[2048,1]{0,1:T(1,128)} %param.10) | copy-start | bytes 24580
  6.1 0.7 %copy-start.8 = (f32[48,1]{0,1:T(1,128)S(1)}, f32[48,1]{0,1:T(1,128)}, u32[]{:S(2)}) copy-start(f32[48,1]{0,1:T(1,128)} %param.15) | copy-start | bytes 580
  12.6 31.0 %copy-start.2 = (f32[48,64]{1,0:T(8,128)S(1)}, f32[48,64]{1,0:T(8,128)}, u32[]{:S(2)}) copy-start(f32[48,64]{1,0:T(8,128)} %base_fine_ref.1) | copy-start | bytes 36868
